TPU v7x, 32 devices: a whole 2x2x4 slice. The times are simulated.
32 devices in a mesh: rows: 8 (over y, x, core), blk: 4 (over z).
Axes of the slice: x: 2, y: 2, z: 4, core: 2. Of those that a mesh axis runs over, the one named last changes fastest.
Arguments:
- tokens: bfloat16 [8, 1024, 1024], P('rows', 'blk'), may hold values from -6 to 6
- segment_ids: int32 [8, 1024], P('rows', 'blk'), may hold values from 0 to 510, as said below
- out_grad: bfloat16 [8, 1024, 1024], P('rows', 'blk'), may hold values from -6 to 6
- qkv_weight: bfloat16 [2, 1024, 3072], P(None, ('rows', 'blk')), may hold values from -0.1875 to 0.1875
- qv_bias: bfloat16 [2, 2048], P(None, ('rows', 'blk')), may hold values from -2 to 2
- out_weight: bfloat16 [2, 1024, 1024], P(None, ('rows', 'blk')), may hold values from -0.75 to 0.75
- out_bias: bfloat16 [2, 1024], P(None, ('rows', 'blk')), may hold values from -2 to 2
- up_weight: bfloat16 [2, 1024, 4096], P(None, ('rows', 'blk')), may hold values from -0.1875 to 0.1875
- up_bias: bfloat16 [2, 4096], P(None, ('rows', 'blk')), may hold values from -2 to 2
- down_weight: bfloat16 [2, 4096, 1024], P(None, ('rows', 'blk')), may hold values from -0.1875 to 0.1875
- down_bias: bfloat16 [2, 1024], P(None, ('rows', 'blk')), may hold values from -2 to 2
- norm_gain: bfloat16 [2, 2, 1024], P(None, None, ('rows', 'blk')), may hold values from 0.25 to 1.75
- norm_shift: bfloat16 [2, 2, 1024], P(None, None, ('rows', 'blk')), may hold values from -3 to 3
Outputs:
- result: bfloat16 [8, 1024, 1024], P('rows', 'blk')
- input_grad: bfloat16 [8, 1024, 1024], P('rows', 'blk')
- qkv_weight_grad: float32 [2, 1024, 3072], P(None, ('rows', 'blk'))
- qv_bias_grad: float32 [2, 2048], P(None, ('rows', 'blk'))
- out_weight_grad: float32 [2, 1024, 1024], P(None, ('rows', 'blk'))
- out_bias_grad: float32 [2, 1024], P(None, ('rows', 'blk'))
- up_weight_grad: float32 [2, 1024, 4096], P(None, ('rows', 'blk'))
- up_bias_grad: float32 [2, 4096], P(None, ('rows', 'blk'))
- down_weight_grad: float32 [2, 4096, 1024], P(None, ('rows', 'blk'))
- down_bias_grad: float32 [2, 1024], P(None, ('rows', 'blk'))
- norm_gain_grad: float32 [2, 2, 1024], P(None, None, ('rows', 'blk'))
- norm_shift_grad: float32 [2, 2, 1024], P(None, None, ('rows', 'blk'))
Inputs may be any that keep to these rules, and one draw needn't show every extreme that they name: `segment_ids`: along each row the ids start at 0 and never fall; in every row one article starts within the first 256 positions and runs into the last 256.
All inputs are finite; a program needn't handle non-finite values.
Results may differ from a plain program's by a relative error of at most 0.025.
Values may be sent and summed in bfloat16 or wider, within the bound.
No kernel may reach another device: no remote copies, remote signals or barrier semaphores. Data moves between devices by JAX's collectives and lax.ppermute only.
A program may use at most 256 MiB of HBM per device.

v0:
```python
import math

import jax
import jax.numpy as jnp
from jax import lax
from jax.sharding import PartitionSpec as P

D = 1024
HEADS = 8
HEAD_DIM = 128


norm_eps = 1e-05
masked_score = -1e30


def layer_norm(values, gain, shift):
    centre = values - jnp.mean(values, axis=-1, keepdims=True)
    spread = jnp.mean(centre * centre, axis=-1, keepdims=True)
    return centre * lax.rsqrt(spread + norm_eps) * gain + shift


def head_slopes(heads):
    return jnp.exp2(-8.0 * (jnp.arange(heads, dtype=jnp.float32) + 1.0) / heads)


def block_scores(
    query_part, key_part, query_places, key_places, query_segments, key_segments, slopes
):
    scores = jnp.einsum(
        "qhd,khd->hqk", query_part, key_part, preferred_element_type=jnp.float32
    ) * HEAD_DIM ** (-0.5)
    distance = (query_places[:, None] - key_places[None, :]).astype(jnp.float32)
    scores = scores - slopes[:, None, None] * distance[None]
    allowed = (query_segments[:, None] == key_segments[None, :]) & (
        key_places[None, :] <= query_places[:, None]
    )
    return (scores, allowed)


def pair_grads(
    query_part,
    grad_part,
    log_total,
    delta_part,
    query_places,
    query_segments,
    key_part,
    value_part,
    key_places,
    key_segments,
    slopes,
):
    scores, allowed = block_scores(
        query_part, key_part, query_places, key_places, query_segments, key_segments, slopes
    )
    probs_block = jnp.where(allowed[None], jnp.exp(scores - log_total[..., None]), 0.0)
    grad_probs = jnp.einsum(
        "qhd,khd->hqk", grad_part, value_part, preferred_element_type=jnp.float32
    )
    grad_scores = (probs_block * (grad_probs - delta_part[..., None])).astype(jnp.bfloat16)
    scale = HEAD_DIM ** (-0.5)
    grad_query = (
        jnp.einsum("hqk,khd->qhd", grad_scores, key_part, preferred_element_type=jnp.float32)
        * scale
    )
    grad_key = (
        jnp.einsum("hqk,qhd->khd", grad_scores, query_part, preferred_element_type=jnp.float32)
        * scale
    )
    grad_value = jnp.einsum(
        "hqk,qhd->khd",
        probs_block.astype(jnp.bfloat16),
        grad_part,
        preferred_element_type=jnp.float32,
    )
    return (grad_query, grad_key, grad_value)


def split_blocks(array, block_width):
    return array.reshape((array.shape[0] // block_width, block_width) + array.shape[1:])


def attend(query_own, keys_all, values_all, query_places, query_segments, key_segments, slopes):
    length = keys_all.shape[0]
    block_width = math.gcd(length, 512)
    key_places = jnp.arange(length, dtype=jnp.int32)
    blocks = (
        split_blocks(keys_all, block_width),
        split_blocks(values_all, block_width),
        split_blocks(key_places, block_width),
        split_blocks(key_segments, block_width),
    )
    own_tokens = query_own.shape[0]

    def stat_step(carry, block_data):
        running_max, running_sum = carry
        key_block, value_block, place_block, segment_block = block_data
        scores, allowed = block_scores(
            query_own, key_block, query_places, place_block, query_segments, segment_block, slopes
        )
        masked = jnp.where(allowed[None], scores, masked_score)
        new_max = jnp.maximum(running_max, jnp.max(masked, axis=2))
        weights = jnp.where(allowed[None], jnp.exp(masked - new_max[..., None]), 0.0)
        running_sum = running_sum * jnp.exp(running_max - new_max) + jnp.sum(weights, axis=2)
        return ((new_max, running_sum), None)

    start_max = jnp.full((HEADS, own_tokens), masked_score, jnp.float32)
    start_sum = jnp.zeros((HEADS, own_tokens), jnp.float32)
    (running_max, running_sum), unused = lax.scan(stat_step, (start_max, start_sum), blocks)
    log_total = running_max + jnp.log(running_sum)

    def out_step(accumulated, block_data):
        key_block, value_block, place_block, segment_block = block_data
        scores, allowed = block_scores(
            query_own, key_block, query_places, place_block, query_segments, segment_block, slopes
        )
        probs_block = jnp.where(allowed[None], jnp.exp(scores - log_total[..., None]), 0.0).astype(
            jnp.bfloat16
        )
        return (
            accumulated
            + jnp.einsum(
                "hqk,khd->qhd", probs_block, value_block, preferred_element_type=jnp.float32
            ),
            None,
        )

    start_out = jnp.zeros((own_tokens, HEADS, HEAD_DIM), jnp.float32)
    attended, unused = lax.scan(out_step, start_out, blocks)
    return (attended, log_total)


def fetch_forward(
    qkv_weight,
    qv_bias,
    out_weight,
    out_bias,
    up_weight,
    up_bias,
    down_weight,
    down_bias,
    norm_gain,
    norm_shift,
    layer_index,
):
    return (
        lax.all_gather(qkv_weight[layer_index], ("rows", "blk"), axis=0, tiled=True),
        lax.all_gather(qv_bias[layer_index], ("rows", "blk"), axis=0, tiled=True),
        lax.all_gather(out_weight[layer_index], ("rows", "blk"), axis=0, tiled=True),
        lax.all_gather(out_bias[layer_index], ("rows", "blk"), axis=0, tiled=True),
        lax.all_gather(up_weight[layer_index], ("rows", "blk"), axis=0, tiled=True),
        lax.all_gather(up_bias[layer_index], ("rows", "blk"), axis=0, tiled=True),
        lax.all_gather(down_weight[layer_index], ("rows", "blk"), axis=0, tiled=True),
        lax.all_gather(down_bias[layer_index], ("rows", "blk"), axis=0, tiled=True),
        lax.all_gather(norm_gain[layer_index], ("rows", "blk"), axis=1, tiled=True),
        lax.all_gather(norm_shift[layer_index], ("rows", "blk"), axis=1, tiled=True),
    )


def fetch_backward(
    qkv_weight,
    qv_bias,
    out_weight,
    out_bias,
    up_weight,
    up_bias,
    down_weight,
    down_bias,
    norm_gain,
    norm_shift,
    layer_index,
):
    return (
        lax.all_gather(qkv_weight[layer_index], ("rows", "blk"), axis=0, tiled=True),
        lax.all_gather(qv_bias[layer_index], ("rows", "blk"), axis=0, tiled=True),
        lax.all_gather(out_weight[layer_index], ("rows", "blk"), axis=0, tiled=True),
        lax.all_gather(out_bias[layer_index], ("rows", "blk"), axis=0, tiled=True),
        lax.all_gather(up_weight[layer_index], ("rows", "blk"), axis=0, tiled=True),
        lax.all_gather(up_bias[layer_index], ("rows", "blk"), axis=0, tiled=True),
        lax.all_gather(down_weight[layer_index], ("rows", "blk"), axis=0, tiled=True),
        lax.all_gather(down_bias[layer_index], ("rows", "blk"), axis=0, tiled=True),
        lax.all_gather(norm_gain[layer_index], ("rows", "blk"), axis=1, tiled=True),
        lax.all_gather(norm_shift[layer_index], ("rows", "blk"), axis=1, tiled=True),
    )


def on_device(
    tokens,
    segment_ids,
    out_grad,
    qkv_weight,
    qv_bias,
    out_weight,
    out_bias,
    up_weight,
    up_bias,
    down_weight,
    down_bias,
    norm_gain,
    norm_shift,
):
    layer_count = qkv_weight.shape[0]
    own_tokens = tokens.shape[1]
    segments_own = segment_ids[0]
    query_places = lax.axis_index("blk") * own_tokens + jnp.arange(own_tokens, dtype=jnp.int32)
    slopes = head_slopes(HEADS)
    shards = (
        qkv_weight,
        qv_bias,
        out_weight,
        out_bias,
        up_weight,
        up_bias,
        down_weight,
        down_bias,
        norm_gain,
        norm_shift,
    )
    stream = tokens[0].astype(jnp.float32)
    stored = []
    for layer_index in range(layer_count):
        weights = fetch_forward(*shards, layer_index)
        w_qkv, b_qv, w_out, b_out, w_up, b_up, w_down, b_down, gains, shifts = weights
        normed = layer_norm(
            stream, gains[0].astype(jnp.float32), shifts[0].astype(jnp.float32)
        ).astype(jnp.bfloat16)
        bias_full = jnp.concatenate([b_qv[:D], jnp.zeros((D,), jnp.bfloat16), b_qv[D:]]).astype(
            jnp.float32
        )
        projected = (jnp.dot(normed, w_qkv, preferred_element_type=jnp.float32) + bias_full).astype(
            jnp.bfloat16
        )
        query_own = projected[:, :D].reshape(own_tokens, HEADS, HEAD_DIM)
        key_own = projected[:, D : 2 * D].reshape(own_tokens, HEADS, HEAD_DIM)
        value_own = projected[:, 2 * D :].reshape(own_tokens, HEADS, HEAD_DIM)
        keys_all, values_all, segments_all = (
            lax.all_gather(key_own, "blk", axis=0, tiled=True),
            lax.all_gather(value_own, "blk", axis=0, tiled=True),
            lax.all_gather(segments_own, "blk", axis=0, tiled=True),
        )
        attended, log_total = attend(
            query_own, keys_all, values_all, query_places, segments_own, segments_all, slopes
        )
        attended_low = attended.reshape(own_tokens, D).astype(jnp.bfloat16)
        middle = (
            stream
            + jnp.dot(attended_low, w_out, preferred_element_type=jnp.float32)
            + b_out.astype(jnp.float32)
        )
        normed_two = layer_norm(
            middle, gains[1].astype(jnp.float32), shifts[1].astype(jnp.float32)
        ).astype(jnp.bfloat16)
        pre_act = jnp.dot(normed_two, w_up, preferred_element_type=jnp.float32) + b_up.astype(
            jnp.float32
        )
        hidden = jax.nn.gelu(pre_act).astype(jnp.bfloat16)
        stored.append(
            (stream, normed, projected, log_total, attended, middle, normed_two, pre_act, hidden)
        )
        stream = (
            middle
            + jnp.dot(hidden, w_down, preferred_element_type=jnp.float32)
            + b_down.astype(jnp.float32)
        )
    final = stream.astype(jnp.bfloat16)[None]
    grad = out_grad[0].astype(jnp.float32)
    layer_grads = [None] * layer_count
    for layer_index in reversed(range(layer_count)):
        weights = fetch_backward(*shards, layer_index)
        w_qkv, b_qv, w_out, b_out, w_up, b_up, w_down, b_down, gains, shifts = weights
        stream_in, normed, projected, log_total, attended, middle, normed_two, pre_act, hidden = (
            stored[layer_index]
        )
        grad_update = grad.astype(jnp.bfloat16)
        grad_b_down = jnp.sum(grad_update.astype(jnp.float32), axis=0)
        grad_w_down = jnp.einsum(
            "tf,td->fd", hidden, grad_update, preferred_element_type=jnp.float32
        )
        grad_hidden = jnp.einsum(
            "td,fd->tf", grad_update, w_down, preferred_element_type=jnp.float32
        )
        unused, gelu_back = jax.vjp(jax.nn.gelu, pre_act)
        grad_pre = gelu_back(grad_hidden)[0].astype(jnp.bfloat16)
        grad_b_up = jnp.sum(grad_pre.astype(jnp.float32), axis=0)
        grad_w_up = jnp.einsum(
            "td,tf->df", normed_two, grad_pre, preferred_element_type=jnp.float32
        )
        grad_normed_two = jnp.einsum(
            "tf,df->td", grad_pre, w_up, preferred_element_type=jnp.float32
        )
        unused, norm_back = jax.vjp(
            layer_norm, middle, gains[1].astype(jnp.float32), shifts[1].astype(jnp.float32)
        )
        grad_from_norm, grad_gain_two, grad_shift_two = norm_back(grad_normed_two)
        grad_middle = grad + grad_from_norm
        grad_branch = grad_middle.astype(jnp.bfloat16)
        grad_b_out = jnp.sum(grad_branch.astype(jnp.float32), axis=0)
        attended_low = attended.reshape(own_tokens, D).astype(jnp.bfloat16)
        grad_w_out = jnp.einsum(
            "te,td->ed", attended_low, grad_branch, preferred_element_type=jnp.float32
        )
        grad_attended = jnp.einsum(
            "td,ed->te", grad_branch, w_out, preferred_element_type=jnp.float32
        )
        grad_attended = grad_attended.astype(jnp.bfloat16).reshape(own_tokens, HEADS, HEAD_DIM)
        delta = jnp.sum(grad_attended.astype(jnp.float32) * attended, axis=2).T
        query_own = projected[:, :D].reshape(own_tokens, HEADS, HEAD_DIM)
        key_own = projected[:, D : 2 * D].reshape(own_tokens, HEADS, HEAD_DIM)
        value_own = projected[:, 2 * D :].reshape(own_tokens, HEADS, HEAD_DIM)
        keys_all, values_all, segments_all = (
            lax.all_gather(key_own, "blk", axis=0, tiled=True),
            lax.all_gather(value_own, "blk", axis=0, tiled=True),
            lax.all_gather(segments_own, "blk", axis=0, tiled=True),
        )
        length = keys_all.shape[0]
        block_width = math.gcd(length, 512)
        row_places = jnp.arange(length, dtype=jnp.int32)
        key_blocks = (
            split_blocks(keys_all, block_width),
            split_blocks(values_all, block_width),
            split_blocks(row_places, block_width),
            split_blocks(segments_all, block_width),
        )

        def key_step(accumulated, block_data):
            key_block, value_block, place_block, segment_block = block_data
            grad_query, grad_key, grad_value = pair_grads(
                query_own,
                grad_attended,
                log_total,
                delta,
                query_places,
                segments_own,
                key_block,
                value_block,
                place_block,
                segment_block,
                slopes,
            )
            return (accumulated + grad_query, (grad_key, grad_value))

        start_query = jnp.zeros((own_tokens, HEADS, HEAD_DIM), jnp.float32)
        grad_query_own, key_terms = lax.scan(key_step, start_query, key_blocks)
        grad_key_own, grad_value_own = (
            lax.psum_scatter(
                key_terms[0].reshape(length, HEADS, HEAD_DIM).astype(jnp.bfloat16),
                "blk",
                scatter_dimension=0,
                tiled=True,
            ).astype(jnp.float32),
            lax.psum_scatter(
                key_terms[1].reshape(length, HEADS, HEAD_DIM).astype(jnp.bfloat16),
                "blk",
                scatter_dimension=0,
                tiled=True,
            ).astype(jnp.float32),
        )
        grad_projected = jnp.concatenate(
            [
                grad_query_own.reshape(own_tokens, D),
                grad_key_own.reshape(own_tokens, D),
                grad_value_own.reshape(own_tokens, D),
            ],
            axis=1,
        ).astype(jnp.bfloat16)
        grad_sums = jnp.sum(grad_projected.astype(jnp.float32), axis=0)
        grad_b_qv = jnp.concatenate([grad_sums[:D], grad_sums[2 * D :]])
        grad_w_qkv = jnp.einsum(
            "td,te->de", normed, grad_projected, preferred_element_type=jnp.float32
        )
        grad_normed = jnp.einsum(
            "te,de->td", grad_projected, w_qkv, preferred_element_type=jnp.float32
        )
        unused, norm_back = jax.vjp(
            layer_norm, stream_in, gains[0].astype(jnp.float32), shifts[0].astype(jnp.float32)
        )
        grad_from_norm, grad_gain_one, grad_shift_one = norm_back(grad_normed)
        grad = grad_middle + grad_from_norm
        layer_grads[layer_index] = (
            lax.psum_scatter(grad_w_qkv, ("rows", "blk"), scatter_dimension=0, tiled=True),
            lax.psum_scatter(grad_b_qv, ("rows", "blk"), scatter_dimension=0, tiled=True),
            lax.psum_scatter(grad_w_out, ("rows", "blk"), scatter_dimension=0, tiled=True),
            lax.psum_scatter(grad_b_out, ("rows", "blk"), scatter_dimension=0, tiled=True),
            lax.psum_scatter(grad_w_up, ("rows", "blk"), scatter_dimension=0, tiled=True),
            lax.psum_scatter(grad_b_up, ("rows", "blk"), scatter_dimension=0, tiled=True),
            lax.psum_scatter(grad_w_down, ("rows", "blk"), scatter_dimension=0, tiled=True),
            lax.psum_scatter(grad_b_down, ("rows", "blk"), scatter_dimension=0, tiled=True),
            lax.psum_scatter(
                jnp.stack([grad_gain_one, grad_gain_two]),
                ("rows", "blk"),
                scatter_dimension=1,
                tiled=True,
            ),
            lax.psum_scatter(
                jnp.stack([grad_shift_one, grad_shift_two]),
                ("rows", "blk"),
                scatter_dimension=1,
                tiled=True,
            ),
        )
    input_grad = grad.astype(jnp.bfloat16)[None]
    stacked = tuple(
        (
            jnp.stack([layer_grads[index][member] for index in range(layer_count)])
            for member in range(10)
        )
    )
    return (
        final,
        input_grad,
        stacked[0],
        stacked[1],
        stacked[2],
        stacked[3],
        stacked[4],
        stacked[5],
        stacked[6],
        stacked[7],
        stacked[8],
        stacked[9],
    )


def solution(mesh):
    in_specs = (
        P("rows", "blk", None),
        P("rows", "blk"),
        P("rows", "blk", None),
        P(None, ("rows", "blk"), None),
        P(None, ("rows", "blk")),
        P(None, ("rows", "blk"), None),
        P(None, ("rows", "blk")),
        P(None, ("rows", "blk"), None),
        P(None, ("rows", "blk")),
        P(None, ("rows", "blk"), None),
        P(None, ("rows", "blk")),
        P(None, None, ("rows", "blk")),
        P(None, None, ("rows", "blk")),
    )
    out_specs = (
        P("rows", "blk", None),
        P("rows", "blk", None),
        P(None, ("rows", "blk"), None),
        P(None, ("rows", "blk")),
        P(None, ("rows", "blk"), None),
        P(None, ("rows", "blk")),
        P(None, ("rows", "blk"), None),
        P(None, ("rows", "blk")),
        P(None, ("rows", "blk"), None),
        P(None, ("rows", "blk")),
        P(None, None, ("rows", "blk")),
        P(None, None, ("rows", "blk")),
    )
    return jax.shard_map(
        on_device, mesh=mesh, in_specs=in_specs, out_specs=out_specs, check_vma=False
    )
```

profile of v0, /device:TPU:0, one launch (start us, length us, event | category | flops | bytes accessed | tf_op | source)
XLA Modules:
  0.0 3957.6 jit_solution(16250627956179279235)
XLA Ops:
  12.7 42.6 %all-reduce.15 = (bf16[2048]{0:T(1024)(128)(2,1)S(1)}, bf16[1024]{0:T(1024)(128)(2,1)S(1)}, bf16[1024]{0:T(1024)(128)(2,1)S(1)}, bf16[2048]{0:T(1024)(128)(2,1)S...) all-reduce(bf16[2048]{0:T(1024)(128)(2,1)S(1)} %dynamic-update-slic, ...), channel_id=5, replica_groups=mesh['rows'=8,'blk'=4] {'rows','blk'}, use_global_device_ids=true, to_apply=%add | all-reduce | flops 8192 | bytes 32768
  56.9 73.4 %all-gather = bf16[1,2,1024]{1,0,2:T(2,128)(2,1)S(1)} all-gather(bf16[1,2,32]{1,0,2:T(2,128)(2,1)S(1)} %copy.165), channel_id=2, replica_groups=mesh['rows'=8,'blk'=4] {'rows','blk'}, dimensions={2}, use_global_device_ids=true | all-gather | bytes 4224 | tf_op jit(solution)/shard_map/all_gather | solution.py:156
  130.3 68.8 %all-gather.1 = bf16[1,2,1024]{1,0,2:T(2,128)(2,1)S(1)} all-gather(bf16[1,2,32]{1,0,2:T(2,128)(2,1)S(1)} %copy.166), channel_id=3, replica_groups=mesh['rows'=8,'blk'=4] {'rows','blk'}, dimensions={2}, use_global_device_ids=true | all-gather | bytes 4224 | tf_op jit(solution)/shard_map/all_gather | solution.py:157
  225.8 9.1 all-gather.4
  236.1 64.5 %all-gather.8 = bf16[1,4096]{1,0:T(2,128)(2,1)S(1)} all-gather(bf16[1,128]{1,0:T(2,128)(2,1)S(1)} %get-tuple-element.1137), channel_id=10, replica_groups=mesh['rows'=8,'blk'=4] {'rows','blk'}, dimensions={1}, use_global_device_ids=true | all-gather | bytes 8448 | tf_op jit(solution)/shard_map/all_gather | solution.py:153
  300.8 72.0 %all-gather.11 = bf16[1,2,1024]{1,0,2:T(2,128)(2,1)S(1)} all-gather(bf16[1,2,32]{1,0,2:T(2,128)(2,1)S(1)} %copy.167), channel_id=13, replica_groups=mesh['rows'=8,'blk'=4] {'rows','blk'}, dimensions={2}, use_global_device_ids=true | all-gather | bytes 4224 | tf_op jit(solution)/shard_map/all_gather | solution.py:156
  372.8 71.0 %all-gather.12 = bf16[1,2,1024]{1,0,2:T(2,128)(2,1)S(1)} all-gather(bf16[1,2,32]{1,0,2:T(2,128)(2,1)S(1)} %copy.168), channel_id=14, replica_groups=mesh['rows'=8,'blk'=4] {'rows','blk'}, dimensions={2}, use_global_device_ids=true | all-gather | bytes 4224 | tf_op jit(solution)/shard_map/all_gather | solution.py:157
  459.9 16.5 while.78
  476.5 14.4 while.79
  495.3 7.9 fusion.148
  503.2 31.3 all-gather.48.cloned.1.call-done
  534.5 7.5 fusion.288
  542.3 63.3 %all-gather.50.cloned.1.call-done = bf16[1,1024,3072]{2,1,0:T(8,128)(2,1)} async-done(((bf16[1,32,3072]{2,1,0:T(8,128)(2,1)}), bf16[1,1024,3072]{2,1,0:T(8,128)(2,1)}) %all-gather.50.cloned.1.call-update) | async-done | bytes 6291472 | tf_op jit(solution)/shard_map/all_gather | solution.py:148
  614.7 66.4 %all-gather.18 = bf16[1,4096]{1,0:T(2,128)(2,1)S(1)} all-gather(bf16[1,128]{1,0:T(2,128)(2,1)S(1)} %get-tuple-element.1136), channel_id=20, replica_groups=mesh['rows'=8,'blk'=4] {'rows','blk'}, dimensions={1}, use_global_device_ids=true | all-gather | bytes 8448 | tf_op jit(solution)/shard_map/all_gather | solution.py:153
  684.6 16.2 while.80
  703.1 12.5 while.81
  716.9 44.1 %all-gather.52.cloned.1.call-done = bf16[1,1024,1024]{2,1,0:T(8,128)(2,1)} async-done(((bf16[1,32,1024]{2,1,0:T(8,128)(2,1)}), bf16[1,1024,1024]{2,1,0:T(8,128)(2,1)}) %all-gather.52.cloned.1.call-update) | async-done | bytes 2097168 | tf_op jit(solution)/shard_map/all_gather | solution.py:150
  763.9 76.2 %all-gather.54.cloned.1.call-done = bf16[1,1024,4096]{2,1,0:T(8,128)(2,1)} async-done(((bf16[1,32,4096]{2,1,0:T(8,128)(2,1)}), bf16[1,1024,4096]{2,1,0:T(8,128)(2,1)}) %all-gather.54.cloned.1.call-update) | async-done | bytes 8388624 | tf_op jit(solution)/shard_map/all_gather | solution.py:152
  840.2 7.8 fusion.151
  848.0 71.6 %all-gather.56.cloned.1.call-done = bf16[1,4096,1024]{2,1,0:T(8,128)(2,1)} async-done(((bf16[1,128,1024]{2,1,0:T(8,128)(2,1)}), bf16[1,4096,1024]{2,1,0:T(8,128)(2,1)}) %all-gather.56.cloned.1.call-update) | async-done | bytes 8388624 | tf_op jit(solution)/shard_map/all_gather | solution.py:154
  919.6 12.3 convert_reduce_fusion
  942.0 30.6 while.82
  974.1 41.1 %reduce-scatter.27.cloned.1.call-done = bf16[256,8,128]{2,1,0:T(8,128)(2,1)} async-done(((bf16[1024,8,128]{2,1,0:T(8,128)(2,1)}), bf16[256,8,128]{2,1,0:T(8,128)(2,1)}) %reduce-scatter.27.cloned.1.call-update) | async-done | bytes 524304 | tf_op jit(solution)/shard_map/reduce_scatter | solution.py:352
  1016.4 44.3 %reduce-scatter.25.cloned.1.call-done = bf16[256,8,128]{2,1,0:T(8,128)(2,1)} async-done(((bf16[1024,8,128]{2,1,0:T(8,128)(2,1)}), bf16[256,8,128]{2,1,0:T(8,128)(2,1)}) %reduce-scatter.25.cloned.1.call-update) | async-done | bytes 524304 | tf_op jit(solution)/shard_map/reduce_scatter | solution.py:346
  1069.3 8.3 convert_reduce_fusion.1
  1089.5 31.1 while.83
  1126.7 37.4 reduce-scatter.31.cloned.1.call-done
  1165.2 44.3 %reduce-scatter.29.cloned.1.call-done = bf16[256,8,128]{2,1,0:T(8,128)(2,1)} async-done(((bf16[1024,8,128]{2,1,0:T(8,128)(2,1)}), bf16[256,8,128]{2,1,0:T(8,128)(2,1)}) %reduce-scatter.29.cloned.1.call-update) | async-done | bytes 524304 | tf_op jit(solution)/shard_map/reduce_scatter | solution.py:346
  1229.4 6.5 fusion.268
  1237.3 6.5 fusion.265
  1244.8 10.8 fusion.250
  1256.8 10.7 fusion.262
  1268.8 9.8 fusion.271
  1279.8 9.8 fusion.270
  1290.4 8.3 fusion.230
  1298.7 46.8 %reduce-scatter.55.cloned.1.call-done = f32[32,2]{1,0:T(8,128)} async-done(((f32[1024,2]{1,0:T(8,128)}), f32[32,2]{1,0:T(8,128)}) %reduce-scatter.55.cloned.1.call-update) | async-done | bytes 272
  1346.3 132.2 %reduce-scatter.51.cloned.1.call-done = f32[32,2]{1,0:T(8,128)} async-done(((f32[1024,2]{1,0:T(8,128)}), f32[32,2]{1,0:T(8,128)}) %reduce-scatter.51.cloned.1.call-update) | async-done | bytes 272
  1482.0 129.4 %reduce-scatter.53.cloned.1.call-done = f32[32,2]{1,0:T(8,128)} async-done(((f32[1024,2]{1,0:T(8,128)}), f32[32,2]{1,0:T(8,128)}) %reduce-scatter.53.cloned.1.call-update) | async-done | bytes 272
  1612.2 132.2 %reduce-scatter.49.cloned.1.call-done = f32[32,2]{1,0:T(8,128)} async-done(((f32[1024,2]{1,0:T(8,128)}), f32[32,2]{1,0:T(8,128)}) %reduce-scatter.49.cloned.1.call-update) | async-done | bytes 272
  1746.3 121.7 %all-reduce.18.cloned.1.call-done = (f32[2048]{0:T(1024)}, f32[2048]{0:T(1024)}, f32[1024]{0:T(1024)}, f32[1024]{0:T(1024)}, f32[4096]{0:T(1024)}, /*index=5*/f32[4096]{0:T(1024)}, f32[1024]{0:T(1024)}, f32[1024]{0:T(1024)}) async-done(((f32[2048]{0:T(1024)}, f32[2048]{0:T(1024)}, f32[1024]{0:T(1024)}, f32[1024]{0:T(1024)}, f32[4096]{0:T(1024)}, /*index=5*/f32[4096]{0:T(1024)}, f32[1024]{0:T(1024)}, ...) | async-done | bytes 65552
  1876.3 143.3 %reduce-scatter.39.cloned.1.call-done = f32[32,1024]{1,0:T(8,128)} async-done(((f32[1024,1024]{1,0:T(8,128)}), f32[32,1024]{1,0:T(8,128)}) %reduce-scatter.39.cloned.1.call-update) | async-done | bytes 131088 | tf_op jit(solution)/shard_map/reduce_scatter | solution.py:383
  2019.5 149.2 %reduce-scatter.37.cloned.1.call-done = f32[32,1024]{1,0:T(8,128)} async-done(((f32[1024,1024]{1,0:T(8,128)}), f32[32,1024]{1,0:T(8,128)}) %reduce-scatter.37.cloned.1.call-update) | async-done | bytes 131088 | tf_op jit(solution)/shard_map/reduce_scatter | solution.py:383
  2170.4 157.8 %reduce-scatter.35.cloned.1.call-done = f32[32,3072]{1,0:T(8,128)} async-done(((f32[1024,3072]{1,0:T(8,128)}), f32[32,3072]{1,0:T(8,128)}) %reduce-scatter.35.cloned.1.call-update) | async-done | bytes 393232 | tf_op jit(solution)/shard_map/reduce_scatter | solution.py:381
  2328.3 161.6 %reduce-scatter.33.cloned.1.call-done = f32[32,3072]{1,0:T(8,128)} async-done(((f32[1024,3072]{1,0:T(8,128)}), f32[32,3072]{1,0:T(8,128)}) %reduce-scatter.33.cloned.1.call-update) | async-done | bytes 393232 | tf_op jit(solution)/shard_map/reduce_scatter | solution.py:381
  2491.9 363.4 %reduce-scatter.47.cloned.1.call-done = f32[128,1024]{1,0:T(8,128)} async-done(((f32[4096,1024]{1,0:T(8,128)}), f32[128,1024]{1,0:T(8,128)}) %reduce-scatter.47.cloned.1.call-update) | async-done | bytes 524304 | tf_op jit(solution)/shard_map/reduce_scatter | solution.py:387
  2855.4 364.3 %reduce-scatter.45.cloned.1.call-done = f32[128,1024]{1,0:T(8,128)} async-done(((f32[4096,1024]{1,0:T(8,128)}), f32[128,1024]{1,0:T(8,128)}) %reduce-scatter.45.cloned.1.call-update) | async-done | bytes 524304 | tf_op jit(solution)/shard_map/reduce_scatter | solution.py:387
  3222.0 362.2 %reduce-scatter.43.cloned.1.call-done = f32[32,4096]{1,0:T(8,128)} async-done(((f32[1024,4096]{1,0:T(8,128)}), f32[32,4096]{1,0:T(8,128)}) %reduce-scatter.43.cloned.1.call-update) | async-done | bytes 524304 | tf_op jit(solution)/shard_map/reduce_scatter | solution.py:385
  3584.2 364.5 %reduce-scatter.41.cloned.1.call-done = f32[32,4096]{1,0:T(8,128)} async-done(((f32[1024,4096]{1,0:T(8,128)}), f32[32,4096]{1,0:T(8,128)}) %reduce-scatter.41.cloned.1.call-update) | async-done | bytes 524304 | tf_op jit(solution)/shard_map/reduce_scatter | solution.py:385
  (576 shorter events, 284.3 us)
Async XLA Ops:
  7.2 208.2 %copy-start.4 = (bf16[1,256,1024]{2,1,0:T(8,128)(2,1)S(1)}, bf16[1,256,1024]{2,1,0:T(8,128)(2,1)}, u32[]{:S(2)}) copy-start(bf16[1,256,1024]{2,1,0:T(8,128)(2,1)} %param.25) | copy-start | bytes 1572868
  7.2 207.7 %all-gather.42.cloned.1.call-start = ((), (), s32[]{:S(2)}) async-start(), calls=%async_computation.32 | async-start | bytes 6488064 | tf_op jit(solution)/shard_map/all_gather | solution.py:148
  9.1 447.4 %all-gather.36.cloned.1.call-start = ((), (), s32[]{:S(2)}) async-start(), calls=%async_computation.17 | async-start | bytes 2621440 | tf_op jit(solution)/shard_map/all_gather | solution.py:238
  208.5 286.8 %copy-start.64 = (f32[1024]{0:T(1024)}, f32[1024]{0:T(1024)S(1)}, u32[]{:S(2)}) copy-start(f32[1024]{0:T(1024)S(1)} %get-tuple-element.929) | copy-start | bytes 12292
  214.8 280.5 %copy-start.70 = (f32[1024]{0:T(1024)}, f32[1024]{0:T(1024)S(1)}, u32[]{:S(2)}) copy-start(f32[1024]{0:T(1024)S(1)} %get-tuple-element.931) | copy-start | bytes 12292
  221.4 255.0 %all-gather.34.cloned.1.call-start = ((), (), s32[]{:S(2)}) async-start(), calls=%async_computation.16 | async-start | bytes 2621440 | tf_op jit(solution)/shard_map/all_gather | solution.py:239
  222.4 270.0 %all-gather.44.cloned.1.call-start = ((), (), s32[]{:S(2)}) async-start(), calls=%async_computation.33 | async-start | bytes 2162688 | tf_op jit(solution)/shard_map/all_gather | solution.py:150
  223.1 272.1 %all-gather.46.cloned.1.call-start = ((), (), s32[]{:S(2)}) async-start(), calls=%async_computation.34 | async-start | bytes 8650752 | tf_op jit(solution)/shard_map/all_gather | solution.py:152
  224.1 310.4 %all-gather.48.cloned.1.call-start = ((), (), s32[]{:S(2)}) async-start(), calls=%async_computation.35 | async-start | bytes 8650752 | tf_op jit(solution)/shard_map/all_gather | solution.py:154
  225.0 380.6 %all-gather.50.cloned.1.call-start = ((), (), s32[]{:S(2)}) async-start(), calls=%async_computation.36 | async-start | bytes 6488064 | tf_op jit(solution)/shard_map/all_gather | solution.py:148
  225.7 455.5 %all-gather.40.cloned.1.call-start = ((), (), s32[]{:S(2)}) async-start(), calls=%async_computation.19 | async-start | bytes 2621440 | tf_op jit(solution)/shard_map/all_gather | solution.py:238
  450.1 484.9 %copy-start.66 = (f32[1024]{0:T(1024)}, f32[1024]{0:T(1024)S(1)}, u32[]{:S(2)}) copy-start(f32[1024]{0:T(1024)S(1)} %get-tuple-element.925) | copy-start | bytes 12292
  456.4 149.2 %copy-start.68 = (f32[1024]{0:T(1024)}, f32[1024]{0:T(1024)S(1)}, u32[]{:S(2)}) copy-start(f32[1024]{0:T(1024)S(1)} %get-tuple-element.928) | copy-start | bytes 12292
  456.4 383.8 %copy-start.72 = (f32[1024]{0:T(1024)}, f32[1024]{0:T(1024)S(1)}, u32[]{:S(2)}) copy-start(f32[1024]{0:T(1024)S(1)} %get-tuple-element.927) | copy-start | bytes 12292
  542.0 68.3 %copy-start.9 = (f32[256,1024]{1,0:T(8,128)}, f32[256,1024]{1,0:T(8,128)S(1)}, u32[]{:S(2)}) copy-start(f32[256,1024]{1,0:T(8,128)S(1)} %get-tuple-element.1147) | copy-start | bytes 3145732
  611.3 91.7 %all-gather.38.cloned.1.call-start = ((), (), s32[]{:S(2)}) async-start(), calls=%async_computation.18 | async-start | bytes 2621440 | tf_op jit(solution)/shard_map/all_gather | solution.py:239
  612.7 148.2 %all-gather.52.cloned.1.call-start = ((), (), s32[]{:S(2)}) async-start(), calls=%async_computation.37 | async-start | bytes 2162688 | tf_op jit(solution)/shard_map/all_gather | solution.py:150
  613.3 226.9 %all-gather.54.cloned.1.call-start = ((), (), s32[]{:S(2)}) async-start(), calls=%async_computation.38 | async-start | bytes 8650752 | tf_op jit(solution)/shard_map/all_gather | solution.py:152
  614.0 305.5 %all-gather.56.cloned.1.call-start = ((), (), s32[]{:S(2)}) async-start(), calls=%async_computation.39 | async-start | bytes 8650752 | tf_op jit(solution)/shard_map/all_gather | solution.py:154
  614.6 400.7 %reduce-scatter.27.cloned.1.call-start = ((), (), s32[]{:S(2)}) async-start(), calls=%async_computation.21 | async-start | bytes 2621440 | tf_op jit(solution)/shard_map/reduce_scatter | solution.py:352
  716.9 131.1 %copy-start.30 = (bf16[256,8,128]{0,2,1:T(8,128)(2,1)}, bf16[256,8,128]{0,2,1:T(8,128)(2,1)S(1)}, u32[]{:S(2)}) copy-start(bf16[256,8,128]{0,2,1:T(8,128)(2,1)S(1)} %convert_element_type.260) | copy-start | bytes 1572868
  763.6 171.4 %copy-start.12 = (f32[256,1024]{1,0:T(8,128)}, f32[256,1024]{1,0:T(8,128)S(1)}, u32[]{:S(2)}) copy-start(f32[256,1024]{1,0:T(8,128)S(1)} %get-tuple-element.1149) | copy-start | bytes 3145732
  763.7 171.4 %copy-start.81 = (f32[256]{0:T(256)}, f32[256]{0:T(256)S(1)}, u32[]{:S(2)}) copy-start(f32[256]{0:T(256)S(1)} %broadcast_multiply_fusion) | copy-start | bytes 3076
  763.9 171.1 %copy-start.85 = (f32[256]{0:T(256)}, f32[256]{0:T(256)S(1)}, u32[]{:S(2)}) copy-start(f32[256]{0:T(256)S(1)} %fusion.261) | copy-start | bytes 3076
  840.2 79.4 %copy-start.43 = (bf16[1,256,1024]{2,1,0:T(8,128)(2,1)S(1)}, bf16[1,256,1024]{2,1,0:T(8,128)(2,1)}, u32[]{:S(2)}) copy-start(bf16[1,256,1024]{2,1,0:T(8,128)(2,1)} %param.27) | copy-start | bytes 1572868
  972.6 89.3 %copy-start.10 = (f32[256,1024]{1,0:T(8,128)S(1)}, f32[256,1024]{1,0:T(8,128)}, u32[]{:S(2)}) copy-start(f32[256,1024]{1,0:T(8,128)} %copy-done.9) | copy-start | bytes 3145732
  972.7 88.1 %reduce-scatter.25.cloned.1.call-start = ((), (), s32[]{:S(2)}) async-start(), calls=%async_computation.20 | async-start | bytes 2621440 | tf_op jit(solution)/shard_map/reduce_scatter | solution.py:346
  973.3 190.8 %reduce-scatter.31.cloned.1.call-start = ((), (), s32[]{:S(2)}) async-start(), calls=%async_computation.23 | async-start | bytes 2621440 | tf_op jit(solution)/shard_map/reduce_scatter | solution.py:352
  1120.7 88.8 %reduce-scatter.29.cloned.1.call-start = ((), (), s32[]{:S(2)}) async-start(), calls=%async_computation.22 | async-start | bytes 2621440 | tf_op jit(solution)/shard_map/reduce_scatter | solution.py:346
  1121.3 224.2 %reduce-scatter.55.cloned.1.call-start = ((), (), s32[]{:S(2)}) async-start(), calls=%async_computation.43 | async-start | bytes 540672
  1122.7 88.3 %copy-start.5 = (bf16[1,256,1024]{2,1,0:T(8,128)(2,1)S(1)}, bf16[1,256,1024]{2,1,0:T(8,128)(2,1)}, u32[]{:S(2)}) copy-start(bf16[1,256,1024]{2,1,0:T(8,128)(2,1)} %param.25) | copy-start | bytes 1572868
  1122.7 88.3 %copy-start.61 = (f32[1024]{0:T(1024)S(1)}, f32[1024]{0:T(1024)}, u32[]{:S(2)}) copy-start(f32[1024]{0:T(1024)} %copy-done.60) | copy-start | bytes 12292
  1122.7 88.3 %copy-start.76 = (f32[256]{0:T(256)S(1)}, f32[256]{0:T(256)}, u32[]{:S(2)}) copy-start(f32[256]{0:T(256)} %copy-done.75) | copy-start | bytes 3076
  1122.8 355.7 %reduce-scatter.51.cloned.1.call-start = ((), (), s32[]{:S(2)}) async-start(), calls=%async_computation.41 | async-start | bytes 540672
  1124.9 86.0 %copy-start.37 = (bf16[256,1024]{1,0:T(8,128)(2,1)}, bf16[256,1024]{1,0:T(8,128)(2,1)S(1)}, u32[]{:S(2)}) copy-start(bf16[256,1024]{1,0:T(8,128)(2,1)S(1)} %copy.138) | copy-start | bytes 1572868
  1126.0 485.4 %reduce-scatter.53.cloned.1.call-start = ((), (), s32[]{:S(2)}) async-start(), calls=%async_computation.42 | async-start | bytes 540672
  1217.8 526.6 %reduce-scatter.49.cloned.1.call-start = ((), (), s32[]{:S(2)}) async-start(), calls=%async_computation.40 | async-start | bytes 540672
  1220.7 647.3 %all-reduce.18.cloned.1.call-start = ((), (), s32[]{:S(2)}) async-start(), calls=%async_computation.44 | async-start | bytes 131072
  1221.5 798.1 %reduce-scatter.39.cloned.1.call-start = ((), (), s32[]{:S(2)}) async-start(), calls=%async_computation.27 | async-start | bytes 4325376 | tf_op jit(solution)/shard_map/reduce_scatter | solution.py:383
  1224.4 944.4 %reduce-scatter.37.cloned.1.call-start = ((), (), s32[]{:S(2)}) async-start(), calls=%async_computation.26 | async-start | bytes 4325376 | tf_op jit(solution)/shard_map/reduce_scatter | solution.py:383
  1228.2 1100.1 %reduce-scatter.35.cloned.1.call-start = ((), (), s32[]{:S(2)}) async-start(), calls=%async_computation.25 | async-start | bytes 12976128 | tf_op jit(solution)/shard_map/reduce_scatter | solution.py:381
  1235.9 1253.9 %reduce-scatter.33.cloned.1.call-start = ((), (), s32[]{:S(2)}) async-start(), calls=%async_computation.24 | async-start | bytes 12976128 | tf_op jit(solution)/shard_map/reduce_scatter | solution.py:381
  1243.8 1611.6 %reduce-scatter.47.cloned.1.call-start = ((), (), s32[]{:S(2)}) async-start(), calls=%async_computation.31 | async-start | bytes 17301504 | tf_op jit(solution)/shard_map/reduce_scatter | solution.py:387
  1255.6 1964.1 %reduce-scatter.45.cloned.1.call-start = ((), (), s32[]{:S(2)}) async-start(), calls=%async_computation.30 | async-start | bytes 17301504 | tf_op jit(solution)/shard_map/reduce_scatter | solution.py:387
  1267.6 2316.6 %reduce-scatter.43.cloned.1.call-start = ((), (), s32[]{:S(2)}) async-start(), calls=%async_computation.29 | async-start | bytes 17301504 | tf_op jit(solution)/shard_map/reduce_scatter | solution.py:385
  1278.6 2670.0 %reduce-scatter.41.cloned.1.call-start = ((), (), s32[]{:S(2)}) async-start(), calls=%async_computation.28 | async-start | bytes 17301504 | tf_op jit(solution)/shard_map/reduce_scatter | solution.py:385
  1290.4 188.8 %copy-start.16 = (f32[256,1024]{1,0:T(8,128)S(1)}, f32[256,1024]{1,0:T(8,128)}, u32[]{:S(2)}) copy-start(f32[256,1024]{1,0:T(8,128)} %copy-done.14) | copy-start | bytes 3145732
  1290.4 188.8 %copy-start.88 = (f32[256]{0:T(256)S(1)}, f32[256]{0:T(256)}, u32[]{:S(2)}) copy-start(f32[256]{0:T(256)} %copy-done.87) | copy-start | bytes 3076
  (92 other events, 510.1 us)
Sparse Core Ops, SparseCore 0:
  11.5 73.3 all-gather.41
  221.6 43.9 all-gather.35
  267.7 47.0 all-gather.33
  317.6 55.5 all-gather.43
  376.0 78.5 all-gather.45
  457.9 76.5 all-gather.47
  537.4 68.1 all-gather.49
  611.5 44.5 all-gather.39
  658.2 44.7 all-gather.37
  705.8 55.0 all-gather.51
  763.9 76.2 all-gather.53
  843.5 75.9 all-gather.55
  972.8 42.4 reduce-scatter.26
  1017.5 43.1 reduce-scatter.24
  1120.8 43.1 reduce-scatter.30
  1166.3 43.1 reduce-scatter.28
  1211.7 133.7 reduce-scatter.54
  1347.7 130.7 reduce-scatter.50
  1480.7 130.7 reduce-scatter.52
  1613.6 130.7 reduce-scatter.48
  1751.4 116.5 all-reduce.17
  1870.3 149.2 reduce-scatter.38
  2021.8 146.8 reduce-scatter.36
  2174.6 153.6 reduce-scatter.34
  2335.3 154.4 reduce-scatter.32
  2492.0 363.2 reduce-scatter.46
  2857.5 362.1 reduce-scatter.44
  3222.0 362.1 reduce-scatter.42
  3586.5 362.1 reduce-scatter.40
where the time goes:
time: 3970 us; the launch traced here: 3960 us
  waiting for transfers between devices  3090 us (78%)
  blocking collectives  468 us (12%)
  matrix products  210 us (5%)
  local copies, waits for them, and re-layouts  96.7 us (2%)
  other arithmetic  75 us (2%)
    reduce_scatter x2, waiting for transfers between devices, on_device(): lax.psum_scatter(grad_w_down, ('rows', 'blk'), scatter_dimension=0, tiled...  728 us
    reduce_scatter x2, waiting for transfers between devices, on_device(): lax.psum_scatter(grad_w_up, ('rows', 'blk'), scatter_dimension=0, tiled=T...  727 us
    unnamed x34, waiting for transfers between devices  566 us
    reduce_scatter x2, waiting for transfers between devices, on_device(): lax.psum_scatter(grad_w_qkv, ('rows', 'blk'), scatter_dimension=0, tiled=...  319 us
    reduce_scatter x2, waiting for transfers between devices, on_device(): lax.psum_scatter(grad_w_out, ('rows', 'blk'), scatter_dimension=0, tiled=...  292 us
    all_gather x2, blocking collectives, fetch_forward(): lax.all_gather(norm_gain[layer_index], ('rows', 'blk'), axis=1, tiled=True)  145 us
    all_gather x2, blocking collectives, fetch_forward(): lax.all_gather(norm_shift[layer_index], ('rows', 'blk'), axis=1, tiled=True)  140 us
    all_gather x2, blocking collectives, fetch_forward(): lax.all_gather(up_bias[layer_index], ('rows', 'blk'), axis=0, tiled=True)  131 us
  transfers between devices with their start and end apart: 29, of which 23 were waited for; matrix products, arithmetic and copies ran while one was open for 6% of the time, Pallas kernels for 0%

commit v1 on v0

v1 whole, which is shorter than its diff:
```python
import functools

import jax
import jax.numpy as jnp
from jax import lax
from jax.experimental import pallas as pl
from jax.experimental.pallas import tpu as pltpu
from jax.sharding import Mesh
from jax.sharding import PartitionSpec as P

D = 1024
HEADS = 8
HEAD_DIM = 128
CORES = 2
norm_eps = 1e-05
masked_score = -1e30
BF = jnp.bfloat16
F32 = jnp.float32
VMEM_BYTES = 48 * 1024 * 1024

HI, XX, CORE, BLK = "hi", "xx", "core", "blk"


def nn(a, b):
    return lax.dot_general(a, b, (((1,), (0,)), ((), ())), preferred_element_type=F32)


def nt(a, b):
    return lax.dot_general(a, b, (((1,), (1,)), ((), ())), preferred_element_type=F32)


def tn(a, b):
    return lax.dot_general(a, b, (((0,), (0,)), ((), ())), preferred_element_type=F32)


def shape(dims, dtype):
    return jax.ShapeDtypeStruct(tuple(dims), dtype)


def run(kernel, outs, smem, arrays, scratch=(), flops=0, trans=0):
    size = lambda s: s.size * s.dtype.itemsize
    moved = sum(size(a) for a in arrays) + sum(size(o) for o in outs)
    return pl.pallas_call(
        kernel,
        out_shape=tuple(outs),
        in_specs=[pl.BlockSpec(memory_space=pltpu.SMEM)] * len(smem)
        + [pl.BlockSpec(memory_space=pltpu.VMEM)] * len(arrays),
        out_specs=tuple(pl.BlockSpec(memory_space=pltpu.VMEM) for _ in outs),
        scratch_shapes=list(scratch),
        compiler_params=pltpu.CompilerParams(vmem_limit_bytes=VMEM_BYTES),
        cost_estimate=pl.CostEstimate(flops=flops, bytes_accessed=moved, transcendentals=trans),
    )(*smem, *arrays)


def slots_of(xs):
    return [(k, dc) for k in range(xs) for dc in range(CORES)]


def lo_minus(me, xs, k, dc):
    return lax.rem(me[1] - k + xs, xs) * CORES + lax.rem(me[2] + dc, CORES)


def lo_plus(me, xs, k, dc):
    return lax.rem(me[1] + k, xs) * CORES + lax.rem(me[2] + dc, CORES)


def shift(x, axis, size, step):
    return lax.ppermute(x, axis, [(i, (i + step) % size) for i in range(size)])


def gather_lo(x, xs):
    out = {}
    for k in range(xs):
        out[k, 0] = x if k == 0 else shift(x, XX, xs, k)
    for k in range(xs):
        out[k, 1] = shift(out[k, 0], CORE, CORES, 1)
    return out


def scatter_lo(parts, xs):
    got = {}
    for k in list(range(1, xs)) + [0]:
        got[k] = shift(parts[k, 1].astype(BF), CORE, CORES, 1)
    terms = [parts[0, 0]]
    for k in range(1, xs):
        both = (parts[k, 0].astype(F32) + got[k].astype(F32)).astype(BF)
        terms.append(shift(both, XX, xs, -k))
    return terms + [got[0]]


def exchange_lo(blocks, xs, sign):
    got, out = {}, {}
    for k in list(range(1, xs)) + [0]:
        got[k] = shift(blocks[k, 1], CORE, CORES, 1)
    for k in range(xs):
        out[k, 0] = blocks[k, 0] if k == 0 else shift(blocks[k, 0], XX, xs, sign * k)
        out[k, 1] = got[k] if k == 0 else shift(got[k], XX, xs, sign * k)
    return out


def gather_hb(x, hs, ts):
    out = {}
    for kh in range(1, hs):
        out[kh, 0] = shift(x, HI, hs, kh)
    for kb in range(ts):
        out[0, kb] = x if kb == 0 else shift(x, BLK, ts, kb)
    for kh in range(1, hs):
        for kb in range(1, ts):
            out[kh, kb] = shift(out[0, kb], HI, hs, kh)
    return out


def scatter_hb(by_hi, hs, ts):
    got = [shift(by_hi[kh], HI, hs, kh) for kh in range(1, hs)]
    total = []
    for kb in range(ts):
        block = by_hi[0][kb].astype(F32)
        for g in got:
            block = block + g[kb].astype(F32)
        total.append(block)
    return [total[0]] + [shift(total[kb].astype(BF), BLK, ts, kb) for kb in range(1, ts)]


def norm_parts(values):
    centre = values - jnp.mean(values, axis=-1, keepdims=True)
    spread = jnp.mean(centre * centre, axis=-1, keepdims=True)
    rstd = lax.rsqrt(spread + norm_eps)
    return centre * rstd, rstd


def entry_kernel(tok, gain, shft, stream, normed):
    values = tok[...].astype(F32)
    stream[...] = values
    unit, _ = norm_parts(values)
    normed[...] = (unit * gain[...] + shft[...]).astype(BF)


def entry(tok, gain, shft):
    n = tok.shape[0]
    return run(entry_kernel, [shape((n, D), F32), shape((n, D), BF)], [], [tok, gain, shft])


def cut_kernel(xs, ts, layers, me, wq, wu, *outs):
    hs = wu.shape[2] // (ts * (outs[1].shape[1] // 1)) if False else None
    at = 0
    for layer in range(layers):
        for k, dc in slots_of(xs):
            lo = lo_plus(me, xs, k, dc)
            out_q, out_u = outs[at], outs[at + 1]
            at += 2
            wide = out_q.shape[1] // 3
            for j in range(3):
                off = pl.multiple_of(j * D + lo * wide, 128)
                out_q[:, j * wide : (j + 1) * wide] = wq[layer, :, pl.ds(off, wide)]
            full = wu.shape[2]
            mine = out_u.shape[1]
            parts = full // (ts * mine) if full // (ts * mine) > 0 else 1
            chunk = mine // 2
            for j in range(2):
                off = pl.multiple_of(j * (full // 2) + lo * chunk, 128)
                out_u[:, j * chunk : (j + 1) * chunk] = wu[layer, :, pl.ds(off, chunk)]


def cut(me, wq, wu, xs, ts):
    layers, rows, full = wu.shape
    outs = []
    for _ in range(layers):
        for _ in slots_of(xs):
            outs += [shape((rows, 3 * D // ts), BF), shape((rows, full // ts), BF)]
    got = run(functools.partial(cut_kernel, xs, ts, layers), outs, [me], [wq, wu])
    blocks = []
    at = 0
    for _ in range(layers):
        q, u = {}, {}
        for s in slots_of(xs):
            q[s], u[s] = got[at], got[at + 1]
            at += 2
        blocks.append((q, u))
    return blocks


def place_kernel(hs, ts, xs, me, *refs):
    out = refs[-1]
    at = 0
    for kh in range(hs):
        h = lax.rem(me[0] - kh + hs, hs)
        for kb in range(ts):
            b = lax.rem(me[3] - kb + ts, ts)
            if xs is None:
                out[h, b] = refs[at][...]
                at += 1
            else:
                for k, dc in slots_of(xs):
                    out[h, lo_minus(me, xs, k, dc), b] = refs[at][...]
                    at += 1


def place(me, pieces, hs, ts, xs):
    arrays = []
    for kh in range(hs):
        for kb in range(ts):
            if xs is None:
                arrays.append(pieces[kh, kb])
            else:
                arrays += [pieces[kh, kb][s] for s in slots_of(xs)]
    rows, cols = arrays[0].shape
    lead = (hs, ts) if xs is None else (hs, ts, ts)
    (out,) = run(
        functools.partial(place_kernel, hs, ts, xs), [shape(lead + (rows, cols), BF)], [me], arrays
    )
    return out.reshape(-1, cols)


def attn_fwd_kernel(ts, xs, heads, me, slopes, *refs):
    normed = refs[:ts]
    w, bias, seg_row, seg_col, qkv, out_t, lse = refs[ts : ts + 7]
    outs = refs[ts + 7 :]
    n = normed[0].shape[0]
    width = heads * HEAD_DIM
    for j, (k, dc) in enumerate(slots_of(xs)):
        lo = lo_minus(me, xs, k, dc)
        got = nn(normed[j][...], w[...]) + bias[...]
        qkv[pl.ds(pl.multiple_of(lo * n, n), n), :] = got.astype(BF)
    scale = HEAD_DIM ** (-0.5)
    for i in range(ts):
        length = (i + 1) * n
        key_at = lax.broadcasted_iota(jnp.int32, (length, n), 0)
        query_at = lax.broadcasted_iota(jnp.int32, (length, n), 1) + i * n
        allowed = (seg_col[:length, :] == seg_row[:, i * n : length]) & (key_at <= query_at)
        distance = (query_at - key_at).astype(F32)
        for h in range(heads):
            here = h * HEAD_DIM
            q = qkv[i * n : length, here : here + HEAD_DIM]
            keys = qkv[:length, width + here : width + here + HEAD_DIM]
            values = qkv[:length, 2 * width + here : 2 * width + here + HEAD_DIM]
            s = nt(keys, q) * scale - slopes[h] * distance
            s = jnp.where(allowed, s, masked_score)
            top = jnp.max(s, axis=0, keepdims=True)
            p = jnp.exp(s - top)
            total = jnp.sum(p, axis=0, keepdims=True)
            out_t[here : here + HEAD_DIM, i * n : length] = tn(values, p.astype(BF)) / total
            lse[h : h + 1, i * n : length] = top + jnp.log(total)
    for j, (k, dc) in enumerate(slots_of(xs)):
        off = pl.multiple_of(lo_minus(me, xs, k, dc) * n, n)
        outs[j][...] = out_t[:, pl.ds(off, n)].T.astype(BF)


def attn_fwd(me, slopes, normed, w, bias, seg_row, seg_col, xs):
    ts = len(normed)
    heads = slopes.shape[0]
    n = normed[0].shape[0]
    length, width = ts * n, heads * HEAD_DIM
    got = run(
        functools.partial(attn_fwd_kernel, ts, xs, heads),
        [shape((length, 3 * width), BF), shape((width, length), F32), shape((heads, length), F32)]
        + [shape((n, width), BF)] * ts,
        [me, slopes],
        normed + [w, bias, seg_row, seg_col],
        flops=2 * length * D * 3 * width + 3 * length * length * width,
    )
    return got[0], got[1], got[2], list(got[3:])


def attn_bwd_kernel(ts, xs, heads, me, slopes, *refs):
    grads = refs[:ts]
    qkv, out_t, lse, w, seg_row, seg_col = refs[ts : ts + 6]
    parts = refs[ts + 6 : 2 * ts + 6]
    souts = refs[2 * ts + 6 : 3 * ts + 6]
    gbuf, dq_buf, dk_buf, dv_buf = refs[3 * ts + 6 :]
    n = grads[0].shape[0]
    width = heads * HEAD_DIM
    scale = HEAD_DIM ** (-0.5)
    for j, (k, dc) in enumerate(slots_of(xs)):
        off = pl.multiple_of(lo_minus(me, xs, k, dc) * n, n)
        gbuf[pl.ds(off, n), :] = grads[j][...]
    dk_buf[...] = jnp.zeros_like(dk_buf)
    dv_buf[...] = jnp.zeros_like(dv_buf)
    for i in range(ts):
        length = (i + 1) * n
        key_at = lax.broadcasted_iota(jnp.int32, (length, n), 0)
        query_at = lax.broadcasted_iota(jnp.int32, (length, n), 1) + i * n
        allowed = (seg_col[:length, :] == seg_row[:, i * n : length]) & (key_at <= query_at)
        distance = (query_at - key_at).astype(F32)
        for h in range(heads):
            here = h * HEAD_DIM
            q = qkv[i * n : length, here : here + HEAD_DIM]
            keys = qkv[:length, width + here : width + here + HEAD_DIM]
            values = qkv[:length, 2 * width + here : 2 * width + here + HEAD_DIM]
            g = gbuf[i * n : length, here : here + HEAD_DIM]
            delta = jnp.sum(
                g.astype(F32).T * out_t[here : here + HEAD_DIM, i * n : length], axis=0, keepdims=True
            )
            s = nt(keys, q) * scale - slopes[h] * distance
            p = jnp.where(allowed, jnp.exp(s - lse[h : h + 1, i * n : length]), 0.0)
            ds = (p * (nt(values, g) - delta)).astype(BF)
            dq_buf[i * n : length, here : here + HEAD_DIM] = tn(ds, keys) * scale
            dk_buf[:length, here : here + HEAD_DIM] += nn(ds, q)
            dv_buf[:length, here : here + HEAD_DIM] += nn(p.astype(BF), g)
    for j, (k, dc) in enumerate(slots_of(xs)):
        off = pl.multiple_of(lo_minus(me, xs, k, dc) * n, n)
        rows = pl.ds(off, n)
        parts[j][:, :width] = dq_buf[rows, :].astype(BF)
        parts[j][:, width : 2 * width] = (dk_buf[rows, :] * scale).astype(BF)
        parts[j][:, 2 * width :] = dv_buf[rows, :].astype(BF)
        souts[j][...] = nt(parts[j][...], w[...]).astype(souts[j].dtype)


def attn_bwd(me, slopes, grads, qkv, out_t, lse, w, seg_row, seg_col, xs):
    ts = len(grads)
    heads = slopes.shape[0]
    n = grads[0].shape[0]
    length, width = ts * n, heads * HEAD_DIM
    got = run(
        functools.partial(attn_bwd_kernel, ts, xs, heads),
        [shape((n, 3 * width), BF)] * ts + [shape((n, D), F32)] + [shape((n, D), BF)] * (ts - 1),
        [me, slopes],
        grads + [qkv, out_t, lse, w, seg_row, seg_col],
        scratch=[pltpu.VMEM((length, width), BF)] + [pltpu.VMEM((length, width), F32)] * 3,
        flops=2 * length * D * 3 * width + 6 * length * length * width,
    )
    return list(got[:ts]), list(got[ts:])


def out_kernel(ts, xs, me, *refs):
    heads = refs[:ts]
    w, bias, stream, gain, shft, middle, normed = refs[ts:]
    width = heads[0].shape[1]
    total = stream[...] + bias[...]
    for j, (k, dc) in enumerate(slots_of(xs)):
        off = pl.multiple_of(lo_plus(me, xs, k, dc) * width, width)
        total = total + nn(heads[j][...], w[pl.ds(off, width), :])
    middle[...] = total
    unit, _ = norm_parts(total)
    normed[...] = (unit * gain[...] + shft[...]).astype(BF)


def out_project(me, heads, w, bias, stream, gain, shft, xs):
    n = stream.shape[0]
    return run(
        functools.partial(out_kernel, len(heads), xs),
        [shape((n, D), F32), shape((n, D), BF)],
        [me],
        heads + [w, bias, stream, gain, shft],
        flops=2 * n * D * D,
    )


def ffn_fwd_kernel(count, *refs):
    normed = refs[:count]
    up, bias, down = refs[count : count + 3]
    outs = refs[count + 3 :]
    root, cubic = 0.7978845608028654, 0.044715
    for j in range(count):
        hidden, slope, part = outs[3 * j : 3 * j + 3]
        u = nn(normed[j][...], up[...]) + bias[...]
        square = u * u
        t = jnp.tanh(root * (u + cubic * square * u))
        half = 0.5 * (1.0 + t)
        hidden[...] = (u * half).astype(BF)
        slope[...] = (half + 0.5 * u * (1.0 - t * t) * (root * (1.0 + 3.0 * cubic * square))).astype(BF)
        part[...] = nn(hidden[...], down[...]).astype(part.dtype)


def ffn_fwd(normed, up, bias, down, kinds):
    n = normed[0].shape[0]
    wide = up.shape[1]
    outs = []
    for kind in kinds:
        outs += [shape((n, wide), BF), shape((n, wide), BF), shape((n, D), kind)]
    got = run(
        functools.partial(ffn_fwd_kernel, len(normed)),
        outs,
        [],
        normed + [up, bias, down],
        flops=4 * n * D * wide * len(normed),
    )
    return list(got[0::3]), list(got[1::3]), list(got[2::3])


def ffn_bwd_kernel(count, *refs):
    grads, slopes = refs[:count], refs[count : 2 * count]
    up, down = refs[2 * count : 2 * count + 2]
    outs = refs[2 * count + 2 :]
    for j in range(count):
        du, part = outs[2 * j : 2 * j + 2]
        du[...] = (nt(grads[j][...], down[...]) * slopes[j][...].astype(F32)).astype(BF)
        part[...] = nt(du[...], up[...]).astype(part.dtype)


def ffn_bwd(grads, slopes, up, down, kinds):
    n = grads[0].shape[0]
    wide = up.shape[1]
    outs = []
    for kind in kinds:
        outs += [shape((n, wide), BF), shape((n, D), kind)]
    got = run(
        functools.partial(ffn_bwd_kernel, len(grads)),
        outs,
        [],
        grads + slopes + [up, down],
        flops=4 * n * D * wide * len(grads),
    )
    return list(got[0::2]), list(got[1::2])


def end_kernel(count, last, *refs):
    terms = refs[:count]
    middle, bias = refs[count : count + 2]
    total = middle[...] + bias[...]
    for t in terms:
        total = total + t[...].astype(F32)
    if last:
        refs[-1][...] = total.astype(BF)
        return
    gain, shft, stream, normed = refs[count + 2 :]
    stream[...] = total
    unit, _ = norm_parts(total)
    normed[...] = (unit * gain[...] + shft[...]).astype(BF)


def layer_end(terms, middle, bias, norm):
    n = middle.shape[0]
    outs = [shape((n, D), BF)] if norm is None else [shape((n, D), F32), shape((n, D), BF)]
    return run(
        functools.partial(end_kernel, len(terms), norm is None),
        outs,
        [],
        terms + [middle, bias] + ([] if norm is None else list(norm)),
    )


def norm_back(values, gain, grad):
    unit, rstd = norm_parts(values)
    scaled = grad * gain
    lead = jnp.mean(scaled, axis=-1, keepdims=True)
    along = jnp.mean(scaled * unit, axis=-1, keepdims=True)
    back = rstd * (scaled - lead - unit * along)
    return back, jnp.sum(grad * unit, axis=0, keepdims=True), jnp.sum(grad, axis=0, keepdims=True)


def mid_back_kernel(count, ts, xs, me, *refs):
    terms = refs[:count]
    grad, middle, gain, w = refs[count : count + 4]
    dh, dy, sums = refs[count + 4 : count + 7]
    outs = refs[count + 7 :]
    total = terms[0][...].astype(F32)
    for t in terms[1:]:
        total = total + t[...].astype(F32)
    back, gains, shifts = norm_back(middle[...], gain[...], total)
    now = grad[...].astype(F32) + back
    dh[...] = now
    dy[...] = now.astype(BF)
    sums[0:1, :] = gains
    sums[1:2, :] = shifts
    sums[2:3, :] = jnp.sum(dy[...].astype(F32), axis=0, keepdims=True)
    width = outs[0].shape[1]
    for j, (k, dc) in enumerate(slots_of(xs)):
        off = pl.multiple_of(lo_plus(me, xs, k, dc) * width, width)
        outs[j][...] = nt(dy[...], w[pl.ds(off, width), :]).astype(BF)


def mid_back(me, terms, grad, middle, gain, w, ts, xs):
    n = middle.shape[0]
    got = run(
        functools.partial(mid_back_kernel, len(terms), ts, xs),
        [shape((n, D), F32), shape((n, D), BF), shape((3, D), F32)] + [shape((n, D // ts), BF)] * ts,
        [me],
        terms + [grad, middle, gain, w],
        flops=2 * n * D * D,
    )
    return got[0], got[1], got[2], list(got[3:])


def start_back_kernel(count, *refs):
    terms = refs[:count]
    grad, stream, gain, dh, dz, sums = refs[count:]
    total = terms[0][...].astype(F32)
    for t in terms[1:]:
        total = total + t[...].astype(F32)
    back, gains, shifts = norm_back(stream[...], gain[...], total)
    now = grad[...] + back
    dh[...] = now
    dz[...] = now.astype(BF)
    sums[0:1, :] = gains
    sums[1:2, :] = shifts
    sums[2:3, :] = jnp.sum(dz[...].astype(F32), axis=0, keepdims=True)


def start_back(terms, grad, stream, gain):
    n = stream.shape[0]
    return run(
        functools.partial(start_back_kernel, len(terms)),
        [shape((n, D), F32), shape((n, D), BF), shape((3, D), F32)],
        [],
        terms + [grad, stream, gain],
    )


def wgrad_cols_kernel(ts, xs, hs, rows, me, *refs):
    left, right = refs[:ts], refs[ts : 2 * ts]
    sums = refs[2 * ts]
    outs = refs[2 * ts + 1 :]
    total = jnp.sum(right[0][...].astype(F32), axis=0, keepdims=True)
    for b in right[1:]:
        total = total + jnp.sum(b[...].astype(F32), axis=0, keepdims=True)
    sums[...] = total
    tile = CORES * ts * rows
    for kh in list(range(1, hs)) + [0]:
        h = lax.rem(me[0] + kh, hs)
        for k in range(xs):
            place_at = (h * ts + lax.rem(me[1] + k, xs) * CORES) * ts * rows
            cols = pl.ds(pl.multiple_of(place_at, tile), tile)
            got = tn(left[0][:, cols], right[0][...])
            for j in range(1, ts):
                got = got + tn(left[j][:, cols], right[j][...])
            for c in range(CORES):
                dc = lax.rem(me[2] + c, CORES)
                for b in range(ts):
                    kb = lax.rem(b - me[3] + ts, ts)
                    at = (c * ts + b) * rows
                    outs[kh][kb, dc, k] = got[at : at + rows, :].astype(BF)


def wgrad_cols(me, left, right, hs, xs):
    ts = len(left)
    rows = D // (hs * ts * ts)
    n, wide = right[0].shape
    got = run(
        functools.partial(wgrad_cols_kernel, ts, xs, hs, rows),
        [shape((1, wide), F32)] + [shape((ts, CORES, xs, rows, wide), BF)] * hs,
        [me],
        left + right,
        flops=2 * ts * n * D * wide,
    )
    return got[0], list(got[1:])


def wgrad_rows_kernel(ts, hs, rows, me, *refs):
    left, right = refs[:ts], refs[ts : 2 * ts]
    outs = refs[2 * ts :]
    group = min(ts, max(1, 256 // rows))
    for kh in list(range(1, hs)) + [0]:
        h = lax.rem(me[0] + kh, hs)
        for first in range(0, ts, group):
            cols = pl.ds(pl.multiple_of((h * ts + first) * rows, group * rows), group * rows)
            got = tn(left[0][:, cols], right[0][...])
            for j in range(1, ts):
                got = got + tn(left[j][:, cols], right[j][...])
            for b in range(group):
                kb = lax.rem(first + b - me[3] + ts, ts)
                outs[kh][kb] = got[b * rows : (b + 1) * rows, :].astype(BF)


def wgrad_rows(me, left, right, hs):
    ts = len(left)
    n, wide = left[0].shape
    rows = wide // (hs * ts)
    return list(
        run(
            functools.partial(wgrad_rows_kernel, ts, hs, rows),
            [shape((ts, rows, D), BF)] * hs,
            [me],
            left + right,
            flops=2 * ts * n * D * wide,
        )
    )


def wgrad_out_kernel(ts, xs, hs, rows, me, *refs):
    left = refs[:ts]
    right, out = refs[ts], refs[ts + 1]
    width = left[0].shape[1]
    for j, (k, dc) in enumerate(slots_of(xs)):
        got = tn(left[j][...], right[...])
        first = lo_plus(me, xs, k, dc) * (width // rows)
        for g in range(width // rows):
            i = first + g
            h = lax.div(i, ts * ts)
            lo = lax.rem(lax.div(i, ts), ts)
            b = lax.rem(i, ts)
            kk = lax.rem(lax.div(lo, CORES) - me[1] + xs, xs)
            dd = lax.rem(lax.rem(lo, CORES) + me[2], CORES)
            kh = lax.rem(h - me[0] + hs, hs)
            kb = lax.rem(b - me[3] + ts, ts)
            out[dd, kk, kh, kb] = got[g * rows : (g + 1) * rows, :].astype(BF)


def wgrad_out(me, left, right, hs, xs):
    ts = len(left)
    rows = D // (hs * ts * ts)
    (got,) = run(
        functools.partial(wgrad_out_kernel, ts, xs, hs, rows),
        [shape((CORES, xs, hs, ts, rows, D), BF)],
        [me],
        left + [right],
        flops=2 * right.shape[0] * D * D,
    )
    return got


def join_kernel(ts, xs, layers, me, *refs):
    out_q, out_u = refs[-2:]
    at = 0
    for layer in range(layers):
        for k, dc in slots_of(xs):
            lo = lo_minus(me, xs, k, dc)
            q, u = refs[at], refs[at + 1]
            at += 2
            wide = q.shape[1] // 3
            for j in range(3):
                off = pl.multiple_of(j * D + lo * wide, 128)
                out_q[layer, :, pl.ds(off, wide)] = q[:, j * wide : (j + 1) * wide].astype(F32)
            chunk = u.shape[1] // 2
            for j in range(2):
                off = pl.multiple_of(j * (chunk * ts) + lo * chunk, 128)
                out_u[layer, :, pl.ds(off, chunk)] = u[:, j * chunk : (j + 1) * chunk].astype(F32)


def join(me, grads, ts, xs):
    layers = len(grads)
    arrays = []
    for q, u in grads:
        for s in slots_of(xs):
            arrays += [q[s], u[s]]
    rows = arrays[0].shape[0]
    return run(
        functools.partial(join_kernel, ts, xs, layers),
        [shape((layers, rows, arrays[0].shape[1] * ts), F32), shape((layers, rows, arrays[1].shape[1] * ts), F32)],
        [me],
        arrays,
    )


def gather_params(flat, index, hs, ts, xs):
    count = hs * ts * ts
    parts = [flat] + [shift(flat, BLK, ts, kb) for kb in range(1, ts)]
    stack = jnp.concatenate(parts, 0)
    stack = jnp.concatenate([stack] + [shift(stack, HI, hs, kh) for kh in range(1, hs)], 0)
    stack = jnp.concatenate([stack] + [shift(stack, XX, xs, k) for k in range(1, xs)], 0)
    stack = jnp.concatenate([stack, shift(stack, CORE, CORES, 1)], 0)
    hi, xx, core, blk = index
    dc, k, kh, kb = jnp.meshgrid(
        jnp.arange(CORES), jnp.arange(xs), jnp.arange(hs), jnp.arange(ts), indexing="ij"
    )
    lo = lax.rem(xx - k + xs, xs) * CORES + lax.rem(core + dc, CORES)
    owner = (lax.rem(hi - kh + hs, hs) * ts + lo) * ts + lax.rem(blk - kb + ts, ts)
    pick = (jnp.arange(count)[:, None] == owner.reshape(1, -1)).astype(BF)
    return jnp.dot(pick, stack, preferred_element_type=F32)


def sum_small(mine, shared, hs, ts, xs):
    mine = mine + shift(mine, CORE, CORES, 1)
    for_all = mine
    for k in range(1, xs):
        for_all = for_all + shift(mine, XX, xs, k)
    both = jnp.concatenate([for_all, shared], 0)
    total = both
    for kh in range(1, hs):
        total = total + shift(both, HI, hs, kh)
    out = total
    for kb in range(1, ts):
        out = out + shift(total, BLK, ts, kb)
    return out


def on_device(
    hs,
    ts,
    xs,
    tokens,
    segment_ids,
    out_grad,
    qkv_weight,
    qv_bias,
    out_weight,
    out_bias,
    up_weight,
    up_bias,
    down_weight,
    down_bias,
    norm_gain,
    norm_shift,
):
    layers = qkv_weight.shape[0]
    n = tokens.shape[1]
    length = ts * n
    heads = HEADS // ts
    index = tuple(lax.axis_index(a) for a in (HI, XX, CORE, BLK))
    hi, xx, core, blk = index
    lo = xx * CORES + core
    me = jnp.stack(index).astype(jnp.int32)
    slots = slots_of(xs)
    turn = [(a * ts + b, b * ts + a) for a in range(ts) for b in range(ts)]
    turned = lambda x: lax.ppermute(x, (XX, CORE, BLK), turn)

    tokens_own = turned(tokens[0])
    segments_own = turned(segment_ids)
    grad_own = turned(out_grad[0])

    flat = jnp.concatenate(
        [
            jnp.concatenate(
                [qv_bias[l], out_bias[l], up_bias[l], down_bias[l], norm_gain[l].reshape(-1), norm_shift[l].reshape(-1)]
            )
            for l in range(layers)
        ]
    )[None]
    params = gather_params(flat, index, hs, ts, xs)
    per = flat.shape[1] // layers
    sizes = [qv_bias.shape[1], out_bias.shape[1], up_bias.shape[1], down_bias.shape[1]] + [out_bias.shape[1]] * 4
    small = []
    for l in range(layers):
        at, fields = l * per, []
        for s in sizes:
            fields.append(params[:, at : at + s])
            at += s
        qv = lax.dynamic_index_in_dim(fields[0].reshape(2, ts, -1), lo, 1, False)
        up = lax.dynamic_index_in_dim(fields[2].reshape(hs, ts, -1), lo, 1, False)
        row = lambda x: x.reshape(1, -1)
        small.append(
            dict(
                qkv=row(jnp.concatenate([qv[0], jnp.zeros_like(qv[0]), qv[1]])),
                up=row(up),
                out=row(fields[1]),
                down=row(fields[3]),
                gains=[row(fields[4]), row(fields[5])],
                shifts=[row(fields[6]), row(fields[7])],
            )
        )

    cuts = cut(me, qkv_weight, up_weight, xs, ts)

    def fetch_cols(blocks):
        mine = exchange_lo(blocks, xs, 1)
        mine = jnp.stack([mine[s] for s in slots])
        got = gather_hb(mine, hs, ts)
        pieces = {key: {s: got[key][j] for j, s in enumerate(slots)} for key in got}
        return place(me, pieces, hs, ts, xs)

    def fetch_rows(block):
        return place(me, gather_hb(block, hs, ts), hs, ts, None)

    def fetch_out(block):
        got = gather_hb(block, hs, ts)
        mine = jnp.stack([got[kh, kb] for kh in range(hs) for kb in range(ts)])
        group = gather_lo(mine, xs)
        pieces = {
            (kh, kb): {s: group[s][kh * ts + kb] for s in slots} for kh in range(hs) for kb in range(ts)
        }
        return place(me, pieces, hs, ts, xs)

    weights = []
    for l in range(layers):
        weights.append(
            dict(
                qkv=fetch_cols(cuts[l][0]),
                out=fetch_out(out_weight[l]),
                up=fetch_cols(cuts[l][1]),
                down=fetch_rows(down_weight[l]),
            )
        )

    seg_by = gather_lo(segments_own, xs)
    seg = jnp.zeros((ts, n), jnp.int32)
    for s in slots:
        seg = lax.dynamic_update_slice(seg, seg_by[s], (lo_minus(me, xs, *s), 0))
    seg_row, seg_col = seg.reshape(1, length), seg.reshape(length, 1)
    slopes = jnp.exp2(-8.0 * (lo * heads + jnp.arange(heads, dtype=F32) + 1.0) / HEADS)

    stream, normed = entry(tokens_own, small[0]["gains"][0], small[0]["shifts"][0])
    stored = []
    for l in range(layers):
        w, sm = weights[l], small[l]
        by = gather_lo(normed, xs)
        all_one = [by[s] for s in slots]
        qkv, out_t, lse, heads_by = attn_fwd(me, slopes, all_one, w["qkv"], sm["qkv"], seg_row, seg_col, xs)
        own = exchange_lo({s: heads_by[j] for j, s in enumerate(slots)}, xs, -1)
        own = [own[s] for s in slots]
        middle, normed_two = out_project(
            me, own, w["out"], sm["out"], stream, sm["gains"][1], sm["shifts"][1], xs
        )
        by = gather_lo(normed_two, xs)
        all_two = [by[s] for s in slots]
        near, far = all_two[:CORES], all_two[CORES:]
        hid_a, gel_a, part_a = ffn_fwd(near, w["up"], sm["up"], w["down"], [F32] + [BF] * (CORES - 1))
        hid_b, gel_b, part_b = ffn_fwd(far, w["up"], sm["up"], w["down"], [BF] * len(far))
        part = dict(zip(slots, part_a + part_b))
        terms = scatter_lo(part, xs)
        stored.append((stream, all_one, qkv, out_t, lse, own, middle, all_two, hid_a + hid_b, gel_a + gel_b))
        if l + 1 < layers:
            stream, normed = layer_end(
                terms, middle, sm["down"], (small[l + 1]["gains"][0], small[l + 1]["shifts"][0])
            )
        else:
            (final,) = layer_end(terms, middle, sm["down"], None)
    result = turned(final)

    dh, dz = grad_own, grad_own
    down_sum = jnp.sum(grad_own.astype(F32), axis=0, keepdims=True)
    mine_sums, shared_sums = [None] * layers, [None] * layers
    q_grads, u_grads, d_grads, o_grads = [[None] * layers for _ in range(4)]

    def reduce_cols(by_hi):
        terms = scatter_hb(by_hi, hs, ts)
        blocks = {}
        for k, dc in slots:
            total = terms[0][dc, k]
            for t in terms[1:]:
                total = total + t[dc, k].astype(F32)
            blocks[k, dc] = total.astype(BF)
        return exchange_lo(blocks, xs, 1)

    def reduce_rows(by_hi):
        terms = scatter_hb(by_hi, hs, ts)
        total = terms[0]
        for t in terms[1:]:
            total = total + t.astype(F32)
        return total

    def reduce_out(g):
        got = shift(g[1], CORE, CORES, 1)
        both = [g[0, k].astype(F32) + got[k].astype(F32) for k in range(xs)]
        total = both[0]
        for k in range(1, xs):
            total = total + shift(both[k].astype(BF), XX, xs, k).astype(F32)
        by_hi = [total[0]] + [total[kh].astype(BF) for kh in range(1, hs)]
        return reduce_rows(by_hi)

    for l in reversed(range(layers)):
        w, sm = weights[l], small[l]
        stream, all_one, qkv, out_t, lse, own, middle, all_two, hidden, gel = stored[l]
        by = gather_lo(dz, xs)
        all_dz = [by[s] for s in slots]
        du_a, part_a = ffn_bwd(all_dz[:CORES], gel[:CORES], w["up"], w["down"], [F32] + [BF] * (CORES - 1))
        du_b, part_b = ffn_bwd(all_dz[CORES:], gel[CORES:], w["up"], w["down"], [BF] * (ts - CORES))
        all_du = du_a + du_b
        terms = scatter_lo(dict(zip(slots, part_a + part_b)), xs)
        d_grads[l] = reduce_rows(wgrad_rows(me, hidden, all_dz, hs))
        up_sum, up_parts = wgrad_cols(me, all_two, all_du, hs, xs)
        u_grads[l] = reduce_cols(up_parts)
        dh1, dy, mid_sums, d_heads = mid_back(me, terms, dh, middle, sm["gains"][1], w["out"], ts, xs)
        by = exchange_lo(dict(zip(slots, d_heads)), xs, 1)
        d_out = [by[s] for s in slots]
        o_grads[l] = reduce_out(wgrad_out(me, own, dy, hs, xs))
        dqkv, parts = attn_bwd(me, slopes, d_out, qkv, out_t, lse, w["qkv"], seg_row, seg_col, xs)
        terms = scatter_lo(dict(zip(slots, parts)), xs)
        qkv_sum, qkv_parts = wgrad_cols(me, all_one, dqkv, hs, xs)
        q_grads[l] = reduce_cols(qkv_parts)
        dh, dz, start_sums = start_back(terms, dh1, stream, sm["gains"][0])
        mine_sums[l] = jnp.concatenate([down_sum, mid_sums, start_sums[:2]], 0)
        width = qkv_sum.shape[1] // 3
        shared_sums[l] = (up_sum, qkv_sum[:, :width], qkv_sum[:, 2 * width :])
        down_sum = start_sums[2:3]
    input_grad = turned(dz)

    wide = max(D, shared_sums[0][0].shape[1])
    rows = []
    for l in range(layers):
        up_sum, q_sum, v_sum = shared_sums[l]
        rows.append(jnp.pad(up_sum, ((0, 0), (0, wide - up_sum.shape[1]))))
        qv = jnp.concatenate([q_sum, v_sum], 1)
        rows.append(jnp.pad(qv, ((0, 0), (0, wide - qv.shape[1]))))
    sums = sum_small(jnp.concatenate(mine_sums, 0), jnp.concatenate(rows, 0), hs, ts, xs)
    device = (hi * ts + lo) * ts + blk
    each = out_bias.shape[1]
    vectors = lax.dynamic_slice(sums[: 6 * layers, :D], (0, device * each), (6 * layers, each))
    vectors = vectors.reshape(layers, 6, each)
    shared = sums[6 * layers :].reshape(layers, 2, wide)
    up_each, qv_each = up_bias.shape[1], qv_bias.shape[1]
    up_grad = lax.dynamic_slice(shared[:, 0], (0, (hi * ts + blk) * up_each), (layers, up_each))
    qv_grad = lax.dynamic_slice(shared[:, 1], (0, (hi * ts + blk) * qv_each), (layers, qv_each))
    q_grad, u_grad = join(me, list(zip(q_grads, u_grads)), ts, xs)
    return (
        result[None],
        input_grad[None],
        q_grad,
        qv_grad,
        jnp.stack(o_grads),
        vectors[:, 3],
        u_grad,
        up_grad,
        jnp.stack(d_grads),
        vectors[:, 0],
        jnp.stack([vectors[:, 4], vectors[:, 1]], 1),
        jnp.stack([vectors[:, 5], vectors[:, 2]], 1),
    )


def solution(mesh):
    ts = mesh.shape["blk"]
    hs = mesh.shape["rows"] // ts
    xs = ts // CORES
    fine = Mesh(mesh.devices.reshape(hs, xs, CORES, ts), (HI, XX, CORE, BLK))
    rows, every = (HI, XX, CORE), (HI, XX, CORE, BLK)
    row_cut = P(None, every, None)
    vec_cut = P(None, every)
    norm_cut = P(None, None, every)
    cuts = (row_cut, vec_cut, row_cut, vec_cut, row_cut, vec_cut, row_cut, vec_cut, norm_cut, norm_cut)
    acts = P(rows, BLK, None)
    return jax.shard_map(
        functools.partial(on_device, hs, ts, xs),
        mesh=fine,
        in_specs=(acts, P(rows, BLK), acts) + cuts,
        out_specs=(acts, acts) + cuts,
        check_vma=False,
    )
```

time: 3970 us -> 722 us (0.18)
  waiting for transfers between devices: 3090 us -> 248 us
  blocking collectives: 468 us -> 0 us
  starting transfers between devices: 2.19 us -> 234 us
  matrix products: 210 us -> 0.13 us
  Pallas kernels: 0 us -> 127 us
    reduce_scatter x12 -> x0, waiting for transfers between devices: 2230 us -> none  [the longest x2 728 us: on_device(): lax.psum_scatter(grad_w_down, ('rows', 'blk'), scatter_dimension=0, tiled...]
    unnamed x34 -> x0, waiting for transfers between devices: 566 us -> none
    all_gather x7 -> x0, blocking collectives: 425 us -> none  [the longest x2 145 us: fetch_forward(): lax.all_gather(norm_gain[layer_index], ('rows', 'blk'), axis=1, tiled=True)]
    all_gather x12 -> x0, waiting for transfers between devices: 289 us -> none  [the longest x2 103 us: fetch_forward(): lax.all_gather(down_weight[layer_index], ('rows', 'blk'), axis=0, tiled=T...]
    ppermute x0 -> x202, waiting for transfers between devices: none -> 248 us  [the longest x197 248 us: shift(): return lax.ppermute(x, axis, [(i, (i + step) % size) for i in range(size)])]
    ppermute x0 -> x202, starting transfers between devices: none -> 234 us  [the longest x197 224 us: shift(): return lax.ppermute(x, axis, [(i, (i + step) % size) for i in range(size)])]
    dot_general x52 -> x1, matrix products: 210 us -> 0.13 us  [gather_params(): return jnp.dot(pick, stack, preferred_element_type=F32)]
    pallas_call x0 -> x39, Pallas kernels: none -> 127 us  [run(): pl.pallas_call(kernel, out_shape=tuple(outs), in_specs=[pl.BlockSpec(memo...]
  transfers between devices with their start and end apart: 29 -> 202, of which waited for: 23 -> 68; matrix products, arithmetic and copies ran while one was open for 6% -> 9% of each run, Pallas kernels for 0% -> 18%
where the time goes in v1:
time: 722 us; the launch traced here: 715 us
  waiting for transfers between devices  248 us (34%)
  starting transfers between devices  234 us (32%)
  Pallas kernels  127 us (18%)
  local copies, waits for them, and re-layouts  65.4 us (9%)
  other arithmetic  37.7 us (5%)
    ppermute x197, waiting for transfers between devices, shift(): return lax.ppermute(x, axis, [(i, (i + step) % size) for i in range(size)])  248 us
    ppermute x197, starting transfers between devices, shift(): return lax.ppermute(x, axis, [(i, (i + step) % size) for i in range(size)])  224 us
    pallas_call x39, Pallas kernels, run(): pl.pallas_call(kernel, out_shape=tuple(outs), in_specs=[pl.BlockSpec(memo...  127 us
    unnamed x355, local copies, waits for them, and re-layouts  43.6 us
  transfers between devices with their start and end apart: 202, of which 68 were waited for; matrix products, arithmetic and copies ran while one was open for 9% of the time, Pallas kernels for 18%

profile of v1, /device:TPU:0, one launch (start us, length us, event | category | flops | bytes accessed | tf_op | source)
XLA Modules:
  0.0 715.2 jit_solution(17958653513574032362)
XLA Ops:
  21.0 4.7 collective-permute-start.5
  98.1 4.6 collective-permute-done.14
  103.2 3.9 collective-permute-done.15
  113.8 4.0 collective-permute-done.44
  119.9 5.4 collective-permute-done.19
  125.3 6.8 collective-permute-done.8.refs_2_
  136.0 7.8 %shard_map.223 = (bf16[1024,768]{1,0:T(8,128)(2,1)S(1)}, f32[256,1024]{1,0:T(8,128)S(1)}, f32[2,1024]{1,0:T(2,128)S(1)}, bf16[256,256]{1,0:T(8,128)(2,1)S(1)}, b...) custom-call(s32[4]{0:T(128)S(1)} %pad_add_fusion.me, ...), custom_call_target="tpu_custom_call" | custom-call | flops 2415919104 | bytes 6835200 | tf_op jit(solution)/shard_map/pallas_call | solution.py:43
  154.7 14.1 %collective-permute-start.46 = (bf16[4,32,1024]{2,1,0:T(8,128)(2,1)S(1)}, bf16[4,32,1024]{2,1,0:T(8,128)(2,1)S(1)}, u32[]{:S(2)}, u32[]{:S(2)}) collective-permute-start(bf16[4,32,1024]{2,1,0:T(8,128)(2,1)S(1)} %pad_maximum_fusion.1), channel_id=1, source_target_pairs={{0,3},{1,0},{2,1},{3,2},{4,7},{5,4},{6,5},{7,6},{8,11},{9,8},{10,9... | collective-permute-start | bytes 786440 | tf_op jit(solution)/shard_map/ppermute | solution.py:68
  178.6 5.0 collective-permute-done.55.refs_5_
  184.2 5.0 collective-permute-done.56.refs_6_
  189.2 5.6 collective-permute-done.57.refs_7_
  201.1 5.0 collective-permute-done.49
  213.1 6.0 shard_map.229
  229.2 5.8 shard_map.228
  245.1 5.5 collective-permute-done.61.refs_1_
  260.8 11.5 %collective-permute-done.64.refs_2_ = bf16[256,1024]{1,0:T(8,128)(2,1)S(1)} collective-permute-done((bf16[256,1024]{1,0:T(8,128)(2,1)S(1)}, bf16[256,1024]{1,0:T(8,128)(2,1)S(1)}, u32[]{:S(2)}, u32[]{:S(2)}) %collective-permute-start.64) | collective-permute-done | bytes 524320 | tf_op jit(solution)/shard_map/ppermute | solution.py:68
  278.8 7.8 %shard_map.232 = (bf16[1024,768]{1,0:T(8,128)(2,1)S(1)}, f32[256,1024]{1,0:T(8,128)S(1)}, f32[2,1024]{1,0:T(2,128)S(1)}, bf16[256,256]{1,0:T(8,128)(2,1)S(1)}, b...) custom-call(s32[4]{0:T(128)S(1)} %pad_add_fusion.me, f32[2]{0:T(128)S(1)} %copy-done.106, ...), custom_call_target="tpu_custom_call" | custom-call | flops 2415919104 | bytes 6835200 | tf_op jit(solution)/shard_map/pallas_call | solution.py:43
  290.6 5.1 collective-permute-start.77
  303.0 5.3 collective-permute-done.78.refs_2_
  314.5 13.9 %collective-permute-done.97 = bf16[4,32,1024]{2,1,0:T(8,128)(2,1)S(1)} collective-permute-done((bf16[4,32,1024]{2,1,0:T(8,128)(2,1)S(1)}, bf16[4,32,1024]{2,1,0:T(8,128)(2,1)S(1)}, u32[]{:S(2)}, u32[]{:S(2)}) %collective-permute-start.97) | collective-permute-done | bytes 262176 | tf_op jit(solution)/shard_map/ppermute | solution.py:68
  336.2 4.5 collective-permute-done.109.refs_7_
  346.4 5.1 collective-permute-start.117
  362.0 6.0 shard_map.238
  369.6 4.6 shard_map.241
  376.0 6.0 shard_map.237
  382.8 6.2 shard_map.240
  401.5 3.7 shard_map.258
  406.0 3.7 shard_map.242
  410.4 3.7 shard_map.253
  423.4 9.9 %shard_map.243 = (bf16[256,768]{1,0:T(8,128)(2,1)S(1)}, bf16[256,768]{1,0:T(8,128)(2,1)S(1)}, bf16[256,768]{1,0:T(8,128)(2,1)S(1)}, bf16[256,768]{1,0:T(8,128)(2...) custom-call(s32[4]{0:T(128)S(1)} %pad_add_fusion.me, ...), custom_call_target="tpu_custom_call" | custom-call | flops 3221225472 | bytes 8929280 | tf_op jit(solution)/shard_map/pallas_call | solution.py:43
  436.0 7.7 %collective-permute-start.201 = (bf16[128,1024]{1,0:T(8,128)(2,1)}, bf16[128,1024]{1,0:T(8,128)(2,1)S(1)}, u32[]{:S(2)}, u32[]{:S(2)}) collective-permute-start(bf16[128,1024]{1,0:T(8,128)(2,1)} %get-tuple-element.278), channel_id=1, source_target_pairs={{0,3},{1,0},{2,1},{3,2},{4,7},{5,4},{6,5},{7,6},{8,11},{9,8},{10,9... | collective-permute-start | bytes 786440 | tf_op jit(solution)/shard_map/ppermute | solution.py:68
  446.3 6.8 collective-permute-done.164
  453.1 5.7 collective-permute-start.199
  461.5 3.7 collective-permute-start.167
  468.3 6.5 collective-permute-start.166
  483.4 21.0 %collective-permute-done.166 = bf16[2,2,32,1024]{3,2,1,0:T(8,128)(2,1)S(1)} collective-permute-done((bf16[2,2,32,1024]{3,2,1,0:T(8,128)(2,1)}, bf16[2,2,32,1024]{3,2,1,0:T(8,128)(2,1)S(1)}, u32[]{:S(2)}, u32[]{:S(2)}) %collective-permute-start.166) | collective-permute-done | bytes 262176 | tf_op jit(solution)/shard_map/ppermute | solution.py:68
  510.1 11.6 %collective-permute-done.160 = bf16[4,2,2,32,768]{4,3,2,1,0:T(8,128)(2,1)S(1)} collective-permute-done((bf16[4,2,2,32,768]{4,3,2,1,0:T(8,128)(2,1)S(1)}, bf16[4,2,2,32,768]{4,3,2,1,0:T(8,128)(2,1)S(1)}, u32[]{:S(2)}, u32[]{:S(2)}) %collective-permute-start.160) | collective-permute-done | bytes 786464 | tf_op jit(solution)/shard_map/ppermute | solution.py:68
  523.0 4.6 shard_map.246
  532.8 4.8 shard_map.245
  538.1 3.7 shard_map.257
  548.2 3.7 shard_map.251
  572.9 9.4 %shard_map.248 = (bf16[256,768]{1,0:T(8,128)(2,1)S(1)}, bf16[256,768]{1,0:T(8,128)(2,1)S(1)}, bf16[256,768]{1,0:T(8,128)(2,1)S(1)}, bf16[256,768]{1,0:T(8,128)(2...) custom-call(s32[4]{0:T(128)S(1)} %pad_add_fusion.me, ...), custom_call_target="tpu_custom_call" | custom-call | flops 3221225472 | bytes 8929280 | tf_op jit(solution)/shard_map/pallas_call | solution.py:43
  600.4 8.6 %collective-permute-done.196 = bf16[128,1024]{1,0:T(8,128)(2,1)S(1)} collective-permute-done((bf16[128,1024]{1,0:T(8,128)(2,1)S(1)}, bf16[128,1024]{1,0:T(8,128)(2,1)S(1)}, u32[]{:S(2)}, u32[]{:S(2)}) %collective-permute-start.196) | collective-permute-done | bytes 262176 | tf_op jit(solution)/shard_map/ppermute | solution.py:68
  618.5 13.4 %collective-permute-done.150 = bf16[2,2,32,1024]{3,2,1,0:T(8,128)(2,1)} collective-permute-done((bf16[2,2,32,1024]{3,2,1,0:T(8,128)(2,1)}, bf16[2,2,32,1024]{3,2,1,0:T(8,128)(2,1)}, u32[]{:S(2)}, u32[]{:S(2)}) %collective-permute-start.150) | collective-permute-done | bytes 262176 | tf_op jit(solution)/shard_map/ppermute | solution.py:68
  651.7 9.1 %collective-permute-done.146 = bf16[2,2,32,768]{3,2,1,0:T(8,128)(2,1)S(1)} collective-permute-done((bf16[2,2,32,768]{3,2,1,0:T(8,128)(2,1)}, bf16[2,2,32,768]{3,2,1,0:T(8,128)(2,1)S(1)}, u32[]{:S(2)}, u32[]{:S(2)}) %collective-permute-start.146) | collective-permute-done | bytes 196640 | tf_op jit(solution)/shard_map/ppermute | solution.py:68
  675.6 5.3 collective-permute-start.143
  683.6 8.4 %collective-permute-done.183 = bf16[2,4,32,1024]{3,2,1,0:T(8,128)(2,1)} collective-permute-done((bf16[2,4,32,1024]{3,2,1,0:T(8,128)(2,1)}, bf16[2,4,32,1024]{3,2,1,0:T(8,128)(2,1)}, u32[]{:S(2)}, u32[]{:S(2)}) %collective-permute-start.183) | collective-permute-done | bytes 524320 | tf_op jit(solution)/shard_map/ppermute | solution.py:68
  700.0 5.2 collective-permute-start.187
  (910 shorter events, 386.0 us)
Async XLA Ops:
  13.2 33.0 %collective-permute-start.29 = (bf16[32,1024]{1,0:T(8,128)(2,1)S(1)}, bf16[32,1024]{1,0:T(8,128)(2,1)S(1)}, u32[]{:S(2)}, u32[]{:S(2)}) collective-permute-start(bf16[32,1024]{1,0:T(8,128)(2,1)S(1)} %get-tuple-element.483.refs_0_), channel_id=1, source_target_pairs={{0,1},{1,2},{2,3},{3,0},{4,5},{5,6},{6,7},{7,4},{8,9},{9,10},{10,1... | collective-permute-start | bytes 196616 | tf_op jit(solution)/shard_map/ppermute | solution.py:68
  13.9 34.9 %collective-permute-start.30 = (bf16[32,1024]{1,0:T(8,128)(2,1)S(1)}, bf16[32,1024]{1,0:T(8,128)(2,1)S(1)}, u32[]{:S(2)}, u32[]{:S(2)}) collective-permute-start(bf16[32,1024]{1,0:T(8,128)(2,1)S(1)} %get-tuple-element.483.refs_0_), channel_id=1, source_target_pairs={{0,2},{1,3},{2,0},{3,1},{4,6},{5,7},{6,4},{7,5},{8,10},{9,11},{10,... | collective-permute-start | bytes 196616 | tf_op jit(solution)/shard_map/ppermute | solution.py:68
  52.5 59.2 %collective-permute-start = (bf16[256,1024]{1,0:T(8,128)(2,1)}, bf16[256,1024]{1,0:T(8,128)(2,1)S(1)}, u32[]{:S(2)}, u32[]{:S(2)}) collective-permute-start(bf16[256,1024]{1,0:T(8,128)(2,1)} %bitcast.739), channel_id=1, source_target_pairs={{0,0},{1,4},{2,8},{3,12},{4,1},{5,5},{6,9},{7,13},{8,2},{9,6},{10,... | collective-permute-start | bytes 1572872 | tf_op jit(solution)/shard_map/ppermute | solution.py:694
  61.2 30.3 %collective-permute-start.40 = (bf16[32,1024]{1,0:T(8,128)(2,1)S(1)}, bf16[32,1024]{1,0:T(8,128)(2,1)S(1)}, u32[]{:S(2)}, u32[]{:S(2)}) collective-permute-start(bf16[32,1024]{1,0:T(8,128)(2,1)S(1)} %get-tuple-element.155), channel_id=1, source_target_pairs={{0,4},{4,0},{1,5},{5,1},{2,6},{6,2},{3,7},{7,3},{8,12},{12,8},{9,1... | collective-permute-start | bytes 196616 | tf_op jit(solution)/shard_map/ppermute | solution.py:68
  65.6 27.4 %collective-permute-start.41 = (bf16[32,1024]{1,0:T(8,128)(2,1)S(1)}, bf16[32,1024]{1,0:T(8,128)(2,1)S(1)}, u32[]{:S(2)}, u32[]{:S(2)}) collective-permute-start(bf16[32,1024]{1,0:T(8,128)(2,1)S(1)} %get-tuple-element.156), channel_id=1, source_target_pairs={{0,8},{8,0},{1,9},{9,1},{2,10},{10,2},{3,11},{11,3},{4,12},{12,4},... | collective-permute-start | bytes 196616 | tf_op jit(solution)/shard_map/ppermute | solution.py:68
  86.1 59.7 %collective-permute-start.51 = (bf16[128,1024]{1,0:T(8,128)(2,1)S(1)}, bf16[128,1024]{1,0:T(8,128)(2,1)S(1)}, u32[]{:S(2)}, u32[]{:S(2)}) collective-permute-start(bf16[128,1024]{1,0:T(8,128)(2,1)S(1)} %get-tuple-element.319.refs_0_), channel_id=1, source_target_pairs={{0,1},{1,2},{2,3},{3,0},{4,5},{5,6},{6,7},{7,4},{8,9},{9,10},{10,1... | collective-permute-start | bytes 786440 | tf_op jit(solution)/shard_map/ppermute | solution.py:68
  107.1 27.5 %collective-permute-start.37 = (bf16[8,32,1024]{2,1,0:T(8,128)(2,1)}, bf16[8,32,1024]{2,1,0:T(8,128)(2,1)S(1)}, u32[]{:S(2)}, u32[]{:S(2)}) collective-permute-start(bf16[8,32,1024]{2,1,0:T(8,128)(2,1)} %bitcast_dynamic-update-slice_fusion.7), channel_id=1, source_target_pairs={{0,8},{8,0},{1,9},{9,1},{2,10},{10,2},{3,11},{11,3},{4,12},{12,4},... | collective-permute-start | bytes 1572872 | tf_op jit(solution)/shard_map/ppermute | solution.py:68
  134.8 36.1 %collective-permute-start.53 = (bf16[128,1024]{1,0:T(8,128)(2,1)S(1)}, bf16[128,1024]{1,0:T(8,128)(2,1)S(1)}, u32[]{:S(2)}, u32[]{:S(2)}) collective-permute-start(bf16[128,1024]{1,0:T(8,128)(2,1)S(1)} %get-tuple-element.319.refs_0_), channel_id=1, source_target_pairs={{0,3},{1,0},{2,1},{3,2},{4,7},{5,4},{6,5},{7,6},{8,11},{9,8},{10,9... | collective-permute-start | bytes 786440 | tf_op jit(solution)/shard_map/ppermute | solution.py:68
  145.8 26.6 %collective-permute-start.45 = (bf16[4,32,1024]{2,1,0:T(8,128)(2,1)S(1)}, bf16[4,32,1024]{2,1,0:T(8,128)(2,1)S(1)}, u32[]{:S(2)}, u32[]{:S(2)}) collective-permute-start(bf16[4,32,1024]{2,1,0:T(8,128)(2,1)S(1)} %pad_maximum_fusion.1), channel_id=1, source_target_pairs={{0,2},{1,3},{2,0},{3,1},{4,6},{5,7},{6,4},{7,5},{8,10},{9,11},{10,... | collective-permute-start | bytes 786440 | tf_op jit(solution)/shard_map/ppermute | solution.py:68
  151.2 22.4 %collective-permute-start.54 = (bf16[128,1024]{1,0:T(8,128)(2,1)S(1)}, bf16[128,1024]{1,0:T(8,128)(2,1)S(1)}, u32[]{:S(2)}, u32[]{:S(2)}) collective-permute-start(bf16[128,1024]{1,0:T(8,128)(2,1)S(1)} %get-tuple-element.319.refs_0_), channel_id=1, source_target_pairs={{0,16},{16,0},{1,17},{17,1},{2,18},{18,2},{3,19},{19,3},{4,20},{20... | collective-permute-start | bytes 786440 | tf_op jit(solution)/shard_map/ppermute | solution.py:68
  172.4 28.6 %collective-permute-start.58 = (bf16[256,1024]{1,0:T(8,128)(2,1)S(1)}, bf16[256,1024]{1,0:T(8,128)(2,1)S(1)}, u32[]{:S(2)}, u32[]{:S(2)}) collective-permute-start(bf16[256,1024]{1,0:T(8,128)(2,1)S(1)} %get-tuple-element.153.refs_0_), channel_id=1, source_target_pairs={{0,8},{8,0},{1,9},{9,1},{2,10},{10,2},{3,11},{11,3},{4,12},{12,4},... | collective-permute-start | bytes 1572872 | tf_op jit(solution)/shard_map/ppermute | solution.py:68
  173.8 21.0 %collective-permute-start.57 = (bf16[128,1024]{1,0:T(8,128)(2,1)S(1)}, bf16[128,1024]{1,0:T(8,128)(2,1)S(1)}, u32[]{:S(2)}, u32[]{:S(2)}) collective-permute-start(bf16[128,1024]{1,0:T(8,128)(2,1)S(1)} %collective-permute-done.53.refs_3_), channel_id=1, source_target_pairs={{0,16},{16,0},{1,17},{17,1},{2,18},{18,2},{3,19},{19,3},{4,20},{20... | collective-permute-start | bytes 786440 | tf_op jit(solution)/shard_map/ppermute | solution.py:68
  178.0 22.5 %collective-permute-start.48 = (bf16[4,32,1024]{2,1,0:T(8,128)(2,1)S(1)}, bf16[4,32,1024]{2,1,0:T(8,128)(2,1)S(1)}, u32[]{:S(2)}, u32[]{:S(2)}) collective-permute-start(bf16[4,32,1024]{2,1,0:T(8,128)(2,1)S(1)} %collective-permute-done.44), channel_id=1, source_target_pairs={{0,16},{16,0},{1,17},{17,1},{2,18},{18,2},{3,19},{19,3},{4,20},{20... | collective-permute-start | bytes 786440 | tf_op jit(solution)/shard_map/ppermute | solution.py:68
  183.6 22.5 %collective-permute-start.49 = (bf16[4,32,1024]{2,1,0:T(8,128)(2,1)S(1)}, bf16[4,32,1024]{2,1,0:T(8,128)(2,1)S(1)}, u32[]{:S(2)}, u32[]{:S(2)}) collective-permute-start(bf16[4,32,1024]{2,1,0:T(8,128)(2,1)S(1)} %collective-permute-done.45), channel_id=1, source_target_pairs={{0,16},{16,0},{1,17},{17,1},{2,18},{18,2},{3,19},{19,3},{4,20},{20... | collective-permute-start | bytes 786440 | tf_op jit(solution)/shard_map/ppermute | solution.py:68
  189.2 32.3 %collective-permute-start.92 = (bf16[32,1024]{1,0:T(8,128)(2,1)S(1)}, bf16[32,1024]{1,0:T(8,128)(2,1)S(1)}, u32[]{:S(2)}, u32[]{:S(2)}) collective-permute-start(bf16[32,1024]{1,0:T(8,128)(2,1)S(1)} %copy-done.102), channel_id=1, source_target_pairs={{0,4},{4,0},{1,5},{5,1},{2,6},{6,2},{3,7},{7,3},{8,12},{12,8},{9,1... | collective-permute-start | bytes 196616 | tf_op jit(solution)/shard_map/ppermute | solution.py:68
  194.8 27.0 %collective-permute-start.93 = (bf16[32,1024]{1,0:T(8,128)(2,1)S(1)}, bf16[32,1024]{1,0:T(8,128)(2,1)S(1)}, u32[]{:S(2)}, u32[]{:S(2)}) collective-permute-start(bf16[32,1024]{1,0:T(8,128)(2,1)S(1)} %copy-done.100), channel_id=1, source_target_pairs={{0,8},{8,0},{1,9},{9,1},{2,10},{10,2},{3,11},{11,3},{4,12},{12,4},... | collective-permute-start | bytes 196616 | tf_op jit(solution)/shard_map/ppermute | solution.py:68
  207.3 67.5 %collective-permute-start.103 = (bf16[128,1024]{1,0:T(8,128)(2,1)S(1)}, bf16[128,1024]{1,0:T(8,128)(2,1)S(1)}, u32[]{:S(2)}, u32[]{:S(2)}) collective-permute-start(bf16[128,1024]{1,0:T(8,128)(2,1)S(1)} %get-tuple-element.318.refs_0_), channel_id=1, source_target_pairs={{0,1},{1,2},{2,3},{3,0},{4,5},{5,6},{6,7},{7,4},{8,9},{9,10},{10,1... | collective-permute-start | bytes 786440 | tf_op jit(solution)/shard_map/ppermute | solution.py:68
  243.8 33.0 %collective-permute-start.89 = (bf16[8,32,1024]{2,1,0:T(8,128)(2,1)S(1)}, bf16[8,32,1024]{2,1,0:T(8,128)(2,1)S(1)}, u32[]{:S(2)}, u32[]{:S(2)}) collective-permute-start(bf16[8,32,1024]{2,1,0:T(8,128)(2,1)S(1)} %bitcast_dynamic-update-slice_fusion), channel_id=1, source_target_pairs={{0,8},{8,0},{1,9},{9,1},{2,10},{10,2},{3,11},{11,3},{4,12},{12,4},... | collective-permute-start | bytes 1572872 | tf_op jit(solution)/shard_map/ppermute | solution.py:68
  272.3 23.4 %collective-permute-start.88 = (bf16[8,32,1024]{2,1,0:T(8,128)(2,1)S(1)}, bf16[8,32,1024]{2,1,0:T(8,128)(2,1)S(1)}, u32[]{:S(2)}, u32[]{:S(2)}) collective-permute-start(bf16[8,32,1024]{2,1,0:T(8,128)(2,1)S(1)} %bitcast_dynamic-update-slice_fusion), channel_id=1, source_target_pairs={{0,4},{4,0},{1,5},{5,1},{2,6},{6,2},{3,7},{7,3},{8,12},{12,8},{9,1... | collective-permute-start | bytes 1572872 | tf_op jit(solution)/shard_map/ppermute | solution.py:68
  289.8 41.5 %collective-permute-start.116 = (bf16[256,1024]{1,0:T(8,128)(2,1)S(1)}, bf16[256,1024]{1,0:T(8,128)(2,1)S(1)}, u32[]{:S(2)}, u32[]{:S(2)}) collective-permute-start(bf16[256,1024]{1,0:T(8,128)(2,1)S(1)} %bitcast.740), channel_id=1, source_target_pairs={{0,0},{1,4},{2,8},{3,12},{4,1},{5,5},{6,9},{7,13},{8,2},{9,6},{10,... | collective-permute-start | bytes 1572872 | tf_op jit(solution)/shard_map/ppermute | solution.py:694
  295.8 32.6 %collective-permute-start.97 = (bf16[4,32,1024]{2,1,0:T(8,128)(2,1)S(1)}, bf16[4,32,1024]{2,1,0:T(8,128)(2,1)S(1)}, u32[]{:S(2)}, u32[]{:S(2)}) collective-permute-start(bf16[4,32,1024]{2,1,0:T(8,128)(2,1)S(1)} %pad_maximum_fusion.2), channel_id=1, source_target_pairs={{0,2},{1,3},{2,0},{3,1},{4,6},{5,7},{6,4},{7,5},{8,10},{9,11},{10,... | collective-permute-start | bytes 786440 | tf_op jit(solution)/shard_map/ppermute | solution.py:68
  297.7 31.5 %collective-permute-start.98 = (bf16[4,32,1024]{2,1,0:T(8,128)(2,1)S(1)}, bf16[4,32,1024]{2,1,0:T(8,128)(2,1)S(1)}, u32[]{:S(2)}, u32[]{:S(2)}) collective-permute-start(bf16[4,32,1024]{2,1,0:T(8,128)(2,1)S(1)} %pad_maximum_fusion.2), channel_id=1, source_target_pairs={{0,3},{1,0},{2,1},{3,2},{4,7},{5,4},{6,5},{7,6},{8,11},{9,8},{10,9... | collective-permute-start | bytes 786440 | tf_op jit(solution)/shard_map/ppermute | solution.py:68
  329.2 22.3 %collective-permute-start.110 = (bf16[256,1024]{1,0:T(8,128)(2,1)S(1)}, bf16[256,1024]{1,0:T(8,128)(2,1)S(1)}, u32[]{:S(2)}, u32[]{:S(2)}) collective-permute-start(bf16[256,1024]{1,0:T(8,128)(2,1)S(1)} %get-tuple-element.173.refs_0_), channel_id=1, source_target_pairs={{0,8},{8,0},{1,9},{9,1},{2,10},{10,2},{3,11},{11,3},{4,12},{12,4},... | collective-permute-start | bytes 1572872 | tf_op jit(solution)/shard_map/ppermute | solution.py:68
  331.3 22.0 %collective-permute-start.118 = (bf16[256,1024]{1,0:T(8,128)(2,1)S(1)}, bf16[256,1024]{1,0:T(8,128)(2,1)S(1)}, u32[]{:S(2)}, u32[]{:S(2)}) collective-permute-start(bf16[256,1024]{1,0:T(8,128)(2,1)S(1)} %collective-permute-done.116.refs_0_.refs_3_.refs_4_), channel_id=1, source_target_pairs={{0,8},{8,0},{1,9},{9,1},{2,10},{10,2},{3,11},{11,3},{4,12},{12,4},... | collective-permute-start | bytes 1572872 | tf_op jit(solution)/shard_map/ppermute | solution.py:68
  346.4 36.4 %collective-permute-start.117 = (bf16[256,1024]{1,0:T(8,128)(2,1)S(1)}, bf16[256,1024]{1,0:T(8,128)(2,1)S(1)}, u32[]{:S(2)}, u32[]{:S(2)}) collective-permute-start(bf16[256,1024]{1,0:T(8,128)(2,1)S(1)} %collective-permute-done.116.refs_0_.refs_3_.refs_4_), channel_id=1, source_target_pairs={{0,4},{4,0},{1,5},{5,1},{2,6},{6,2},{3,7},{7,3},{8,12},{12,8},{9,1... | collective-permute-start | bytes 1572872 | tf_op jit(solution)/shard_map/ppermute | solution.py:68
  393.0 21.6 %collective-permute-start.112 = (bf16[256,1024]{1,0:T(8,128)(2,1)}, bf16[256,1024]{1,0:T(8,128)(2,1)}, u32[]{:S(2)}, u32[]{:S(2)}) collective-permute-start(bf16[256,1024]{1,0:T(8,128)(2,1)} %copy-done.96), channel_id=1, source_target_pairs={{0,4},{4,0},{1,5},{5,1},{2,6},{6,2},{3,7},{7,3},{8,12},{12,8},{9,1... | collective-permute-start | bytes 1572872 | tf_op jit(solution)/shard_map/ppermute | solution.py:68
  393.8 42.2 %collective-permute-start.114 = (bf16[256,1024]{1,0:T(8,128)(2,1)}, bf16[256,1024]{1,0:T(8,128)(2,1)}, u32[]{:S(2)}, u32[]{:S(2)}) collective-permute-start(bf16[256,1024]{1,0:T(8,128)(2,1)} %copy-done.91), channel_id=1, source_target_pairs={{0,4},{4,0},{1,5},{5,1},{2,6},{6,2},{3,7},{7,3},{8,12},{12,8},{9,1... | collective-permute-start | bytes 1572872 | tf_op jit(solution)/shard_map/ppermute | solution.py:68
  405.2 29.3 %collective-permute-start.198 = (bf16[4,128,1024]{2,1,0:T(8,128)(2,1)}, bf16[4,128,1024]{2,1,0:T(8,128)(2,1)S(1)}, u32[]{:S(2)}, u32[]{:S(2)}) collective-permute-start(bf16[4,128,1024]{2,1,0:T(8,128)(2,1)} %get-tuple-element.273), channel_id=1, source_target_pairs={{0,16},{16,0},{1,17},{17,1},{2,18},{18,2},{3,19},{19,3},{4,20},{20... | collective-permute-start | bytes 3145736 | tf_op jit(solution)/shard_map/ppermute | solution.py:68
  419.4 33.7 %collective-permute-start.164 = (bf16[4,2,2,32,1024]{4,3,2,1,0:T(8,128)(2,1)}, bf16[4,2,2,32,1024]{4,3,2,1,0:T(8,128)(2,1)}, u32[]{:S(2)}, u32[]{:S(2)}) collective-permute-start(bf16[4,2,2,32,1024]{4,3,2,1,0:T(8,128)(2,1)} %get-tuple-element.249), channel_id=1, source_target_pairs={{0,16},{16,0},{1,17},{17,1},{2,18},{18,2},{3,19},{19,3},{4,20},{20... | collective-permute-start | bytes 3145736 | tf_op jit(solution)/shard_map/ppermute | solution.py:68
  420.9 22.7 %collective-permute-start.113 = (bf16[256,1024]{1,0:T(8,128)(2,1)S(1)}, bf16[256,1024]{1,0:T(8,128)(2,1)S(1)}, u32[]{:S(2)}, u32[]{:S(2)}) collective-permute-start(bf16[256,1024]{1,0:T(8,128)(2,1)S(1)} %add_convert_fusion.4), channel_id=1, source_target_pairs={{0,8},{8,0},{1,9},{9,1},{2,10},{10,2},{3,11},{11,3},{4,12},{12,4},... | collective-permute-start | bytes 1572872 | tf_op jit(solution)/shard_map/ppermute | solution.py:68
  434.5 73.6 %collective-permute-start.188 = (bf16[2,2,4,32,1024]{4,3,2,1,0:T(8,128)(2,1)}, bf16[2,2,4,32,1024]{4,3,2,1,0:T(8,128)(2,1)}, u32[]{:S(2)}, u32[]{:S(2)}) collective-permute-start(bf16[2,2,4,32,1024]{4,3,2,1,0:T(8,128)(2,1)} %slice_bitcast_fusion), channel_id=1, source_target_pairs={{0,4},{4,0},{1,5},{5,1},{2,6},{6,2},{3,7},{7,3},{8,12},{12,8},{9,1... | collective-permute-start | bytes 3145736 | tf_op jit(solution)/shard_map/ppermute | solution.py:68
  436.0 22.8 %collective-permute-start.201 = (bf16[128,1024]{1,0:T(8,128)(2,1)}, bf16[128,1024]{1,0:T(8,128)(2,1)S(1)}, u32[]{:S(2)}, u32[]{:S(2)}) collective-permute-start(bf16[128,1024]{1,0:T(8,128)(2,1)} %get-tuple-element.278), channel_id=1, source_target_pairs={{0,3},{1,0},{2,1},{3,2},{4,7},{5,4},{6,5},{7,6},{8,11},{9,8},{10,9... | collective-permute-start | bytes 786440 | tf_op jit(solution)/shard_map/ppermute | solution.py:68
  445.0 29.8 %collective-permute-start.129 = (bf16[256,1024]{1,0:T(8,128)(2,1)S(1)}, bf16[256,1024]{1,0:T(8,128)(2,1)S(1)}, u32[]{:S(2)}, u32[]{:S(2)}) collective-permute-start(bf16[256,1024]{1,0:T(8,128)(2,1)S(1)} %get-tuple-element.201), channel_id=1, source_target_pairs={{0,4},{4,0},{1,5},{5,1},{2,6},{6,2},{3,7},{7,3},{8,12},{12,8},{9,1... | collective-permute-start | bytes 1572872 | tf_op jit(solution)/shard_map/ppermute | solution.py:68
  461.5 21.2 %collective-permute-start.167 = (bf16[2,2,32,1024]{3,2,1,0:T(8,128)(2,1)}, bf16[2,2,32,1024]{3,2,1,0:T(8,128)(2,1)S(1)}, u32[]{:S(2)}, u32[]{:S(2)}) collective-permute-start(bf16[2,2,32,1024]{3,2,1,0:T(8,128)(2,1)} %get-tuple-element.281), channel_id=1, source_target_pairs={{0,3},{1,0},{2,1},{3,2},{4,7},{5,4},{6,5},{7,6},{8,11},{9,8},{10,9... | collective-permute-start | bytes 786440 | tf_op jit(solution)/shard_map/ppermute | solution.py:68
  468.3 36.1 %collective-permute-start.166 = (bf16[2,2,32,1024]{3,2,1,0:T(8,128)(2,1)}, bf16[2,2,32,1024]{3,2,1,0:T(8,128)(2,1)S(1)}, u32[]{:S(2)}, u32[]{:S(2)}) collective-permute-start(bf16[2,2,32,1024]{3,2,1,0:T(8,128)(2,1)} %get-tuple-element.282), channel_id=1, source_target_pairs={{0,2},{1,3},{2,0},{3,1},{4,6},{5,7},{6,4},{7,5},{8,10},{9,11},{10,... | collective-permute-start | bytes 786440 | tf_op jit(solution)/shard_map/ppermute | solution.py:68
  474.8 32.4 %collective-permute-start.165 = (bf16[2,2,32,1024]{3,2,1,0:T(8,128)(2,1)}, bf16[2,2,32,1024]{3,2,1,0:T(8,128)(2,1)S(1)}, u32[]{:S(2)}, u32[]{:S(2)}) collective-permute-start(bf16[2,2,32,1024]{3,2,1,0:T(8,128)(2,1)} %get-tuple-element.280), channel_id=1, source_target_pairs={{0,1},{1,2},{2,3},{3,0},{4,5},{5,6},{6,7},{7,4},{8,9},{9,10},{10,1... | collective-permute-start | bytes 786440 | tf_op jit(solution)/shard_map/ppermute | solution.py:68
  479.3 28.8 %collective-permute-start.131 = (bf16[256,1024]{1,0:T(8,128)(2,1)S(1)}, bf16[256,1024]{1,0:T(8,128)(2,1)S(1)}, u32[]{:S(2)}, u32[]{:S(2)}) collective-permute-start(bf16[256,1024]{1,0:T(8,128)(2,1)S(1)} %get-tuple-element.203.refs_0_.refs_4_), channel_id=1, source_target_pairs={{0,8},{8,0},{1,9},{9,1},{2,10},{10,2},{3,11},{11,3},{4,12},{12,4},... | collective-permute-start | bytes 1572872 | tf_op jit(solution)/shard_map/ppermute | solution.py:68
  482.7 27.4 %collective-permute-start.115 = (bf16[256,1024]{1,0:T(8,128)(2,1)S(1)}, bf16[256,1024]{1,0:T(8,128)(2,1)S(1)}, u32[]{:S(2)}, u32[]{:S(2)}) collective-permute-start(bf16[256,1024]{1,0:T(8,128)(2,1)S(1)} %shard_map.239), channel_id=1, source_target_pairs={{0,0},{1,4},{2,8},{3,12},{4,1},{5,5},{6,9},{7,13},{8,2},{9,6},{10,... | collective-permute-start | bytes 1572872 | tf_op jit(solution)/shard_map/ppermute | solution.py:694
  522.7 21.1 %collective-permute-start.163 = (bf16[2,2,32,768]{3,2,1,0:T(8,128)(2,1)}, bf16[2,2,32,768]{3,2,1,0:T(8,128)(2,1)S(1)}, u32[]{:S(2)}, u32[]{:S(2)}) collective-permute-start(bf16[2,2,32,768]{3,2,1,0:T(8,128)(2,1)} %get-tuple-element.289), channel_id=1, source_target_pairs={{0,3},{1,0},{2,1},{3,2},{4,7},{5,4},{6,5},{7,6},{8,11},{9,8},{10,9... | collective-permute-start | bytes 589832 | tf_op jit(solution)/shard_map/ppermute | solution.py:68
  522.8 33.9 %collective-permute-start.162 = (bf16[2,2,32,768]{3,2,1,0:T(8,128)(2,1)}, bf16[2,2,32,768]{3,2,1,0:T(8,128)(2,1)}, u32[]{:S(2)}, u32[]{:S(2)}) collective-permute-start(bf16[2,2,32,768]{3,2,1,0:T(8,128)(2,1)} %get-tuple-element.290), channel_id=1, source_target_pairs={{0,2},{1,3},{2,0},{3,1},{4,6},{5,7},{6,4},{7,5},{8,10},{9,11},{10,... | collective-permute-start | bytes 589832 | tf_op jit(solution)/shard_map/ppermute | solution.py:68
  541.8 40.6 %collective-permute-start.194 = (bf16[4,128,1024]{2,1,0:T(8,128)(2,1)}, bf16[4,128,1024]{2,1,0:T(8,128)(2,1)S(1)}, u32[]{:S(2)}, u32[]{:S(2)}) collective-permute-start(bf16[4,128,1024]{2,1,0:T(8,128)(2,1)} %get-tuple-element.267), channel_id=1, source_target_pairs={{0,16},{16,0},{1,17},{17,1},{2,18},{18,2},{3,19},{19,3},{4,20},{20... | collective-permute-start | bytes 3145736 | tf_op jit(solution)/shard_map/ppermute | solution.py:68
  552.3 37.7 %collective-permute-start.148 = (bf16[4,2,2,32,1024]{4,3,2,1,0:T(8,128)(2,1)}, bf16[4,2,2,32,1024]{4,3,2,1,0:T(8,128)(2,1)S(1)}, u32[]{:S(2)}, u32[]{:S(2)}) collective-permute-start(bf16[4,2,2,32,1024]{4,3,2,1,0:T(8,128)(2,1)} %get-tuple-element.237), channel_id=1, source_target_pairs={{0,16},{16,0},{1,17},{17,1},{2,18},{18,2},{3,19},{19,3},{4,20},{20... | collective-permute-start | bytes 3145736 | tf_op jit(solution)/shard_map/ppermute | solution.py:68
  586.7 22.3 %collective-permute-start.196 = (bf16[128,1024]{1,0:T(8,128)(2,1)S(1)}, bf16[128,1024]{1,0:T(8,128)(2,1)S(1)}, u32[]{:S(2)}, u32[]{:S(2)}) collective-permute-start(bf16[128,1024]{1,0:T(8,128)(2,1)S(1)} %get-tuple-element.276), channel_id=1, source_target_pairs={{0,2},{1,3},{2,0},{3,1},{4,6},{5,7},{6,4},{7,5},{8,10},{9,11},{10,... | collective-permute-start | bytes 786440 | tf_op jit(solution)/shard_map/ppermute | solution.py:68
  586.7 22.3 %collective-permute-start.195 = (bf16[128,1024]{1,0:T(8,128)(2,1)S(1)}, bf16[128,1024]{1,0:T(8,128)(2,1)S(1)}, u32[]{:S(2)}, u32[]{:S(2)}) collective-permute-start(bf16[128,1024]{1,0:T(8,128)(2,1)S(1)} %get-tuple-element.274), channel_id=1, source_target_pairs={{0,1},{1,2},{2,3},{3,0},{4,5},{5,6},{6,7},{7,4},{8,9},{9,10},{10,1... | collective-permute-start | bytes 786440 | tf_op jit(solution)/shard_map/ppermute | solution.py:68
  596.4 40.1 %collective-permute-start.144 = (bf16[4,2,2,32,768]{4,3,2,1,0:T(8,128)(2,1)}, bf16[4,2,2,32,768]{4,3,2,1,0:T(8,128)(2,1)}, u32[]{:S(2)}, u32[]{:S(2)}) collective-permute-start(bf16[4,2,2,32,768]{4,3,2,1,0:T(8,128)(2,1)} %get-tuple-element.231), channel_id=1, source_target_pairs={{0,16},{16,0},{1,17},{17,1},{2,18},{18,2},{3,19},{19,3},{4,20},{20... | collective-permute-start | bytes 2359304 | tf_op jit(solution)/shard_map/ppermute | solution.py:68
  608.9 22.9 %collective-permute-start.150 = (bf16[2,2,32,1024]{3,2,1,0:T(8,128)(2,1)}, bf16[2,2,32,1024]{3,2,1,0:T(8,128)(2,1)}, u32[]{:S(2)}, u32[]{:S(2)}) collective-permute-start(bf16[2,2,32,1024]{3,2,1,0:T(8,128)(2,1)} %get-tuple-element.286), channel_id=1, source_target_pairs={{0,2},{1,3},{2,0},{3,1},{4,6},{5,7},{6,4},{7,5},{8,10},{9,11},{10,... | collective-permute-start | bytes 786440 | tf_op jit(solution)/shard_map/ppermute | solution.py:68
  631.8 38.4 %collective-permute-start.182 = (bf16[2,2,4,32,1024]{4,3,2,1,0:T(8,128)(2,1)}, bf16[2,2,4,32,1024]{4,3,2,1,0:T(8,128)(2,1)}, u32[]{:S(2)}, u32[]{:S(2)}) collective-permute-start(bf16[2,2,4,32,1024]{4,3,2,1,0:T(8,128)(2,1)} %slice_bitcast_fusion.1), channel_id=1, source_target_pairs={{0,4},{4,0},{1,5},{5,1},{2,6},{6,2},{3,7},{7,3},{8,12},{12,8},{9,1... | collective-permute-start | bytes 3145736 | tf_op jit(solution)/shard_map/ppermute | solution.py:68
  675.6 32.0 %collective-permute-start.143 = (bf16[256,1024]{1,0:T(8,128)(2,1)}, bf16[256,1024]{1,0:T(8,128)(2,1)}, u32[]{:S(2)}, u32[]{:S(2)}) collective-permute-start(bf16[256,1024]{1,0:T(8,128)(2,1)} %get-tuple-element.225), channel_id=1, source_target_pairs={{0,0},{1,4},{2,8},{3,12},{4,1},{5,5},{6,9},{7,13},{8,2},{9,6},{10,... | collective-permute-start | bytes 1572872 | tf_op jit(solution)/shard_map/ppermute | solution.py:694
  (323 other events, 3969.9 us)

commit v2 on v1

v2 whole, which is shorter than its diff:
```python
import functools

import jax
import jax.numpy as jnp
from jax import lax
from jax.experimental import pallas as pl
from jax.experimental.pallas import tpu as pltpu
from jax.sharding import Mesh
from jax.sharding import PartitionSpec as P

D = 1024
HEADS = 8
HEAD_DIM = 128
CORES = 2
norm_eps = 1e-05
masked_score = -1e30
BF = jnp.bfloat16
F32 = jnp.float32
TILE = 16
VMEM_BYTES = 32 * 1024 * 1024

HI, XX, CORE, BLK = "hi", "xx", "core", "blk"


def nn(a, b):
    return lax.dot_general(a, b, (((1,), (0,)), ((), ())), preferred_element_type=F32)


def nt(a, b):
    return lax.dot_general(a, b, (((1,), (1,)), ((), ())), preferred_element_type=F32)


def tn(a, b):
    return lax.dot_general(a, b, (((0,), (0,)), ((), ())), preferred_element_type=F32)


def shape(dims, dtype):
    return jax.ShapeDtypeStruct(tuple(dims), dtype)


def run(kernel, outs, smem, arrays, scratch=(), flops=0, trans=0):
    size = lambda s: s.size * s.dtype.itemsize
    moved = sum(size(a) for a in arrays) + sum(size(o) for o in outs)
    return pl.pallas_call(
        kernel,
        out_shape=tuple(outs),
        in_specs=[pl.BlockSpec(memory_space=pltpu.SMEM)] * len(smem)
        + [pl.BlockSpec(memory_space=pltpu.VMEM)] * len(arrays),
        out_specs=tuple(pl.BlockSpec(memory_space=pltpu.VMEM) for _ in outs),
        scratch_shapes=list(scratch),
        compiler_params=pltpu.CompilerParams(vmem_limit_bytes=VMEM_BYTES),
        cost_estimate=pl.CostEstimate(flops=flops, bytes_accessed=moved, transcendentals=trans),
    )(*smem, *arrays)


def slots_of(xs):
    return [(k, dc) for k in range(xs) for dc in range(CORES)]


def lo_minus(me, xs, k, dc):
    return lax.rem(me[1] - k + xs, xs) * CORES + lax.rem(me[2] + dc, CORES)


def lo_plus(me, xs, k, dc):
    return lax.rem(me[1] + k, xs) * CORES + lax.rem(me[2] + dc, CORES)


def block_minus(me, xs, k, dc):
    return lax.rem(me[2] + dc, CORES) * xs + lax.rem(me[1] - k + xs, xs)


def tie(x, *after):
    return lax.optimization_barrier((x, after))[0]


def shift(x, axis, size, step):
    return lax.ppermute(x, axis, [(i, (i + step) % size) for i in range(size)])


def gather_lo(x, xs):
    out = {}
    for k in range(xs):
        out[k, 0] = x if k == 0 else shift(x, XX, xs, k)
    for k in range(xs):
        out[k, 1] = shift(out[k, 0], CORE, CORES, 1)
    return out


def scatter_lo(parts, xs):
    got = {}
    for k in list(range(1, xs)) + [0]:
        got[k] = shift(parts[k, 1].astype(BF), CORE, CORES, 1)
    terms = [parts[0, 0]]
    for k in range(1, xs):
        both = (parts[k, 0].astype(F32) + got[k].astype(F32)).astype(BF)
        terms.append(shift(both, XX, xs, -k))
    return terms + [got[0]]


def send_lo(x, xs, k, dc):
    if k == 0 and dc == 0:
        return x
    pairs = [
        (a * CORES + c, ((a + k) % xs) * CORES + (c + dc) % CORES) for a in range(xs) for c in range(CORES)
    ]
    return lax.ppermute(x, (XX, CORE), pairs)


def exchange_lo(blocks, xs, sign):
    order = [s for s in slots_of(xs) if s[0]] + [s for s in slots_of(xs) if not s[0]]
    return {(k, dc): send_lo(blocks[k, dc], xs, sign * k, dc) for k, dc in order}


class Work:
    def __init__(self, steps):
        self.steps = steps
        next(steps)

    def step(self, *after):
        try:
            return self.steps.send(after)
        except StopIteration as end:
            return end.value


def fetch(x, out, hs, ts):
    out[0, 0] = way = x
    for kb in range(ts):
        came = way
        up = [shift(came, HI, hs, kh) for kh in range(1, hs)]
        if kb + 1 < ts:
            way = shift(came, BLK, ts, 1)
        after = yield came
        up, way = tie((up, way), after)
        for kh in range(1, hs):
            out[kh, kb] = up[kh - 1]
        if kb + 1 < ts:
            out[0, kb + 1] = way
    return up


def reduce(parts, out, hs, ts):
    got = [shift(parts[kh], HI, hs, kh) for kh in range(1, hs)]
    after = yield parts
    got = tie(got, after)
    total = []
    for kb in range(ts):
        block = parts[0][kb].astype(F32)
        for g in got:
            block = block + g[kb].astype(F32)
        total.append(block if kb == 0 else block.astype(BF))
    out.append(total[0])
    for kb in range(1, ts):
        way = shift(total[kb], BLK, ts, kb)
        after = yield total
        way = tie(way, after)
        out.append(way)
    return way


def pieces_of(out, hs, ts):
    return [out[kh, kb] for kh in range(hs) for kb in range(ts)]


def total_of(terms, at=slice(None)):
    total = terms[0][at].astype(F32)
    for t in terms[1:]:
        total = total + t[at].astype(F32)
    return total


def norm_parts(values):
    centre = values - jnp.mean(values, axis=-1, keepdims=True)
    spread = jnp.mean(centre * centre, axis=-1, keepdims=True)
    rstd = lax.rsqrt(spread + norm_eps)
    return centre * rstd, rstd


def near_kernel(xs, ts, each, me, wq, *refs):
    given, outs, line = refs[:6], refs[6:-9], refs[-9]
    weight, fields, sems = refs[-8], refs[-7:-1], refs[-1]
    copies = [pltpu.make_async_copy(wq.at[0], weight, sems.at[0])]
    for j in range(6):
        copies.append(pltpu.make_async_copy(given[j], fields[j], sems.at[j + 1]))
    for c in copies:
        c.start()
    line[...] = jnp.zeros_like(line)
    for c in copies:
        c.wait()
    layers, rows, _ = wq.shape
    for layer in range(layers):
        at = layer * each * 12
        for f in fields[:4]:
            wide = f.shape[1]
            line[0:1, at : at + wide] = f[layer : layer + 1, :].astype(F32)
            at += wide
        for f in fields[4:]:
            for j in range(2):
                line[0:1, at : at + each] = f[layer, j : j + 1, :].astype(F32)
                at += each
    small = line[...].astype(BF)
    chunk = outs[0].shape[1] // 3
    for out, (k, dc) in zip(outs, slots_of(xs)):
        lo = lo_plus(me, xs, k, dc)
        for j in range(3):
            off = pl.multiple_of((j * ts + lo) * chunk, 128)
            out[:rows, j * chunk : (j + 1) * chunk] = weight[:, pl.ds(off, chunk)]
        out[rows:, :] = small


def near_cuts_of(me, wq, fields, xs, ts):
    _, rows, full = wq.shape
    outs = [shape((rows + TILE, full // ts), BF)] * ts
    got = pl.pallas_call(
        functools.partial(near_kernel, xs, ts, fields[1].shape[1]),
        out_shape=tuple(outs),
        in_specs=[pl.BlockSpec(memory_space=pltpu.SMEM)] + [pl.BlockSpec(memory_space=pl.ANY)] * 7,
        out_specs=tuple(pl.BlockSpec(memory_space=pltpu.VMEM) for _ in outs),
        scratch_shapes=[pltpu.VMEM((TILE, full // ts), F32), pltpu.VMEM(wq.shape[1:], BF)]
        + [pltpu.VMEM(f.shape, BF) for f in fields]
        + [pltpu.SemaphoreType.DMA((7,))],
        compiler_params=pltpu.CompilerParams(vmem_limit_bytes=VMEM_BYTES),
    )(me, wq, *fields)
    return dict(zip(slots_of(xs), got))


def message_kernel(tok, ids, msg):
    n = tok.shape[0]
    msg[:n, :] = tok[...]
    high = ids[...] // 256
    below = jnp.concatenate([high, ids[...] - high * 256], 0).astype(F32)
    fill = jnp.concatenate([below, jnp.zeros((TILE - 2, n), F32)], 0)
    msg[n:, :] = jnp.zeros((TILE, D), BF)
    msg[n:, :n] = fill.astype(BF)


def message_of(tok, ids):
    (got,) = run(message_kernel, [shape((tok.shape[0] + TILE, D), BF)], [], [tok, ids])
    return got


def rest_kernel(xs, ts, me, wq, wu, *outs):
    layers = wq.shape[0]
    chunk = wq.shape[2] // (3 * ts)
    half = wu.shape[2] // (2 * ts)
    for rest, (k, dc) in zip(outs, slots_of(xs)):
        lo = lo_plus(me, xs, k, dc)
        at = 0
        for layer in range(layers):
            if layer:
                for j in range(3):
                    got = wq[layer, :, pl.ds(pl.multiple_of((j * ts + lo) * chunk, 128), chunk)]
                    rest[:, at : at + chunk] = got
                    at += chunk
            for j in range(2):
                got = wu[layer, :, pl.ds(pl.multiple_of((j * ts + lo) * half, 128), half)]
                rest[:, at : at + half] = got
                at += half


def rest_cuts_of(me, wq, wu, xs, ts):
    layers, rows, full = wu.shape
    wide = 3 * D // ts
    got = run(
        functools.partial(rest_kernel, xs, ts),
        [shape((rows, layers * (wide + full // ts) - wide), BF)] * ts,
        [me],
        [wq, wu],
    )
    return dict(zip(slots_of(xs), got))


def fold_in(out, block, at, cols):
    rows = block.shape[0]
    for p in range(block.shape[1] // cols):
        out[p * rows : (p + 1) * rows, at : at + cols] = block[:, p * cols : (p + 1) * cols]


def pack_first_kernel(count, rows, *refs):
    blocks, out_w, out = refs[:count], refs[count], refs[count + 1]
    wide = blocks[0].shape[1]
    for j, block in enumerate(blocks):
        out[j * rows : (j + 1) * rows, :wide] = block[:rows, :]
    fold_in(out, out_w.at[0], wide, out.shape[1] - wide)
    tail = jnp.concatenate([b[rows : rows + 1, :].astype(F32) for b in blocks], 0)
    tail = jnp.concatenate([tail, jnp.zeros((TILE - count, wide), F32)], 0)
    out[count * rows :, :wide] = tail.astype(BF)
    out[count * rows :, wide:] = jnp.zeros((TILE, out.shape[1] - wide), BF)


def pack_first(blocks, out_w):
    count = len(blocks)
    rows, wide = blocks[0].shape[0] - TILE, blocks[0].shape[1]
    (got,) = run(
        functools.partial(pack_first_kernel, count, rows),
        [shape((count * rows + TILE, wide + D // count), BF)],
        [],
        blocks + [out_w],
    )
    return got


def pack_rest_kernel(count, layers, wide, *refs):
    blocks, down, out_w = refs[:count], refs[count], refs[count + 1]
    outs = refs[count + 2 :]
    rows = blocks[0].shape[0]
    cols = outs[0].shape[1] // 2
    at = 0
    for layer in range(layers):
        if layer:
            attn = outs[2 * layer - 1]
            for j, block in enumerate(blocks):
                attn[j * rows : (j + 1) * rows, :wide] = block[:, at : at + wide]
            fold_in(attn, out_w.at[layer], wide, D // count)
            at += wide
        ffn = outs[2 * layer]
        for j, block in enumerate(blocks):
            ffn[j * rows : (j + 1) * rows, :cols] = block[:, at : at + cols]
        fold_in(ffn, down.at[layer], cols, cols)
        at += cols


def pack_rest(blocks, down, out_w, wide, cols):
    count = len(blocks)
    rows = blocks[0].shape[0]
    layers = down.shape[0]
    outs = []
    for layer in range(layers):
        if layer:
            outs.append(shape((count * rows, wide + D // count), BF))
        outs.append(shape((count * rows, 2 * cols), BF))
    return run(
        functools.partial(pack_rest_kernel, count, layers, wide), outs, [], blocks + [down, out_w]
    )


def params_kernel(hs, ts, xs, rows, layers, each, me, *refs):
    pieces = refs[: hs * ts]
    vec, up, qkv = refs[hs * ts :]
    count = hs * ts * ts
    values = jnp.concatenate([p[ts * rows : ts * rows + ts, : qkv.shape[1]].astype(F32) for p in pieces], 0).astype(BF)
    at = lax.broadcasted_iota(jnp.int32, (1, count), 1)
    kh, kb, slot = at // (ts * ts), (at // ts) % ts, at % ts
    k, dc = slot // CORES, slot % CORES
    h = lax.rem(me[0] - kh + hs, hs)
    l = lax.rem(me[1] - k + xs, xs) * CORES + lax.rem(me[2] + dc, CORES)
    b = lax.rem(me[3] - kb + ts, ts)
    owner = (h * ts + l) * ts + b
    pick = (lax.broadcasted_iota(jnp.int32, (count, count), 0) == owner).astype(BF)
    table = nn(pick, values).astype(BF)
    lo = me[1] * CORES + me[2]

    def spread(first, size, wide):
        tile = lax.broadcasted_iota(jnp.int32, (size, wide), 1) % size
        same = (tile == lax.broadcasted_iota(jnp.int32, (size, wide), 0)).astype(BF)
        return nn(table[:, first : first + size], same)

    def keep(x, mask):
        return jnp.sum(jnp.where(mask, x, 0.0), axis=0, keepdims=True)

    row = lambda wide: lax.broadcasted_iota(jnp.int32, (count, wide), 0)
    col = lambda wide: lax.broadcasted_iota(jnp.int32, (count, wide), 1)
    full = each * count
    own_up, own_q = full * up.shape[1] // D, qkv.shape[1] // 3
    for layer in range(layers):
        first = layer * each * 12
        member = row(own_q) // ts % ts == lo
        part = row(own_q) % ts == col(own_q) // (2 * each)
        half = row(own_q) // (ts * ts)
        q = spread(first, 2 * each, own_q)
        qkv[layer : layer + 1, :own_q] = keep(q, member & part & (half == 0))
        qkv[layer : layer + 1, own_q : 2 * own_q] = jnp.zeros((1, own_q), F32)
        qkv[layer : layer + 1, 2 * own_q :] = keep(q, member & part & (half == 1))
        first = first + 2 * each
        mine = col(full) // each == row(full)
        for f, skip in enumerate((0, 5, 6, 7, 8, 9)):
            vec[layer * 6 + f : layer * 6 + f + 1, :] = keep(spread(first + skip * each, each, full), mine)
        here = (row(own_up) // ts % ts == lo) & (
            (row(own_up) // (ts * ts)) * ts + row(own_up) % ts == col(own_up) // (4 * each)
        )
        up[layer : layer + 1, :] = keep(spread(first + each, 4 * each, own_up), here)


def params(me, pieces, rows, layers, each, own_up, own_q, hs, ts, xs):
    return run(
        functools.partial(params_kernel, hs, ts, xs, rows, layers, each),
        [shape((layers * 6, D), F32), shape((layers, own_up), F32), shape((layers, 3 * own_q), F32)],
        [me],
        pieces,
    )


def fold_out(piece, rows, at, cols, parts):
    return jnp.concatenate([piece[p * rows : (p + 1) * rows, at : at + cols] for p in range(parts)], 1)


def piece_at(refs, at, whole, hs, ts, me):
    kh, kb = at // ts, at % ts
    h = lax.rem(me[0] - kh + hs, hs)
    if whole:
        return refs[kh].at[kb], h, kb
    return refs[at], h, lax.rem(me[3] - kb + ts, ts)


def place_attn_kernel(hs, ts, xs, whole, with_out, me, *refs):
    qkv = refs[-2] if with_out else refs[-1]
    rows, wide = qkv.shape[3:]
    for at in range(hs * ts):
        piece, h, b = piece_at(refs, at, whole, hs, ts, me)
        for j, (k, dc) in enumerate(slots_of(xs)):
            qkv[h, lo_minus(me, xs, k, dc), b] = piece[j * rows : (j + 1) * rows, :wide]
        if with_out:
            out = refs[-1]
            cols = out.shape[3] // ts
            for p in range(ts):
                out[h, b, :, p * cols : (p + 1) * cols] = piece[p * rows : (p + 1) * rows, wide : wide + cols]


def place_attn(me, pieces, rows, hs, ts, xs, with_out):
    whole = len(pieces) == hs
    wide = 3 * D // ts
    got = run(
        functools.partial(place_attn_kernel, hs, ts, xs, whole, with_out),
        [shape((hs, ts, ts, rows, wide), BF)] + ([shape((hs, ts, rows, D), BF)] if with_out else []),
        [me],
        pieces,
    )
    return (got[0].reshape(D, wide),) + tuple(got[1:])


def place_ffn_kernel(hs, ts, xs, whole, me, *refs):
    up, down = refs[-2:]
    rows, cols = up.shape[3:]
    tall = down.shape[2]
    for at in range(hs * ts):
        piece, h, b = piece_at(refs, at, whole, hs, ts, me)
        for j, (k, dc) in enumerate(slots_of(xs)):
            up[h, lo_minus(me, xs, k, dc), b] = piece[j * rows : (j + 1) * rows, :cols]
        for p in range(D // cols):
            down[h, b, :, p * cols : (p + 1) * cols] = piece[p * tall : (p + 1) * tall, cols:]


def place_ffn(me, pieces, hs, ts, xs):
    whole = len(pieces) == hs
    tall, wide = pieces[0].shape[-2:]
    cols = wide // 2
    up, down = run(
        functools.partial(place_ffn_kernel, hs, ts, xs, whole),
        [shape((hs, ts, ts, tall // ts, cols), BF), shape((hs, ts, tall * cols // D, D), BF)],
        [me],
        pieces,
    )
    return up.reshape(D, cols), down.reshape(-1, D)


def place_out_kernel(hs, ts, xs, me, *refs):
    out = refs[-1]
    for j, (k, dc) in enumerate(slots_of(xs)):
        out[:, lo_minus(me, xs, k, dc)] = refs[j][...]


def place_out(me, group, hs, ts, xs):
    _, _, rows, wide = group[0].shape
    (got,) = run(
        functools.partial(place_out_kernel, hs, ts, xs), [shape((hs, ts, ts, rows, wide), BF)], [me], group
    )
    return got.reshape(-1, wide)


def attn_fwd_kernel(ts, xs, heads, raw, layer, me, slopes, *refs):
    given = refs[:ts]
    if raw:
        w, bias, vec = refs[ts : ts + 3]
        qkv, out_t, lse, seg_row, seg_col = refs[ts + 3 : ts + 8]
        outs, normed = refs[ts + 8 : 2 * ts + 8], refs[2 * ts + 8 : 3 * ts + 8]
    else:
        normed = given
        w, bias, seg_row, seg_col = refs[ts : ts + 4]
        qkv, out_t, lse = refs[ts + 4 : ts + 7]
        outs = refs[ts + 7 :]
    n = normed[0].shape[0]
    width = heads * HEAD_DIM
    for j, (k, dc) in enumerate(slots_of(xs)):
        off = pl.multiple_of(block_minus(me, xs, k, dc) * n, n)
        if raw:
            unit, _ = norm_parts(given[j][:n, :].astype(F32))
            normed[j][...] = (unit * vec[2:3, :] + vec[4:5, :]).astype(BF)
            ids = given[j][n : n + 8, :n].astype(F32)
            ids = ids[0:1, :] * 256.0 + ids[1:2, :]
            seg_row[:, pl.ds(off, n)] = ids
            seg_col[pl.ds(off, n), :] = jnp.broadcast_to(ids, (128, n)).T
        got = nn(normed[j][...], w[...]) + bias[layer : layer + 1, :]
        qkv[pl.ds(off, n), :] = got.astype(BF)
    scale = HEAD_DIM ** (-0.5)
    for i in range(ts):
        length = (i + 1) * n
        key_at = lax.broadcasted_iota(jnp.int32, (length, n), 0)
        query_at = lax.broadcasted_iota(jnp.int32, (length, n), 1) + i * n
        allowed = (seg_col[:length, 0:1] == seg_row[:, i * n : length]) & (key_at <= query_at)
        distance = (query_at - key_at).astype(F32)
        for h in range(heads):
            here = h * HEAD_DIM
            q = qkv[i * n : length, here : here + HEAD_DIM]
            keys = qkv[:length, width + here : width + here + HEAD_DIM]
            values = qkv[:length, 2 * width + here : 2 * width + here + HEAD_DIM]
            s = nt(keys, q) * scale - slopes[h] * distance
            s = jnp.where(allowed, s, masked_score)
            top = jnp.max(s, axis=0, keepdims=True)
            p = jnp.exp(s - top)
            total = jnp.sum(p, axis=0, keepdims=True)
            out_t[here : here + HEAD_DIM, i * n : length] = tn(values, p.astype(BF)) / total
            lse[h : h + 1, i * n : length] = top + jnp.log(total)
    for j, (k, dc) in enumerate(slots_of(xs)):
        off = pl.multiple_of(block_minus(me, xs, k, dc) * n, n)
        outs[j][...] = out_t[:, pl.ds(off, n)].T.astype(BF)


def attn_fwd(me, slopes, given, w, bias, layer, xs, vec=None, segs=None):
    ts = len(given)
    raw = vec is not None
    heads = slopes.shape[0]
    n = given[0].shape[0] - (TILE if raw else 0)
    length, width = ts * n, heads * HEAD_DIM
    got = run(
        functools.partial(attn_fwd_kernel, ts, xs, heads, raw, layer),
        [shape((length, 3 * width), BF), shape((width, length), F32), shape((heads, length), F32)]
        + ([shape((1, length), F32), shape((length, 128), F32)] if raw else [])
        + [shape((n, width), BF)] * ts
        + ([shape((n, D), BF)] * ts if raw else []),
        [me, slopes],
        given + [w, bias] + ([vec] if raw else list(segs)),
        flops=2 * length * D * 3 * width + 3 * length * length * width,
    )
    if raw:
        return got[0], got[1], got[2], list(got[5 : 5 + ts]), list(got[5 + ts :]), (got[3], got[4])
    return got[0], got[1], got[2], list(got[3:]), given, segs


def attn_bwd_kernel(ts, xs, heads, me, slopes, *refs):
    grads = refs[:ts]
    qkv, out_t, lse, w, seg_row, seg_col = refs[ts : ts + 6]
    parts = refs[ts + 6 : 2 * ts + 6]
    souts = refs[2 * ts + 6 : 3 * ts + 6]
    gbuf, dq_buf, dk_buf, dv_buf = refs[3 * ts + 6 :]
    n = grads[0].shape[0]
    width = heads * HEAD_DIM
    scale = HEAD_DIM ** (-0.5)
    for j, (k, dc) in enumerate(slots_of(xs)):
        off = pl.multiple_of(block_minus(me, xs, k, dc) * n, n)
        gbuf[pl.ds(off, n), :] = grads[j][...]
    dk_buf[...] = jnp.zeros_like(dk_buf)
    dv_buf[...] = jnp.zeros_like(dv_buf)
    for i in range(ts):
        length = (i + 1) * n
        key_at = lax.broadcasted_iota(jnp.int32, (length, n), 0)
        query_at = lax.broadcasted_iota(jnp.int32, (length, n), 1) + i * n
        allowed = (seg_col[:length, 0:1] == seg_row[:, i * n : length]) & (key_at <= query_at)
        distance = (query_at - key_at).astype(F32)
        for h in range(heads):
            here = h * HEAD_DIM
            q = qkv[i * n : length, here : here + HEAD_DIM]
            keys = qkv[:length, width + here : width + here + HEAD_DIM]
            values = qkv[:length, 2 * width + here : 2 * width + here + HEAD_DIM]
            g = gbuf[i * n : length, here : here + HEAD_DIM]
            delta = jnp.sum(
                g.astype(F32).T * out_t[here : here + HEAD_DIM, i * n : length], axis=0, keepdims=True
            )
            s = nt(keys, q) * scale - slopes[h] * distance
            p = jnp.where(allowed, jnp.exp(s - lse[h : h + 1, i * n : length]), 0.0)
            ds = (p * (nt(values, g) - delta)).astype(BF)
            dq_buf[i * n : length, here : here + HEAD_DIM] = tn(ds, keys) * scale
            dk_buf[:length, here : here + HEAD_DIM] += nn(ds, q)
            dv_buf[:length, here : here + HEAD_DIM] += nn(p.astype(BF), g)
    for j, (k, dc) in enumerate(slots_of(xs)):
        off = pl.multiple_of(block_minus(me, xs, k, dc) * n, n)
        rows = pl.ds(off, n)
        parts[j][:, :width] = dq_buf[rows, :].astype(BF)
        parts[j][:, width : 2 * width] = (dk_buf[rows, :] * scale).astype(BF)
        parts[j][:, 2 * width :] = dv_buf[rows, :].astype(BF)
        souts[j][...] = nt(parts[j][...], w[...]).astype(souts[j].dtype)


def attn_bwd(me, slopes, grads, qkv, out_t, lse, w, seg_row, seg_col, xs):
    ts = len(grads)
    heads = slopes.shape[0]
    n = grads[0].shape[0]
    length, width = ts * n, heads * HEAD_DIM
    got = run(
        functools.partial(attn_bwd_kernel, ts, xs, heads),
        [shape((n, 3 * width), BF)] * ts + [shape((n, D), F32)] + [shape((n, D), BF)] * (ts - 1),
        [me, slopes],
        grads + [qkv, out_t, lse, w, seg_row, seg_col],
        scratch=[pltpu.VMEM((length, width), BF)] + [pltpu.VMEM((length, width), F32)] * 3,
        flops=2 * length * D * 3 * width + 6 * length * length * width,
    )
    return list(got[:ts]), list(got[ts:])


def out_kernel(ts, xs, at, me, *refs):
    heads = refs[:ts]
    w, vec, stream, middle, normed = refs[ts:]
    width = heads[0].shape[1]
    total = stream[: middle.shape[0], :].astype(F32) + vec[at : at + 1, :]
    for j, (k, dc) in enumerate(slots_of(xs)):
        off = pl.multiple_of(lo_plus(me, xs, k, dc) * width, width)
        total = total + nn(heads[j][...], w[pl.ds(off, width), :])
    middle[...] = total
    unit, _ = norm_parts(total)
    normed[...] = (unit * vec[at + 3 : at + 4, :] + vec[at + 5 : at + 6, :]).astype(BF)


def out_project(me, heads, w, vec, layer, stream, xs):
    n = heads[0].shape[0]
    return run(
        functools.partial(out_kernel, len(heads), xs, 6 * layer),
        [shape((n, D), F32), shape((n, D), BF)],
        [me],
        heads + [w, vec, stream],
        flops=2 * n * D * D,
    )


def ffn_fwd_kernel(count, layer, *refs):
    normed = refs[:count]
    up, bias, down = refs[count : count + 3]
    outs = refs[count + 3 :]
    root, cubic = 0.7978845608028654, 0.044715
    for j in range(count):
        hidden, slope, part = outs[3 * j : 3 * j + 3]
        u = nn(normed[j][...], up[...]) + bias[layer : layer + 1, :]
        square = u * u
        t = jnp.tanh(root * (u + cubic * square * u))
        half = 0.5 * (1.0 + t)
        hidden[...] = (u * half).astype(BF)
        slope[...] = (half + 0.5 * u * (1.0 - t * t) * (root * (1.0 + 3.0 * cubic * square))).astype(BF)
        part[...] = nn(hidden[...], down[...]).astype(part.dtype)


def ffn_fwd(normed, up, bias, layer, down, kinds):
    n = normed[0].shape[0]
    wide = up.shape[1]
    outs = []
    for kind in kinds:
        outs += [shape((n, wide), BF), shape((n, wide), BF), shape((n, D), kind)]
    got = run(
        functools.partial(ffn_fwd_kernel, len(normed), layer),
        outs,
        [],
        normed + [up, bias, down],
        flops=4 * n * D * wide * len(normed),
    )
    return list(got[0::3]), list(got[1::3]), list(got[2::3])


def ffn_bwd_kernel(count, *refs):
    grads, slopes = refs[:count], refs[count : 2 * count]
    up, down = refs[2 * count : 2 * count + 2]
    outs = refs[2 * count + 2 :]
    for j in range(count):
        du, part = outs[2 * j : 2 * j + 2]
        du[...] = (nt(grads[j][...], down[...]) * slopes[j][...].astype(F32)).astype(BF)
        part[...] = nt(du[...], up[...]).astype(part.dtype)


def ffn_bwd(grads, slopes, up, down, kinds):
    n = grads[0].shape[0]
    wide = up.shape[1]
    outs = []
    for kind in kinds:
        outs += [shape((n, wide), BF), shape((n, D), kind)]
    got = run(
        functools.partial(ffn_bwd_kernel, len(grads)),
        outs,
        [],
        grads + slopes + [up, down],
        flops=4 * n * D * wide * len(grads),
    )
    return list(got[0::2]), list(got[1::2])


def end_kernel(count, at, last, *refs):
    terms = refs[:count]
    middle, vec = refs[count : count + 2]
    total = middle[...] + vec[at + 1 : at + 2, :]
    for t in terms:
        total = total + t[...].astype(F32)
    if last:
        refs[-1][...] = total.astype(BF)
        return
    stream, normed = refs[count + 2 :]
    stream[...] = total
    unit, _ = norm_parts(total)
    normed[...] = (unit * vec[at + 8 : at + 9, :] + vec[at + 10 : at + 11, :]).astype(BF)


def layer_end(terms, middle, vec, layer, last):
    n = middle.shape[0]
    outs = [shape((n, D), BF)] if last else [shape((n, D), F32), shape((n, D), BF)]
    return run(functools.partial(end_kernel, len(terms), 6 * layer, last), outs, [], terms + [middle, vec])


def norm_back(values, gain, grad):
    unit, rstd = norm_parts(values)
    scaled = grad * gain
    lead = jnp.mean(scaled, axis=-1, keepdims=True)
    along = jnp.mean(scaled * unit, axis=-1, keepdims=True)
    back = rstd * (scaled - lead - unit * along)
    return back, jnp.sum(grad * unit, axis=0, keepdims=True), jnp.sum(grad, axis=0, keepdims=True)


def mid_back_kernel(count, ts, xs, at, me, *refs):
    terms = refs[:count]
    grad, middle, vec, w = refs[count : count + 4]
    dh, dy, sums = refs[count + 4 : count + 7]
    outs = refs[count + 7 :]
    total = terms[0][...].astype(F32)
    for t in terms[1:]:
        total = total + t[...].astype(F32)
    back, gains, shifts = norm_back(middle[...], vec[at : at + 1, :], total)
    now = grad[...].astype(F32) + back
    dh[...] = now
    dy[...] = now.astype(BF)
    sums[0:1, :] = gains
    sums[1:2, :] = shifts
    sums[2:3, :] = jnp.sum(dy[...].astype(F32), axis=0, keepdims=True)
    width = outs[0].shape[1]
    for j, (k, dc) in enumerate(slots_of(xs)):
        off = pl.multiple_of(lo_plus(me, xs, k, dc) * width, width)
        outs[j][...] = nt(dy[...], w[pl.ds(off, width), :]).astype(BF)


def mid_back(me, terms, grad, middle, vec, layer, w, ts, xs):
    n = middle.shape[0]
    got = run(
        functools.partial(mid_back_kernel, len(terms), ts, xs, 6 * layer + 3),
        [shape((n, D), F32), shape((n, D), BF), shape((3, D), F32)] + [shape((n, D // ts), BF)] * ts,
        [me],
        terms + [grad, middle, vec, w],
        flops=2 * n * D * D,
    )
    return got[0], got[1], got[2], list(got[3:])


def start_back_kernel(count, at, *refs):
    terms = refs[:count]
    grad, stream, vec, dh, dz, sums = refs[count:]
    total = terms[0][...].astype(F32)
    for t in terms[1:]:
        total = total + t[...].astype(F32)
    back, gains, shifts = norm_back(stream[: dh.shape[0], :].astype(F32), vec[at : at + 1, :], total)
    now = grad[...] + back
    dh[...] = now
    dz[...] = now.astype(BF)
    sums[0:1, :] = gains
    sums[1:2, :] = shifts
    sums[2:3, :] = jnp.sum(dz[...].astype(F32), axis=0, keepdims=True)


def start_back(terms, grad, stream, vec, layer):
    n = grad.shape[0]
    return run(
        functools.partial(start_back_kernel, len(terms), 6 * layer + 2),
        [shape((n, D), F32), shape((n, D), BF), shape((3, D), F32)],
        [],
        terms + [grad, stream, vec],
    )


def column_sums(refs):
    total = jnp.sum(refs[0][...].astype(F32), axis=0, keepdims=True)
    for b in refs[1:]:
        total = total + jnp.sum(b[...].astype(F32), axis=0, keepdims=True)
    return total


def cols_part(ts, xs, hs, rows, me, left, right, put):
    tile = CORES * ts * rows
    for kh in list(range(1, hs)) + [0]:
        h = lax.rem(me[0] + kh, hs)
        for k in range(xs):
            place_at = (h * ts + lax.rem(me[1] + k, xs) * CORES) * ts * rows
            cols = pl.ds(pl.multiple_of(place_at, tile), tile)
            got = tn(left[0][:, cols], right[0][...])
            for j in range(1, ts):
                got = got + tn(left[j][:, cols], right[j][...])
            for c in range(CORES):
                dc = lax.rem(me[2] + c, CORES)
                for b in range(ts):
                    kb = lax.rem(b - me[3] + ts, ts)
                    at = (c * ts + b) * rows
                    put(kh, kb, dc, k, got[at : at + rows, :].astype(BF))


def wgrad_cols_kernel(ts, xs, hs, rows, beside, me, *refs):
    left, right = refs[:ts], refs[ts : 2 * ts]
    refs = refs[2 * ts :]
    if beside:
        near, refs = refs[0], refs[1:]
    refs[0][...] = column_sums(right)
    outs = refs[1:]
    wide = right[0].shape[1]

    def put(kh, kb, dc, k, block):
        outs[kh][kb, k * CORES + dc, :, :wide] = block

    cols_part(ts, xs, hs, rows, me, left, right, put)
    if beside:
        cols = outs[0].shape[3] - wide
        for kh in range(hs):
            for kb in range(ts):
                for p in range(ts):
                    outs[kh][kb, p, :, wide:] = near[kh, kb, :, p * cols : (p + 1) * cols]


def wgrad_cols(me, left, right, hs, xs, near=None):
    ts = len(left)
    rows = D // (hs * ts * ts)
    n, wide = right[0].shape
    beside = near is not None
    got = run(
        functools.partial(wgrad_cols_kernel, ts, xs, hs, rows, beside),
        [shape((1, wide), F32)] + [shape((ts, ts, rows, wide + (D // ts if beside else 0)), BF)] * hs,
        [me],
        left + right + ([near] if beside else []),
        flops=2 * ts * n * D * wide,
    )
    return got[0], list(got[1:])


def wgrad_down_kernel(ts, hs, rows, tall, me, *refs):
    hidden, dz = refs[:ts], refs[ts : 2 * ts]
    outs = refs[2 * ts :]
    cols = outs[0].shape[3]
    group = min(ts, max(1, 256 // tall))
    for kh in list(range(1, hs)) + [0]:
        h = lax.rem(me[0] + kh, hs)
        for first in range(0, ts, group):
            take = pl.ds(pl.multiple_of((h * ts + first) * tall, group * tall), group * tall)
            got = tn(hidden[0][:, take], dz[0][...])
            for j in range(1, ts):
                got = got + tn(hidden[j][:, take], dz[j][...])
            for b in range(group):
                kb = lax.rem(first + b - me[3] + ts, ts)
                for g in range(ts):
                    p, low = (g * rows) // tall, (g * rows) % tall
                    outs[kh][kb, g] = got[
                        b * tall + low : b * tall + low + rows, p * cols : (p + 1) * cols
                    ].astype(BF)


def wgrad_down(me, hidden, dz, hs):
    ts = len(hidden)
    rows = D // (hs * ts * ts)
    n, wide = hidden[0].shape
    return list(
        run(
            functools.partial(wgrad_down_kernel, ts, hs, rows, wide // (hs * ts)),
            [shape((ts, ts, rows, wide), BF)] * hs,
            [me],
            hidden + dz,
            flops=2 * ts * n * D * wide,
        )
    )


def wgrad_out_kernel(ts, xs, hs, rows, me, *refs):
    left = refs[:ts]
    right, out = refs[ts], refs[ts + 1]
    width = left[0].shape[1]
    for j, (k, dc) in enumerate(slots_of(xs)):
        got = tn(left[j][...], right[...])
        first = lo_plus(me, xs, k, dc) * (width // rows)
        for g in range(width // rows):
            i = first + g
            h = lax.div(i, ts * ts)
            lo = lax.rem(lax.div(i, ts), ts)
            b = lax.rem(i, ts)
            kk = lax.rem(lax.div(lo, CORES) - me[1] + xs, xs)
            dd = lax.rem(lax.rem(lo, CORES) + me[2], CORES)
            kh = lax.rem(h - me[0] + hs, hs)
            kb = lax.rem(b - me[3] + ts, ts)
            out[dd, kk, kh, kb] = got[g * rows : (g + 1) * rows, :].astype(BF)


def wgrad_out(me, left, right, hs, xs):
    ts = len(left)
    rows = D // (hs * ts * ts)
    (got,) = run(
        functools.partial(wgrad_out_kernel, ts, xs, hs, rows),
        [shape((CORES, xs, hs, ts, rows, D), BF)],
        [me],
        left + [right],
        flops=2 * right.shape[0] * D * D,
    )
    return got


def join_kernel(ts, xs, layers, me, *refs):
    out_q, out_u = refs[-2:]
    wide = out_q.shape[2] // (3 * ts)
    chunk = out_u.shape[2] // (2 * ts)
    at = 0
    for layer in range(layers):
        for k, dc in slots_of(xs):
            lo = lo_minus(me, xs, k, dc)
            q, u = refs[at], refs[at + 1]
            at += 2
            for j in range(3):
                off = pl.multiple_of(j * D + lo * wide, 128)
                out_q[layer, :, pl.ds(off, wide)] = q[:, j * wide : (j + 1) * wide].astype(F32)
            for j in range(2):
                off = pl.multiple_of(j * (chunk * ts) + lo * chunk, 128)
                out_u[layer, :, pl.ds(off, chunk)] = u[:, j * chunk : (j + 1) * chunk].astype(F32)


def join(me, grads, ts, xs):
    layers = len(grads)
    arrays = []
    for q, u in grads:
        for s in slots_of(xs):
            arrays += [q[s], u[s]]
    rows = arrays[0].shape[0]
    return run(
        functools.partial(join_kernel, ts, xs, layers),
        [shape((layers, rows, arrays[0].shape[1] * ts), F32), shape((layers, rows, arrays[1].shape[1] * ts), F32)],
        [me],
        arrays,
    )


def sum_small(mine, shared, hs, ts, xs):
    mine = mine + shift(mine, CORE, CORES, 1)
    for_all = mine
    for k in range(1, xs):
        for_all = for_all + shift(mine, XX, xs, k)
    both = jnp.concatenate([for_all, shared], 0)
    total = both
    for kh in range(1, hs):
        total = total + shift(both, HI, hs, kh)
    out = total
    for kb in range(1, ts):
        out = out + shift(total, BLK, ts, kb)
    return out


def on_device(
    hs,
    ts,
    xs,
    tokens,
    segment_ids,
    out_grad,
    qkv_weight,
    qv_bias,
    out_weight,
    out_bias,
    up_weight,
    up_bias,
    down_weight,
    down_bias,
    norm_gain,
    norm_shift,
):
    layers = qkv_weight.shape[0]
    n = tokens.shape[1]
    length = ts * n
    heads = HEADS // ts
    index = tuple(lax.axis_index(a) for a in (HI, XX, CORE, BLK))
    hi, xx, core, blk = index
    lo = xx * CORES + core
    me = jnp.stack(index).astype(jnp.int32)
    slots = slots_of(xs)
    place_of = [(a % xs) * CORES + a // xs for a in range(ts)]
    turn = [(place_of[a] * ts + b, place_of[b] * ts + a) for a in range(ts) for b in range(ts)]
    turned = lambda x: lax.ppermute(x, (XX, CORE, BLK), turn)
    rows, each = qkv_weight.shape[1], out_bias.shape[1]
    wide, cols = 3 * D // ts, up_weight.shape[2] // ts
    fields = (qv_bias, out_bias, up_bias, down_bias, norm_gain, norm_shift)
    slopes = jnp.exp2(-8.0 * (lo * heads + jnp.arange(heads, dtype=F32) + 1.0) / HEADS)

    def own_columns(cuts):
        mine = exchange_lo(cuts, xs, 1)
        return [mine[s] for s in slots]

    def gather_out(near):
        group = gather_lo(near, xs)
        return place_out(me, [group[s] for s in slots], hs, ts, xs)

    mine = own_columns(near_cuts_of(me, qkv_weight, fields, xs, ts))
    tokens_own = turned(tie(message_of(tokens[0], segment_ids), mine))
    attn_out, ffn_out = {}, {}
    attn_work = Work(fetch(pack_first(mine, out_weight), attn_out, hs, ts))
    late_q, late_u = tie((qkv_weight, up_weight), mine)
    rest = own_columns(rest_cuts_of(me, late_q, late_u, xs, ts))
    packed = pack_rest(rest, down_weight, out_weight, wide, cols)
    for _ in range(ts):
        attn_work.step()
    by = gather_lo(tokens_own, xs)
    given = [by[s] for s in slots]
    attn_pieces = pieces_of(attn_out, hs, ts)
    ffn_work = Work(fetch(packed[0], ffn_out, hs, ts))
    w_qkv, out_near = place_attn(me, attn_pieces, rows, hs, ts, xs, True)
    vec, up_vec, qkv_vec = params(me, attn_pieces, rows, layers, each, cols, wide // 3, hs, ts, xs)

    stream = tokens_own
    stored, weights = [], []
    segs = None
    for l in range(layers):
        more = l + 1 < layers
        given = tie(given, ffn_work.step(w_qkv))
        if l + 1 == layers:
            grad_own = turned(tie(out_grad[0], given))
        w_out = gather_out(out_near)
        qkv, out_t, lse, heads_by, all_one, segs = attn_fwd(
            me, slopes, given, w_qkv, qkv_vec, l, xs, vec if l == 0 else None, segs
        )
        own = exchange_lo({s: heads_by[j] for j, s in enumerate(slots)}, xs, -1)
        own = tie([own[s] for s in slots], ffn_work.step(heads_by))
        if l + 1 == layers:
            own = tie(own, grad_own)
        middle, normed_two = out_project(me, own, w_out, vec, l, stream, xs)
        by = gather_lo(normed_two, xs)
        all_two = [by[s] for s in slots]
        near, far = all_two[:CORES], all_two[CORES:]
        if l == 0:
            near = tie(near, ffn_work.step(middle))
        while ffn_work.step() is not None and (hs - 1, ts - 1) not in ffn_out:
            pass
        ffn_pieces = pieces_of(ffn_out, hs, ts)
        if more:
            next_attn, next_ffn = {}, {}
            attn_work = Work(fetch(tie(packed[2 * l + 1], ffn_out[0, ts - 1]), next_attn, hs, ts))
        w_up, w_down = place_ffn(me, ffn_pieces, hs, ts, xs)
        hid_a, gel_a, part_a = ffn_fwd(near, w_up, up_vec, l, w_down, [F32] + [BF] * (CORES - 1))
        far = tie(far, part_a)
        if more:
            far = tie(far, attn_work.step(part_a))
        else:
            grad_by = gather_lo(tie(grad_own, all_two), xs)
        hid_b, gel_b, part_b = ffn_fwd(far, w_up, up_vec, l, w_down, [BF] * len(far))
        terms = scatter_lo(dict(zip(slots, part_a + part_b)), xs)
        stored.append((stream, all_one, qkv, out_t, lse, own, middle, all_two, hid_a + hid_b, gel_a + gel_b))
        weights.append((w_qkv, w_out, w_up, w_down))
        if more:
            terms = tie(terms, attn_work.step(part_b))
            ffn_work = Work(fetch(tie(packed[2 * l + 2], part_b), next_ffn, hs, ts))
            stream, normed = layer_end(terms, middle, vec, l, False)
            by = gather_lo(normed, xs)
            given = [by[s] for s in slots]
            given = tie(given, attn_work.step(normed), ffn_work.step(normed))
            while (hs - 1, ts - 1) not in next_attn:
                attn_work.step()
            w_qkv, out_near = place_attn(me, pieces_of(next_attn, hs, ts), rows, hs, ts, xs, True)
            attn_out, ffn_out = next_attn, next_ffn
        else:
            (final,) = layer_end(terms, middle, vec, l, True)
    result = turned(final)

    dh, dz = grad_own, grad_own
    down_sum = jnp.sum(grad_own.astype(F32), axis=0, keepdims=True)
    mine_sums, shared_sums = [None] * layers, [None] * layers
    q_grads, u_grads, d_grads, o_grads = [[None] * layers for _ in range(4)]

    def send_cols(terms, at=slice(None)):
        blocks = {s: total_of(terms, (j, slice(None), at)).astype(BF) for j, s in enumerate(slots)}
        return exchange_lo(blocks, xs, 1)

    def unfolded(terms, at=slice(None), count=D // cols):
        total = total_of(terms, (slice(None), slice(None), at))
        total = total.reshape(count, -1, total.shape[-1])
        return jnp.concatenate([total[p] for p in range(count)], 1)

    def marker(parts):
        return parts[-1][0, 0, :8, :128]

    class Sums:
        def __init__(self, parts, *after):
            self.terms = []
            if after:
                parts = parts[:1] + list(tie(parts[1:], after))
            self.work = Work(reduce(parts, self.terms, hs, ts))
            self.step = self.work.step

        def finish(self, *after):
            while len(self.terms) < ts:
                self.step(*after)
            return self.terms

    late = None
    for l in reversed(range(layers)):
        w_qkv, w_out, w_up, w_down = weights[l]
        stream, all_one, qkv, out_t, lse, own, middle, all_two, hidden, gel = stored[l]
        first_layer = l == 0
        by = grad_by if late is None else gather_lo(dz, xs)
        all_dz = [by[s] for s in slots]
        near, far = all_dz[:CORES], all_dz[CORES:]
        if late:
            near = tie(near, late["d"].step(dz), late["u"].step(dz))
            late["a"] = Sums(late["a_parts"], near)
        else:
            near = tie(near, final)
        du_a, part_a = ffn_bwd(near, gel[:CORES], w_up, w_down, [F32] + [BF] * (CORES - 1))
        far = tie(far, part_a)
        if late:
            far = tie(far, late["d"].step(part_a))
        du_b, part_b = ffn_bwd(far, gel[CORES:], w_up, w_down, [BF] * (ts - CORES))
        all_du = du_a + du_b
        terms = scatter_lo(dict(zip(slots, part_a + part_b)), xs)
        d_parts = wgrad_down(me, hidden, tie(all_dz, part_b), hs)
        d_sums = Sums(d_parts)
        up_sum, u_parts = wgrad_cols(me, all_two, tie(all_du, marker(d_parts)), hs, xs)
        terms = tie(terms, up_sum)
        if late:
            terms = tie(terms, late["u"].step(part_b), late["a"].step(up_sum))
        dh1, dy, mid_sums, d_heads = mid_back(me, terms, dh, middle, vec, l, w_out, ts, xs)
        by = exchange_lo(dict(zip(slots, d_heads)), xs, 1)
        d_out = [by[s] for s in slots]
        out_part = wgrad_out(me, own, dy, hs, xs)
        got = shift(out_part[1], CORE, CORES, 1)
        both = [(out_part[0, k].astype(F32) + got[k].astype(F32)) for k in range(xs)]
        o_sent = [both[k].astype(BF) for k in range(1, xs)]
        o_got = [shift(o_sent[k - 1], XX, xs, k) for k in range(1, xs)]
        d_out = tie(d_out, o_sent)
        if late:
            d_out = tie(d_out, late["u"].step(dy), late["a"].step(dy))
        else:
            d_out = tie(d_out, d_sums.step(dy))
            u_sums = Sums(u_parts, d_out)
        dqkv, parts = attn_bwd(me, slopes, d_out, qkv, out_t, lse, w_qkv, *segs, xs)
        o_near = both[0]
        for g in tie(o_got, dqkv):
            o_near = o_near + g.astype(F32)
        o_near = o_near.astype(BF)
        terms = scatter_lo(dict(zip(slots, tie(parts, o_near))), xs)
        qkv_sum, a_parts = wgrad_cols(me, all_one, dqkv, hs, xs, o_near)
        terms = tie(terms, qkv_sum, d_sums.step(dqkv))
        if late:
            u_sums = Sums(u_parts, qkv_sum)
        dh, dz, start_sums = start_back(terms, dh1, stream, vec, l)
        mine_sums[l] = jnp.concatenate([down_sum, mid_sums, start_sums[:2]], 0)
        third = wide // 3
        shared_sums[l] = (up_sum, qkv_sum[:, :third], qkv_sum[:, 2 * third :])
        down_sum = start_sums[2:3]
        if not first_layer:
            late = dict(d=d_sums, u=u_sums, a_parts=a_parts)
    u_sums.step(dz)
    a_sums = Sums(a_parts, u_sums.terms)
    late["a"].step(dz)
    d_sums.finish(dz)
    d_grads[0] = unfolded(d_sums.terms)
    a_sums.step()
    u_grads[0] = send_cols(u_sums.finish())
    d_grads[1] = unfolded(late["d"].finish(dz))
    u_grads[1] = send_cols(late["u"].finish(dz))
    q_grads[1] = send_cols(late["a"].finish(dz), slice(0, wide))
    o_grads[1] = unfolded(late["a"].terms, slice(wide, None), ts)
    a_sums.finish()
    q_grads[0] = send_cols(a_sums.terms, slice(0, wide))
    o_grads[0] = unfolded(a_sums.terms, slice(wide, None), ts)
    input_grad = turned(dz)

    full = max(D, shared_sums[0][0].shape[1])
    pad = lambda x: jnp.pad(x, ((0, 0), (0, full - x.shape[1])))
    both = []
    for l in range(layers):
        up_sum, q_sum, v_sum = shared_sums[l]
        both += [pad(up_sum), pad(jnp.concatenate([q_sum, v_sum], 1))]
    sums = sum_small(jnp.concatenate(mine_sums, 0), jnp.concatenate(both, 0), hs, ts, xs)
    device = (hi * ts + lo) * ts + blk
    vectors = lax.dynamic_slice(sums[: 6 * layers, :D], (0, device * each), (6 * layers, each))
    vectors = vectors.reshape(layers, 6, each)
    shared = sums[6 * layers :].reshape(layers, 2, full)
    up_each, qv_each = up_bias.shape[1], qv_bias.shape[1]
    up_grad = lax.dynamic_slice(shared[:, 0], (0, (hi * ts + blk) * up_each), (layers, up_each))
    qv_grad = lax.dynamic_slice(shared[:, 1], (0, (hi * ts + blk) * qv_each), (layers, qv_each))
    q_grad, u_grad = join(me, list(zip(q_grads, u_grads)), ts, xs)
    return (
        result[None],
        input_grad[None],
        q_grad,
        qv_grad,
        jnp.stack(o_grads),
        vectors[:, 3],
        u_grad,
        up_grad,
        jnp.stack(d_grads),
        vectors[:, 0],
        jnp.stack([vectors[:, 4], vectors[:, 1]], 1),
        jnp.stack([vectors[:, 5], vectors[:, 2]], 1),
    )


def solution(mesh):
    ts = mesh.shape["blk"]
    hs = mesh.shape["rows"] // ts
    xs = ts // CORES
    fine = Mesh(mesh.devices.reshape(hs, xs, CORES, ts), (HI, XX, CORE, BLK))
    rows, every = (HI, XX, CORE), (HI, XX, CORE, BLK)
    row_cut = P(None, every, None)
    vec_cut = P(None, every)
    norm_cut = P(None, None, every)
    cuts = (row_cut, vec_cut, row_cut, vec_cut, row_cut, vec_cut, row_cut, vec_cut, norm_cut, norm_cut)
    acts = P(rows, BLK, None)
    return jax.shard_map(
        functools.partial(on_device, hs, ts, xs),
        mesh=fine,
        in_specs=(acts, P(rows, BLK), acts) + cuts,
        out_specs=(acts, acts) + cuts,
        check_vma=False,
    )
```

time: 722 us -> 624 us (0.86)
  starting transfers between devices: 234 us -> 143 us
  waiting for transfers between devices: 248 us -> 298 us
  local copies, waits for them, and re-layouts: 65.4 us -> 37.9 us
  Pallas kernels: 127 us -> 105 us
  other arithmetic: 37.7 us -> 27.7 us
    ppermute x197 -> x104, starting transfers between devices: 224 us -> 103 us  [shift(): return lax.ppermute(x, axis, [(i, (i + step) % size) for i in range(size)])]
    ppermute x0 -> x30, waiting for transfers between devices: none -> 47.6 us  [send_lo(): return lax.ppermute(x, (XX, CORE), pairs)]
    ppermute x0 -> x30, starting transfers between devices: none -> 31.3 us  [send_lo(): return lax.ppermute(x, (XX, CORE), pairs)]
    pallas_call x39 -> x40, Pallas kernels: 127 us -> 104 us  [run(): pl.pallas_call(kernel, out_shape=tuple(outs), in_specs=[pl.BlockSpec(memo...]
    unnamed x355 -> x244, local copies, waits for them, and re-layouts: 43.6 us -> 35 us
    ppermute x197 -> x104, waiting for transfers between devices: 248 us -> 251 us  [shift(): return lax.ppermute(x, axis, [(i, (i + step) % size) for i in range(size)])]
  transfers between devices with their start and end apart: 202 -> 138, of which waited for: 68 -> 63; matrix products, arithmetic and copies ran while one was open for 9% -> 5% of each run, Pallas kernels for 18% -> 14%
where the time goes in v2:
time: 624 us; the launch traced here: 614 us
  waiting for transfers between devices  298 us (48%)
  starting transfers between devices  143 us (23%)
  Pallas kernels  105 us (17%)
  local copies, waits for them, and re-layouts  37.9 us (6%)
  other arithmetic  27.7 us (4%)
    ppermute x104, waiting for transfers between devices, shift(): return lax.ppermute(x, axis, [(i, (i + step) % size) for i in range(size)])  251 us
    pallas_call x40, Pallas kernels, run(): pl.pallas_call(kernel, out_shape=tuple(outs), in_specs=[pl.BlockSpec(memo...  104 us
    ppermute x104, starting transfers between devices, shift(): return lax.ppermute(x, axis, [(i, (i + step) % size) for i in range(size)])  103 us
    ppermute x30, waiting for transfers between devices, send_lo(): return lax.ppermute(x, (XX, CORE), pairs)  47.6 us
    unnamed x244, local copies, waits for them, and re-layouts  35 us
    ppermute x30, starting transfers between devices, send_lo(): return lax.ppermute(x, (XX, CORE), pairs)  31.3 us
  transfers between devices with their start and end apart: 138, of which 63 were waited for; matrix products, arithmetic and copies ran while one was open for 5% of the time, Pallas kernels for 14%

profile of v2, /device:TPU:0, one launch (start us, length us, event | category | flops | bytes accessed | tf_op | source)
XLA Modules:
  0.0 613.9 jit_solution(7317471212588417088)
XLA Ops:
  24.1 3.6 collective-permute-done.13.refs_1_
  28.2 7.2 %collective-permute-done.14.refs_5_ = bf16[144,1024]{1,0:T(8,128)(2,1)S(1)} collective-permute-done((bf16[144,1024]{1,0:T(8,128)(2,1)S(1)}, bf16[144,1024]{1,0:T(8,128)(2,1)S(1)}, u32[]{:S(2)}, u32[]{:S(2)}) %collective-permute-start.14) | collective-permute-done | bytes 294944 | tf_op jit(solution)/shard_map/ppermute | solution.py:77
  35.4 10.4 %collective-permute-done.15.refs_2_ = bf16[144,1024]{1,0:T(8,128)(2,1)S(1)} collective-permute-done((bf16[144,1024]{1,0:T(8,128)(2,1)S(1)}, bf16[144,1024]{1,0:T(8,128)(2,1)S(1)}, u32[]{:S(2)}, u32[]{:S(2)}) %collective-permute-start.15) | collective-permute-done | bytes 294944 | tf_op jit(solution)/shard_map/ppermute | solution.py:77
  46.2 13.2 %collective-permute-start.5 = (bf16[272,1024]{1,0:T(8,128)(2,1)S(1)}, bf16[272,1024]{1,0:T(8,128)(2,1)}, u32[]{:S(2)}, u32[]{:S(2)}) collective-permute-start(bf16[272,1024]{1,0:T(8,128)(2,1)S(1)} %collective-permute-done.3.refs_0_.refs_6_.refs_4_), channel_id=1, source_target_pairs={{0,8},{8,0},{1,9},{9,1},{2,10},{10,2},{3,11},{11,3},{4,12},{12,4},... | collective-permute-start | bytes 1671176 | tf_op jit(solution)/shard_map/ppermute | solution.py:77
  62.5 10.2 %collective-permute-done.8.refs_2_ = bf16[32,2816]{1,0:T(8,128)(2,1)S(1)} collective-permute-done((bf16[32,2816]{1,0:T(8,128)(2,1)S(1)}, bf16[32,2816]{1,0:T(8,128)(2,1)S(1)}, u32[]{:S(2)}, u32[]{:S(2)}) %collective-permute-start.8) | collective-permute-done | bytes 180256 | tf_op jit(solution)/shard_map/ppermute | solution.py:106
  80.3 8.9 %collective-permute-done.10.refs_4_ = bf16[128,2048]{1,0:T(8,128)(2,1)S(1)} collective-permute-done((bf16[128,2048]{1,0:T(8,128)(2,1)S(1)}, bf16[128,2048]{1,0:T(8,128)(2,1)S(1)}, u32[]{:S(2)}, u32[]{:S(2)}) %collective-permute-start.10) | collective-permute-done | bytes 524320 | tf_op jit(solution)/shard_map/ppermute | solution.py:77
  94.7 8.6 %shard_map.227 = (bf16[1024,768]{1,0:T(8,128)(2,1)S(1)}, f32[256,1024]{1,0:T(8,128)S(1)}, f32[2,1024]{1,0:T(2,128)S(1)}, f32[1,1024]{1,0:T(1,128)S(1)}, f32[1024...) custom-call(s32[4]{0:T(128)S(1)} %pad_add_fusion.me, ...), custom_call_target="tpu_custom_call" | custom-call | flops 2415919104 | bytes 9635840 | tf_op jit(solution)/shard_map/pallas_call | solution.py:44
  113.1 5.6 collective-permute-done.21.refs_3_
  126.3 9.2 %collective-permute-done.31.refs_0_.refs_2_ = bf16[256,1024]{1,0:T(8,128)(2,1)S(1)} collective-permute-done((bf16[256,1024]{1,0:T(8,128)(2,1)S(1)}, bf16[256,1024]{1,0:T(8,128)(2,1)S(1)}, u32[]{:S(2)}, u32[]{:S(2)}) %collective-permute-start.31) | collective-permute-done | bytes 524320 | tf_op jit(solution)/shard_map/ppermute | solution.py:77
  140.2 3.7 shard_map.231
  147.4 3.7 shard_map.232
  155.9 7.1 %collective-permute-done.38.refs_5_ = bf16[128,1024]{1,0:T(8,128)(2,1)S(1)} collective-permute-done((bf16[128,1024]{1,0:T(8,128)(2,1)S(1)}, bf16[128,1024]{1,0:T(8,128)(2,1)S(1)}, u32[]{:S(2)}, u32[]{:S(2)}) %collective-permute-start.38) | collective-permute-done | bytes 262176 | tf_op jit(solution)/shard_map/ppermute | solution.py:77
  168.5 10.2 %collective-permute-done.43.refs_6_ = bf16[128,1024]{1,0:T(8,128)(2,1)S(1)} collective-permute-done((bf16[128,1024]{1,0:T(8,128)(2,1)S(1)}, bf16[128,1024]{1,0:T(8,128)(2,1)S(1)}, u32[]{:S(2)}, u32[]{:S(2)}) %collective-permute-start.43) | collective-permute-done | bytes 262176 | tf_op jit(solution)/shard_map/ppermute | solution.py:77
  178.7 3.4 collective-permute-done.44.refs_3_
  184.1 7.2 %collective-permute-done.49.refs_7_ = bf16[128,1024]{1,0:T(8,128)(2,1)S(1)} collective-permute-done((bf16[128,1024]{1,0:T(8,128)(2,1)S(1)}, bf16[128,1024]{1,0:T(8,128)(2,1)S(1)}, u32[]{:S(2)}, u32[]{:S(2)}) %collective-permute-start.49) | collective-permute-done | bytes 262176 | tf_op jit(solution)/shard_map/ppermute | solution.py:77
  193.7 6.1 collective-permute-done.47.refs_5_
  202.7 6.9 %shard_map.235 = (bf16[1024,768]{1,0:T(8,128)(2,1)S(1)}, f32[256,1024]{1,0:T(8,128)S(1)}, f32[2,1024]{1,0:T(2,128)S(1)}, bf16[256,256]{1,0:T(8,128)(2,1)S(1)}, b...) custom-call(s32[4]{0:T(128)S(1)} %pad_add_fusion.me, ...), custom_call_target="tpu_custom_call" | custom-call | flops 2415919104 | bytes 7358464 | tf_op jit(solution)/shard_map/pallas_call | solution.py:44
  218.4 12.2 %collective-permute-done.51.refs_2_ = bf16[256,256]{1,0:T(8,128)(2,1)S(1)} collective-permute-done((bf16[256,256]{1,0:T(8,128)(2,1)S(1)}, bf16[256,256]{1,0:T(8,128)(2,1)S(1)}, u32[]{:S(2)}, u32[]{:S(2)}) %collective-permute-start.51) | collective-permute-done | bytes 131104 | tf_op jit(solution)/shard_map/ppermute | solution.py:106
  238.2 11.5 %collective-permute-done.61.refs_0_.refs_2_ = bf16[256,1024]{1,0:T(8,128)(2,1)S(1)} collective-permute-done((bf16[256,1024]{1,0:T(8,128)(2,1)S(1)}, bf16[256,1024]{1,0:T(8,128)(2,1)S(1)}, u32[]{:S(2)}, u32[]{:S(2)}) %collective-permute-start.61) | collective-permute-done | bytes 524320 | tf_op jit(solution)/shard_map/ppermute | solution.py:77
  252.0 3.7 shard_map.239
  255.7 3.8 shard_map.240
  263.0 12.1 %collective-permute-done.68.refs_0_.refs_6_ = bf16[256,1024]{1,0:T(8,128)(2,1)S(1)} collective-permute-done((bf16[256,1024]{1,0:T(8,128)(2,1)S(1)}, bf16[256,1024]{1,0:T(8,128)(2,1)S(1)}, u32[]{:S(2)}, u32[]{:S(2)}) %collective-permute-start.68) | collective-permute-done | bytes 524320 | tf_op jit(solution)/shard_map/ppermute | solution.py:77
  275.1 10.8 %collective-permute-done.64.refs_1_ = bf16[256,1024]{1,0:T(8,128)(2,1)S(1)} collective-permute-done((bf16[256,1024]{1,0:T(8,128)(2,1)S(1)}, bf16[256,1024]{1,0:T(8,128)(2,1)S(1)}, u32[]{:S(2)}, u32[]{:S(2)}) %collective-permute-start.64) | collective-permute-done | bytes 524320 | tf_op jit(solution)/shard_map/ppermute | solution.py:77
  300.1 3.3 shard_map.244
  303.4 5.4 collective-permute-done.71.refs_1_
  313.0 11.2 %collective-permute-done.77 = bf16[4,4,32,1024]{3,2,1,0:T(8,128)(2,1)S(1)} collective-permute-done((bf16[4,4,32,1024]{3,2,1,0:T(8,128)(2,1)S(1)}, bf16[4,4,32,1024]{3,2,1,0:T(8,128)(2,1)S(1)}, u32[]{:S(2)}, u32[]{:S(2)}) %collective-permute-start.77) | collective-permute-done | bytes 1048608 | tf_op jit(solution)/shard_map/ppermute | solution.py:77
  332.5 7.9 %shard_map.248 = (bf16[256,768]{1,0:T(8,128)(2,1)S(1)}, bf16[256,768]{1,0:T(8,128)(2,1)S(1)}, bf16[256,768]{1,0:T(8,128)(2,1)S(1)}, bf16[256,768]{1,0:T(8,128)(2...) custom-call(s32[4]{0:T(128)S(1)} %pad_add_fusion.me, ...), custom_call_target="tpu_custom_call" | custom-call | flops 3221225472 | bytes 9449472 | tf_op jit(solution)/shard_map/pallas_call | solution.py:44
  340.5 3.7 collective-permute-done.78
  352.0 8.6 %collective-permute-done.80.refs_1_ = bf16[256,1024]{1,0:T(8,128)(2,1)S(1)} collective-permute-done((bf16[256,1024]{1,0:T(8,128)(2,1)S(1)}, bf16[256,1024]{1,0:T(8,128)(2,1)S(1)}, u32[]{:S(2)}, u32[]{:S(2)}) %collective-permute-start.80) | collective-permute-done | bytes 524320 | tf_op jit(solution)/shard_map/ppermute | solution.py:77
  363.6 9.7 %collective-permute-done.83 = bf16[4,4,32,1024]{3,2,1,0:T(8,128)(2,1)S(1)} collective-permute-done((bf16[4,4,32,1024]{3,2,1,0:T(8,128)(2,1)S(1)}, bf16[4,4,32,1024]{3,2,1,0:T(8,128)(2,1)S(1)}, u32[]{:S(2)}, u32[]{:S(2)}) %collective-permute-start.83) | collective-permute-done | bytes 1048608 | tf_op jit(solution)/shard_map/ppermute | solution.py:77
  386.1 3.7 shard_map.253
  389.8 12.2 %collective-permute-done.90 = bf16[4,4,32,1024]{3,2,1,0:T(8,128)(2,1)S(1)} collective-permute-done((bf16[4,4,32,1024]{3,2,1,0:T(8,128)(2,1)S(1)}, bf16[4,4,32,1024]{3,2,1,0:T(8,128)(2,1)S(1)}, u32[]{:S(2)}, u32[]{:S(2)}) %collective-permute-start.90) | collective-permute-done | bytes 1048608 | tf_op jit(solution)/shard_map/ppermute | solution.py:77
  411.6 3.9 shard_map.258
  417.4 5.4 collective-permute-start.66
  422.8 8.7 %shard_map.256 = (bf16[256,768]{1,0:T(8,128)(2,1)S(1)}, bf16[256,768]{1,0:T(8,128)(2,1)S(1)}, bf16[256,768]{1,0:T(8,128)(2,1)S(1)}, bf16[256,768]{1,0:T(8,128)(2...) custom-call(s32[4]{0:T(128)S(1)} %pad_add_fusion.me, ...), custom_call_target="tpu_custom_call" | custom-call | flops 3221225472 | bytes 9449472 | tf_op jit(solution)/shard_map/pallas_call | solution.py:44
  436.8 8.3 %collective-permute-start.118 = (bf16[4,32,1024]{2,1,0:T(8,128)(2,1)}, bf16[4,32,1024]{2,1,0:T(8,128)(2,1)S(1)}, u32[]{:S(2)}, u32[]{:S(2)}) collective-permute-start(bf16[4,32,1024]{2,1,0:T(8,128)(2,1)} %get-tuple-element.611), channel_id=1, source_target_pairs={{0,1},{1,2},{2,3},{3,0},{4,5},{5,6},{6,7},{7,4},{8,9},{9,10},{10,1... | collective-permute-start | bytes 786440 | tf_op jit(solution)/shard_map/ppermute | solution.py:77
  445.0 4.5 collective-permute-start.119
  449.5 16.3 %collective-permute-done.137 = bf16[4,32,1024]{2,1,0:T(8,128)(2,1)S(1)} collective-permute-done((bf16[4,32,1024]{2,1,0:T(8,128)(2,1)}, bf16[4,32,1024]{2,1,0:T(8,128)(2,1)S(1)}, u32[]{:S(2)}, u32[]{:S(2)}) %collective-permute-start.137) | collective-permute-done | bytes 262176 | tf_op jit(solution)/shard_map/ppermute | solution.py:77
  475.1 3.6 shard_map.257
  482.9 4.3 collective-permute-start.134
  489.3 4.5 collective-permute-done.133
  494.6 15.6 %collective-permute-done.134 = bf16[4,32,1024]{2,1,0:T(8,128)(2,1)S(1)} collective-permute-done((bf16[4,32,1024]{2,1,0:T(8,128)(2,1)S(1)}, bf16[4,32,1024]{2,1,0:T(8,128)(2,1)S(1)}, u32[]{:S(2)}, u32[]{:S(2)}) %collective-permute-start.134) | collective-permute-done | bytes 262176 | tf_op jit(solution)/shard_map/ppermute | solution.py:77
  514.5 12.5 %collective-permute-done.135 = bf16[4,32,1024]{2,1,0:T(8,128)(2,1)S(1)} collective-permute-done((bf16[4,32,1024]{2,1,0:T(8,128)(2,1)S(1)}, bf16[4,32,1024]{2,1,0:T(8,128)(2,1)S(1)}, u32[]{:S(2)}, u32[]{:S(2)}) %collective-permute-start.135) | collective-permute-done | bytes 262176 | tf_op jit(solution)/shard_map/ppermute | solution.py:77
  550.4 6.9 %collective-permute-start.130 = (f32[16,1024]{1,0:T(8,128)S(1)}, f32[16,1024]{1,0:T(8,128)S(1)}, u32[]{:S(2)}, u32[]{:S(2)}) collective-permute-start(f32[16,1024]{1,0:T(8,128)S(1)} %add.566), channel_id=1, source_target_pairs={{0,1},{1,2},{2,3},{3,0},{4,5},{5,6},{6,7},{7,4},{8,9},{9,10},{10,1... | collective-permute-start | bytes 196616 | tf_op jit(solution)/shard_map/ppermute | solution.py:77
  562.8 4.2 collective-permute-done.131
  571.3 3.9 collective-permute-start.108
  578.2 6.6 %collective-permute-done.107 = bf16[4,32,1024]{2,1,0:T(8,128)(2,1)S(1)} collective-permute-done((bf16[4,32,1024]{2,1,0:T(8,128)(2,1)}, bf16[4,32,1024]{2,1,0:T(8,128)(2,1)S(1)}, u32[]{:S(2)}, u32[]{:S(2)}) %collective-permute-start.107) | collective-permute-done | bytes 262176 | tf_op jit(solution)/shard_map/ppermute | solution.py:77
  584.8 7.2 %collective-permute-start.123 = (bf16[32,768]{1,0:T(8,128)(2,1)}, bf16[32,768]{1,0:T(8,128)(2,1)S(1)}, u32[]{:S(2)}, u32[]{:S(2)}) collective-permute-start(bf16[32,768]{1,0:T(8,128)(2,1)} %get-tuple-element.635), channel_id=1, source_target_pairs={{0,8},{4,12},{8,0},{12,4},{1,9},{5,13},{9,1},{13,5},{2,10},{6,14},... | collective-permute-start | bytes 147464 | tf_op jit(solution)/shard_map/ppermute | solution.py:106
  (569 shorter events, 250.0 us)
Async XLA Ops:
  20.1 26.1 %collective-permute-start.3 = (bf16[272,1024]{1,0:T(8,128)(2,1)S(1)}, bf16[272,1024]{1,0:T(8,128)(2,1)S(1)}, u32[]{:S(2)}, u32[]{:S(2)}) collective-permute-start(bf16[272,1024]{1,0:T(8,128)(2,1)S(1)} %shard_map.220), channel_id=1, source_target_pairs={{0,0},{1,8},{2,4},{3,12},{8,1},{9,9},{10,5},{11,13},{4,2},{5,10},{... | collective-permute-start | bytes 1671176 | tf_op jit(solution)/shard_map/ppermute | solution.py:975
  28.2 17.6 %collective-permute-start.15 = (bf16[144,1024]{1,0:T(8,128)(2,1)S(1)}, bf16[144,1024]{1,0:T(8,128)(2,1)S(1)}, u32[]{:S(2)}, u32[]{:S(2)}) collective-permute-start(bf16[144,1024]{1,0:T(8,128)(2,1)S(1)} %collective-permute-done.13.refs_1_), channel_id=1, source_target_pairs={{0,1},{1,2},{2,3},{3,0},{4,5},{5,6},{6,7},{7,4},{8,9},{9,10},{10,1... | collective-permute-start | bytes 884744 | tf_op jit(solution)/shard_map/ppermute | solution.py:77
  46.2 34.0 %collective-permute-start.5 = (bf16[272,1024]{1,0:T(8,128)(2,1)S(1)}, bf16[272,1024]{1,0:T(8,128)(2,1)}, u32[]{:S(2)}, u32[]{:S(2)}) collective-permute-start(bf16[272,1024]{1,0:T(8,128)(2,1)S(1)} %collective-permute-done.3.refs_0_.refs_6_.refs_4_), channel_id=1, source_target_pairs={{0,8},{8,0},{1,9},{9,1},{2,10},{10,2},{3,11},{11,3},{4,12},{12,4},... | collective-permute-start | bytes 1671176 | tf_op jit(solution)/shard_map/ppermute | solution.py:77
  75.6 17.2 %collective-permute-start.4 = (bf16[272,1024]{1,0:T(8,128)(2,1)S(1)}, bf16[272,1024]{1,0:T(8,128)(2,1)}, u32[]{:S(2)}, u32[]{:S(2)}) collective-permute-start(bf16[272,1024]{1,0:T(8,128)(2,1)S(1)} %collective-permute-done.3.refs_0_.refs_6_.refs_4_), channel_id=1, source_target_pairs={{0,4},{4,0},{1,5},{5,1},{2,6},{6,2},{3,7},{7,3},{8,12},{12,8},{9,1... | collective-permute-start | bytes 1671176 | tf_op jit(solution)/shard_map/ppermute | solution.py:77
  91.3 15.9 %collective-permute-start.22 = (bf16[128,2048]{1,0:T(8,128)(2,1)}, bf16[128,2048]{1,0:T(8,128)(2,1)}, u32[]{:S(2)}, u32[]{:S(2)}) collective-permute-start(bf16[128,2048]{1,0:T(8,128)(2,1)} %collective-permute-done.11.refs_1_), channel_id=1, source_target_pairs={{0,16},{16,0},{1,17},{17,1},{2,18},{18,2},{3,19},{19,3},{4,20},{20... | collective-permute-start | bytes 1572872 | tf_op jit(solution)/shard_map/ppermute | solution.py:77
  92.8 25.9 %collective-permute-start.24 = (bf16[2,4,32,1024]{3,2,1,0:T(8,128)(2,1)}, bf16[2,4,32,1024]{3,2,1,0:T(8,128)(2,1)S(1)}, u32[]{:S(2)}, u32[]{:S(2)}) collective-permute-start(bf16[2,4,32,1024]{3,2,1,0:T(8,128)(2,1)} %get-tuple-element.346.refs_0_), channel_id=1, source_target_pairs={{0,4},{4,0},{1,5},{5,1},{2,6},{6,2},{3,7},{7,3},{8,12},{12,8},{9,1... | collective-permute-start | bytes 1572872 | tf_op jit(solution)/shard_map/ppermute | solution.py:77
  93.0 25.7 %collective-permute-start.26 = (bf16[2,4,32,1024]{3,2,1,0:T(8,128)(2,1)}, bf16[2,4,32,1024]{3,2,1,0:T(8,128)(2,1)S(1)}, u32[]{:S(2)}, u32[]{:S(2)}) collective-permute-start(bf16[2,4,32,1024]{3,2,1,0:T(8,128)(2,1)} %collective-permute-done.25.refs_2_), channel_id=1, source_target_pairs={{0,4},{4,0},{1,5},{5,1},{2,6},{6,2},{3,7},{7,3},{8,12},{12,8},{9,1... | collective-permute-start | bytes 1572872 | tf_op jit(solution)/shard_map/ppermute | solution.py:77
  155.1 28.1 %collective-permute-start.45 = (bf16[128,2048]{1,0:T(8,128)(2,1)S(1)}, bf16[128,2048]{1,0:T(8,128)(2,1)S(1)}, u32[]{:S(2)}, u32[]{:S(2)}) collective-permute-start(bf16[128,2048]{1,0:T(8,128)(2,1)S(1)} %get-tuple-element.377.refs_0_), channel_id=1, source_target_pairs={{0,16},{16,0},{1,17},{17,1},{2,18},{18,2},{3,19},{19,3},{4,20},{20... | collective-permute-start | bytes 1572872 | tf_op jit(solution)/shard_map/ppermute | solution.py:77
  163.0 20.3 %collective-permute-start.46 = (bf16[128,2048]{1,0:T(8,128)(2,1)S(1)}, bf16[128,2048]{1,0:T(8,128)(2,1)S(1)}, u32[]{:S(2)}, u32[]{:S(2)}) collective-permute-start(bf16[128,2048]{1,0:T(8,128)(2,1)S(1)} %get-tuple-element.377.refs_0_), channel_id=1, source_target_pairs={{0,1},{1,2},{2,3},{3,0},{4,5},{5,6},{6,7},{7,4},{8,9},{9,10},{10,1... | collective-permute-start | bytes 1572872 | tf_op jit(solution)/shard_map/ppermute | solution.py:77
  165.4 16.7 %collective-permute-start.44 = (bf16[128,1024]{1,0:T(8,128)(2,1)S(1)}, bf16[128,1024]{1,0:T(8,128)(2,1)S(1)}, u32[]{:S(2)}, u32[]{:S(2)}) collective-permute-start(bf16[128,1024]{1,0:T(8,128)(2,1)S(1)} %collective-permute-done.39.refs_2_), channel_id=1, source_target_pairs={{0,1},{1,2},{2,3},{3,0},{4,5},{5,6},{6,7},{7,4},{8,9},{9,10},{10,1... | collective-permute-start | bytes 786440 | tf_op jit(solution)/shard_map/ppermute | solution.py:77
  167.9 25.8 %collective-permute-start.41 = (bf16[256,1024]{1,0:T(8,128)(2,1)S(1)}, bf16[256,1024]{1,0:T(8,128)(2,1)S(1)}, u32[]{:S(2)}, u32[]{:S(2)}) collective-permute-start(bf16[256,1024]{1,0:T(8,128)(2,1)S(1)} %get-tuple-element.389.refs_0_), channel_id=1, source_target_pairs={{0,8},{8,0},{1,9},{9,1},{2,10},{10,2},{3,11},{11,3},{4,12},{12,4},... | collective-permute-start | bytes 1572872 | tf_op jit(solution)/shard_map/ppermute | solution.py:77
  183.3 16.5 %collective-permute-start.47 = (bf16[128,2048]{1,0:T(8,128)(2,1)S(1)}, bf16[128,2048]{1,0:T(8,128)(2,1)S(1)}, u32[]{:S(2)}, u32[]{:S(2)}) collective-permute-start(bf16[128,2048]{1,0:T(8,128)(2,1)S(1)} %collective-permute-done.46.refs_1_), channel_id=1, source_target_pairs={{0,16},{16,0},{1,17},{17,1},{2,18},{18,2},{3,19},{19,3},{4,20},{20... | collective-permute-start | bytes 1572872 | tf_op jit(solution)/shard_map/ppermute | solution.py:77
  184.1 16.8 %collective-permute-start.40 = (bf16[256,1024]{1,0:T(8,128)(2,1)S(1)}, bf16[256,1024]{1,0:T(8,128)(2,1)S(1)}, u32[]{:S(2)}, u32[]{:S(2)}) collective-permute-start(bf16[256,1024]{1,0:T(8,128)(2,1)S(1)} %get-tuple-element.389.refs_0_), channel_id=1, source_target_pairs={{0,4},{4,0},{1,5},{5,1},{2,6},{6,2},{3,7},{7,3},{8,12},{12,8},{9,1... | collective-permute-start | bytes 1572872 | tf_op jit(solution)/shard_map/ppermute | solution.py:77
  201.0 32.0 %collective-permute-start.56 = (bf16[2,4,32,1024]{3,2,1,0:T(8,128)(2,1)S(1)}, bf16[2,4,32,1024]{3,2,1,0:T(8,128)(2,1)S(1)}, u32[]{:S(2)}, u32[]{:S(2)}) collective-permute-start(bf16[2,4,32,1024]{3,2,1,0:T(8,128)(2,1)S(1)} %get-tuple-element.409.refs_0_), channel_id=1, source_target_pairs={{0,4},{4,0},{1,5},{5,1},{2,6},{6,2},{3,7},{7,3},{8,12},{12,8},{9,1... | collective-permute-start | bytes 1572872 | tf_op jit(solution)/shard_map/ppermute | solution.py:77
  201.3 31.6 %collective-permute-start.58 = (bf16[2,4,32,1024]{3,2,1,0:T(8,128)(2,1)S(1)}, bf16[2,4,32,1024]{3,2,1,0:T(8,128)(2,1)S(1)}, u32[]{:S(2)}, u32[]{:S(2)}) collective-permute-start(bf16[2,4,32,1024]{3,2,1,0:T(8,128)(2,1)S(1)} %collective-permute-done.57.refs_2_), channel_id=1, source_target_pairs={{0,4},{4,0},{1,5},{5,1},{2,6},{6,2},{3,7},{7,3},{8,12},{12,8},{9,1... | collective-permute-start | bytes 1572872 | tf_op jit(solution)/shard_map/ppermute | solution.py:77
  201.6 32.1 %collective-permute-start.55 = (bf16[256,1024]{1,0:T(8,128)(2,1)S(1)}, bf16[256,1024]{1,0:T(8,128)(2,1)S(1)}, u32[]{:S(2)}, u32[]{:S(2)}) collective-permute-start(bf16[256,1024]{1,0:T(8,128)(2,1)S(1)} %bitcast.302), channel_id=1, source_target_pairs={{0,0},{1,8},{2,4},{3,12},{8,1},{9,9},{10,5},{11,13},{4,2},{5,10},{... | collective-permute-start | bytes 1572872 | tf_op jit(solution)/shard_map/ppermute | solution.py:975
  262.5 23.5 %collective-permute-start.64 = (bf16[256,1024]{1,0:T(8,128)(2,1)S(1)}, bf16[256,1024]{1,0:T(8,128)(2,1)S(1)}, u32[]{:S(2)}, u32[]{:S(2)}) collective-permute-start(bf16[256,1024]{1,0:T(8,128)(2,1)S(1)} %add_convert_fusion.4), channel_id=1, source_target_pairs={{0,8},{8,0},{1,9},{9,1},{2,10},{10,2},{3,11},{11,3},{4,12},{12,4},... | collective-permute-start | bytes 1572872 | tf_op jit(solution)/shard_map/ppermute | solution.py:77
  263.0 24.0 %collective-permute-start.67 = (bf16[256,1024]{1,0:T(8,128)(2,1)S(1)}, bf16[256,1024]{1,0:T(8,128)(2,1)S(1)}, u32[]{:S(2)}, u32[]{:S(2)}) collective-permute-start(bf16[256,1024]{1,0:T(8,128)(2,1)S(1)} %collective-permute-done.55.refs_0_.refs_3_.refs_4_), channel_id=1, source_target_pairs={{0,4},{4,0},{1,5},{5,1},{2,6},{6,2},{3,7},{7,3},{8,12},{12,8},{9,1... | collective-permute-start | bytes 1572872 | tf_op jit(solution)/shard_map/ppermute | solution.py:77
  299.2 25.0 %collective-permute-start.77 = (bf16[4,4,32,1024]{3,2,1,0:T(8,128)(2,1)S(1)}, bf16[4,4,32,1024]{3,2,1,0:T(8,128)(2,1)S(1)}, u32[]{:S(2)}, u32[]{:S(2)}) collective-permute-start(bf16[4,4,32,1024]{3,2,1,0:T(8,128)(2,1)S(1)} %get-tuple-element.468), channel_id=1, source_target_pairs={{0,16},{16,0},{1,17},{17,1},{2,18},{18,2},{3,19},{19,3},{4,20},{20... | collective-permute-start | bytes 3145736 | tf_op jit(solution)/shard_map/ppermute | solution.py:77
  327.4 16.8 %collective-permute-start.78 = (bf16[2,4,32,1024]{3,2,1,0:T(8,128)(2,1)S(1)}, bf16[2,4,32,1024]{3,2,1,0:T(8,128)(2,1)S(1)}, u32[]{:S(2)}, u32[]{:S(2)}) collective-permute-start(bf16[2,4,32,1024]{3,2,1,0:T(8,128)(2,1)S(1)} %fusion.5), channel_id=1, source_target_pairs={{0,8},{8,0},{1,9},{9,1},{2,10},{10,2},{3,11},{11,3},{4,12},{12,4},... | collective-permute-start | bytes 1572872 | tf_op jit(solution)/shard_map/ppermute | solution.py:77
  348.4 24.9 %collective-permute-start.83 = (bf16[4,4,32,1024]{3,2,1,0:T(8,128)(2,1)S(1)}, bf16[4,4,32,1024]{3,2,1,0:T(8,128)(2,1)S(1)}, u32[]{:S(2)}, u32[]{:S(2)}) collective-permute-start(bf16[4,4,32,1024]{3,2,1,0:T(8,128)(2,1)S(1)} %get-tuple-element.498), channel_id=1, source_target_pairs={{0,16},{16,0},{1,17},{17,1},{2,18},{18,2},{3,19},{19,3},{4,20},{20... | collective-permute-start | bytes 3145736 | tf_op jit(solution)/shard_map/ppermute | solution.py:77
  363.6 16.1 %collective-permute-start.86 = (bf16[4,32,1024]{2,1,0:T(8,128)(2,1)S(1)}, bf16[4,32,1024]{2,1,0:T(8,128)(2,1)S(1)}, u32[]{:S(2)}, u32[]{:S(2)}) collective-permute-start(bf16[4,32,1024]{2,1,0:T(8,128)(2,1)S(1)} %get-tuple-element.627), channel_id=1, source_target_pairs={{0,3},{1,0},{2,1},{3,2},{4,7},{5,4},{6,5},{7,6},{8,11},{9,8},{10,9... | collective-permute-start | bytes 786440 | tf_op jit(solution)/shard_map/ppermute | solution.py:77
  376.4 25.6 %collective-permute-start.90 = (bf16[4,4,32,1024]{3,2,1,0:T(8,128)(2,1)S(1)}, bf16[4,4,32,1024]{3,2,1,0:T(8,128)(2,1)S(1)}, u32[]{:S(2)}, u32[]{:S(2)}) collective-permute-start(bf16[4,4,32,1024]{3,2,1,0:T(8,128)(2,1)S(1)} %get-tuple-element.529), channel_id=1, source_target_pairs={{0,16},{16,0},{1,17},{17,1},{2,18},{18,2},{3,19},{19,3},{4,20},{20... | collective-permute-start | bytes 3145736 | tf_op jit(solution)/shard_map/ppermute | solution.py:77
  382.5 20.8 %collective-permute-start.89 = (bf16[256,1024]{1,0:T(8,128)(2,1)S(1)}, bf16[256,1024]{1,0:T(8,128)(2,1)S(1)}, u32[]{:S(2)}, u32[]{:S(2)}) collective-permute-start(bf16[256,1024]{1,0:T(8,128)(2,1)S(1)} %get-tuple-element.505), channel_id=1, source_target_pairs={{0,4},{4,0},{1,5},{5,1},{2,6},{6,2},{3,7},{7,3},{8,12},{12,8},{9,1... | collective-permute-start | bytes 1572872 | tf_op jit(solution)/shard_map/ppermute | solution.py:77
  384.4 18.9 %collective-permute-start.88 = (bf16[256,1024]{1,0:T(8,128)(2,1)S(1)}, bf16[256,1024]{1,0:T(8,128)(2,1)S(1)}, u32[]{:S(2)}, u32[]{:S(2)}) collective-permute-start(bf16[256,1024]{1,0:T(8,128)(2,1)S(1)} %add_convert_fusion.1), channel_id=1, source_target_pairs={{0,8},{8,0},{1,9},{9,1},{2,10},{10,2},{3,11},{11,3},{4,12},{12,4},... | collective-permute-start | bytes 1572872 | tf_op jit(solution)/shard_map/ppermute | solution.py:77
  409.8 23.2 %collective-permute-start.95 = (bf16[2,4,32,1024]{3,2,1,0:T(8,128)(2,1)S(1)}, bf16[2,4,32,1024]{3,2,1,0:T(8,128)(2,1)S(1)}, u32[]{:S(2)}, u32[]{:S(2)}) collective-permute-start(bf16[2,4,32,1024]{3,2,1,0:T(8,128)(2,1)S(1)} %fusion.2), channel_id=1, source_target_pairs={{0,8},{8,0},{1,9},{9,1},{2,10},{10,2},{3,11},{11,3},{4,12},{12,4},... | collective-permute-start | bytes 1572872 | tf_op jit(solution)/shard_map/ppermute | solution.py:77
  416.6 49.3 %collective-permute-start.99 = (bf16[4,4,32,1024]{3,2,1,0:T(8,128)(2,1)}, bf16[4,4,32,1024]{3,2,1,0:T(8,128)(2,1)}, u32[]{:S(2)}, u32[]{:S(2)}) collective-permute-start(bf16[4,4,32,1024]{3,2,1,0:T(8,128)(2,1)} %get-tuple-element.578), channel_id=1, source_target_pairs={{0,16},{16,0},{1,17},{17,1},{2,18},{18,2},{3,19},{19,3},{4,20},{20... | collective-permute-start | bytes 3145736 | tf_op jit(solution)/shard_map/ppermute | solution.py:77
  417.4 17.3 %collective-permute-start.66 = (bf16[256,1024]{1,0:T(8,128)(2,1)}, bf16[256,1024]{1,0:T(8,128)(2,1)}, u32[]{:S(2)}, u32[]{:S(2)}) collective-permute-start(bf16[256,1024]{1,0:T(8,128)(2,1)} %shard_map.241), channel_id=1, source_target_pairs={{0,0},{1,8},{2,4},{3,12},{8,1},{9,9},{10,5},{11,13},{4,2},{5,10},{... | collective-permute-start | bytes 1572872 | tf_op jit(solution)/shard_map/ppermute | solution.py:975
  434.4 44.3 %collective-permute-start.96 = (bf16[256,1024]{1,0:T(8,128)(2,1)}, bf16[256,1024]{1,0:T(8,128)(2,1)}, u32[]{:S(2)}, u32[]{:S(2)}) collective-permute-start(bf16[256,1024]{1,0:T(8,128)(2,1)} %get-tuple-element.562), channel_id=1, source_target_pairs={{0,4},{4,0},{1,5},{5,1},{2,6},{6,2},{3,7},{7,3},{8,12},{12,8},{9,1... | collective-permute-start | bytes 1572872 | tf_op jit(solution)/shard_map/ppermute | solution.py:77
  434.5 31.3 %collective-permute-start.137 = (bf16[4,32,1024]{2,1,0:T(8,128)(2,1)}, bf16[4,32,1024]{2,1,0:T(8,128)(2,1)S(1)}, u32[]{:S(2)}, u32[]{:S(2)}) collective-permute-start(bf16[4,32,1024]{2,1,0:T(8,128)(2,1)} %get-tuple-element.628), channel_id=1, source_target_pairs={{0,2},{1,3},{2,0},{3,1},{4,6},{5,7},{6,4},{7,5},{8,10},{9,11},{10,... | collective-permute-start | bytes 786440 | tf_op jit(solution)/shard_map/ppermute | solution.py:77
  436.8 44.5 %collective-permute-start.118 = (bf16[4,32,1024]{2,1,0:T(8,128)(2,1)}, bf16[4,32,1024]{2,1,0:T(8,128)(2,1)S(1)}, u32[]{:S(2)}, u32[]{:S(2)}) collective-permute-start(bf16[4,32,1024]{2,1,0:T(8,128)(2,1)} %get-tuple-element.611), channel_id=1, source_target_pairs={{0,1},{1,2},{2,3},{3,0},{4,5},{5,6},{6,7},{7,4},{8,9},{9,10},{10,1... | collective-permute-start | bytes 786440 | tf_op jit(solution)/shard_map/ppermute | solution.py:77
  445.0 37.7 %collective-permute-start.119 = (bf16[4,32,1024]{2,1,0:T(8,128)(2,1)}, bf16[4,32,1024]{2,1,0:T(8,128)(2,1)S(1)}, u32[]{:S(2)}, u32[]{:S(2)}) collective-permute-start(bf16[4,32,1024]{2,1,0:T(8,128)(2,1)} %get-tuple-element.610), channel_id=1, source_target_pairs={{0,2},{1,3},{2,0},{3,1},{4,6},{5,7},{6,4},{7,5},{8,10},{9,11},{10,... | collective-permute-start | bytes 786440 | tf_op jit(solution)/shard_map/ppermute | solution.py:77
  465.8 17.0 %collective-permute-start.115 = (bf16[4,32,1024]{2,1,0:T(8,128)(2,1)}, bf16[4,32,1024]{2,1,0:T(8,128)(2,1)S(1)}, u32[]{:S(2)}, u32[]{:S(2)}) collective-permute-start(bf16[4,32,1024]{2,1,0:T(8,128)(2,1)} %get-tuple-element.625), channel_id=1, source_target_pairs={{0,1},{1,2},{2,3},{3,0},{4,5},{5,6},{6,7},{7,4},{8,9},{9,10},{10,1... | collective-permute-start | bytes 786440 | tf_op jit(solution)/shard_map/ppermute | solution.py:77
  465.8 44.4 %collective-permute-start.98 = (bf16[256,1024]{1,0:T(8,128)(2,1)}, bf16[256,1024]{1,0:T(8,128)(2,1)S(1)}, u32[]{:S(2)}, u32[]{:S(2)}) collective-permute-start(bf16[256,1024]{1,0:T(8,128)(2,1)} %copy-done.47), channel_id=1, source_target_pairs={{0,4},{4,0},{1,5},{5,1},{2,6},{6,2},{3,7},{7,3},{8,12},{12,8},{9,1... | collective-permute-start | bytes 1572872 | tf_op jit(solution)/shard_map/ppermute | solution.py:77
  478.7 49.4 %collective-permute-start.101 = (bf16[4,4,32,1024]{3,2,1,0:T(8,128)(2,1)}, bf16[4,4,32,1024]{3,2,1,0:T(8,128)(2,1)}, u32[]{:S(2)}, u32[]{:S(2)}) collective-permute-start(bf16[4,4,32,1024]{3,2,1,0:T(8,128)(2,1)} %get-tuple-element.586), channel_id=1, source_target_pairs={{0,16},{16,0},{1,17},{17,1},{2,18},{18,2},{3,19},{19,3},{4,20},{20... | collective-permute-start | bytes 3145736 | tf_op jit(solution)/shard_map/ppermute | solution.py:77
  481.2 30.3 %collective-permute-start.97 = (bf16[256,1024]{1,0:T(8,128)(2,1)S(1)}, bf16[256,1024]{1,0:T(8,128)(2,1)S(1)}, u32[]{:S(2)}, u32[]{:S(2)}) collective-permute-start(bf16[256,1024]{1,0:T(8,128)(2,1)S(1)} %add_convert_fusion), channel_id=1, source_target_pairs={{0,8},{8,0},{1,9},{9,1},{2,10},{10,2},{3,11},{11,3},{4,12},{12,4},... | collective-permute-start | bytes 1572872 | tf_op jit(solution)/shard_map/ppermute | solution.py:77
  482.9 27.4 %collective-permute-start.134 = (bf16[4,32,1024]{2,1,0:T(8,128)(2,1)S(1)}, bf16[4,32,1024]{2,1,0:T(8,128)(2,1)S(1)}, u32[]{:S(2)}, u32[]{:S(2)}) collective-permute-start(bf16[4,32,1024]{2,1,0:T(8,128)(2,1)S(1)} %get-tuple-element.621), channel_id=1, source_target_pairs={{0,2},{1,3},{2,0},{3,1},{4,6},{5,7},{6,4},{7,5},{8,10},{9,11},{10,... | collective-permute-start | bytes 786440 | tf_op jit(solution)/shard_map/ppermute | solution.py:77
  493.8 34.1 %collective-permute-start.116 = (bf16[4,32,1024]{2,1,0:T(8,128)(2,1)}, bf16[4,32,1024]{2,1,0:T(8,128)(2,1)}, u32[]{:S(2)}, u32[]{:S(2)}) collective-permute-start(bf16[4,32,1024]{2,1,0:T(8,128)(2,1)} %get-tuple-element.624), channel_id=1, source_target_pairs={{0,2},{1,3},{2,0},{3,1},{4,6},{5,7},{6,4},{7,5},{8,10},{9,11},{10,... | collective-permute-start | bytes 786440 | tf_op jit(solution)/shard_map/ppermute | solution.py:77
  510.2 17.9 %collective-permute-start.117 = (bf16[4,32,1024]{2,1,0:T(8,128)(2,1)}, bf16[4,32,1024]{2,1,0:T(8,128)(2,1)}, u32[]{:S(2)}, u32[]{:S(2)}) collective-permute-start(bf16[4,32,1024]{2,1,0:T(8,128)(2,1)} %get-tuple-element.623), channel_id=1, source_target_pairs={{0,3},{1,0},{2,1},{3,2},{4,7},{5,4},{6,5},{7,6},{8,11},{9,8},{10,9... | collective-permute-start | bytes 786440 | tf_op jit(solution)/shard_map/ppermute | solution.py:77
  510.2 16.8 %collective-permute-start.135 = (bf16[4,32,1024]{2,1,0:T(8,128)(2,1)S(1)}, bf16[4,32,1024]{2,1,0:T(8,128)(2,1)S(1)}, u32[]{:S(2)}, u32[]{:S(2)}) collective-permute-start(bf16[4,32,1024]{2,1,0:T(8,128)(2,1)S(1)} %get-tuple-element.620), channel_id=1, source_target_pairs={{0,3},{1,0},{2,1},{3,2},{4,7},{5,4},{6,5},{7,6},{8,11},{9,8},{10,9... | collective-permute-start | bytes 786440 | tf_op jit(solution)/shard_map/ppermute | solution.py:77
  511.5 24.8 %collective-permute-start.105 = (bf16[4,4,32,1024]{3,2,1,0:T(8,128)(2,1)}, bf16[4,4,32,1024]{3,2,1,0:T(8,128)(2,1)}, u32[]{:S(2)}, u32[]{:S(2)}) collective-permute-start(bf16[4,4,32,1024]{3,2,1,0:T(8,128)(2,1)} %get-tuple-element.589), channel_id=1, source_target_pairs={{0,16},{16,0},{1,17},{17,1},{2,18},{18,2},{3,19},{19,3},{4,20},{20... | collective-permute-start | bytes 3145736 | tf_op jit(solution)/shard_map/ppermute | solution.py:77
  531.0 40.4 %collective-permute-start.102 = (bf16[4,32,1024]{2,1,0:T(8,128)(2,1)}, bf16[4,32,1024]{2,1,0:T(8,128)(2,1)}, u32[]{:S(2)}, u32[]{:S(2)}) collective-permute-start(bf16[4,32,1024]{2,1,0:T(8,128)(2,1)} %get-tuple-element.616), channel_id=1, source_target_pairs={{0,1},{1,2},{2,3},{3,0},{4,5},{5,6},{6,7},{7,4},{8,9},{9,10},{10,1... | collective-permute-start | bytes 786440 | tf_op jit(solution)/shard_map/ppermute | solution.py:77
  533.0 42.9 %collective-permute-start.103 = (bf16[4,32,1024]{2,1,0:T(8,128)(2,1)}, bf16[4,32,1024]{2,1,0:T(8,128)(2,1)}, u32[]{:S(2)}, u32[]{:S(2)}) collective-permute-start(bf16[4,32,1024]{2,1,0:T(8,128)(2,1)} %get-tuple-element.618), channel_id=1, source_target_pairs={{0,2},{1,3},{2,0},{3,1},{4,6},{5,7},{6,4},{7,5},{8,10},{9,11},{10,... | collective-permute-start | bytes 786440 | tf_op jit(solution)/shard_map/ppermute | solution.py:77
  567.0 17.8 %collective-permute-start.107 = (bf16[4,32,1024]{2,1,0:T(8,128)(2,1)}, bf16[4,32,1024]{2,1,0:T(8,128)(2,1)S(1)}, u32[]{:S(2)}, u32[]{:S(2)}) collective-permute-start(bf16[4,32,1024]{2,1,0:T(8,128)(2,1)} %get-tuple-element.614), channel_id=1, source_target_pairs={{0,2},{1,3},{2,0},{3,1},{4,6},{5,7},{6,4},{7,5},{8,10},{9,11},{10,... | collective-permute-start | bytes 786440 | tf_op jit(solution)/shard_map/ppermute | solution.py:77
  571.3 21.7 %collective-permute-start.108 = (bf16[4,32,1024]{2,1,0:T(8,128)(2,1)}, bf16[4,32,1024]{2,1,0:T(8,128)(2,1)S(1)}, u32[]{:S(2)}, u32[]{:S(2)}) collective-permute-start(bf16[4,32,1024]{2,1,0:T(8,128)(2,1)} %get-tuple-element.613), channel_id=1, source_target_pairs={{0,3},{1,0},{2,1},{3,2},{4,7},{5,4},{6,5},{7,6},{8,11},{9,8},{10,9... | collective-permute-start | bytes 786440 | tf_op jit(solution)/shard_map/ppermute | solution.py:77
  575.8 35.0 %collective-permute-start.100 = (bf16[256,1024]{1,0:T(8,128)(2,1)S(1)}, bf16[256,1024]{1,0:T(8,128)(2,1)S(1)}, u32[]{:S(2)}, u32[]{:S(2)}) collective-permute-start(bf16[256,1024]{1,0:T(8,128)(2,1)S(1)} %get-tuple-element.584), channel_id=1, source_target_pairs={{0,0},{1,8},{2,4},{3,12},{8,1},{9,9},{10,5},{11,13},{4,2},{5,10},{... | collective-permute-start | bytes 1572872 | tf_op jit(solution)/shard_map/ppermute | solution.py:975
  576.5 20.3 %collective-permute-start.122 = (bf16[32,1024]{1,0:T(8,128)(2,1)}, bf16[32,1024]{1,0:T(8,128)(2,1)S(1)}, u32[]{:S(2)}, u32[]{:S(2)}) collective-permute-start(bf16[32,1024]{1,0:T(8,128)(2,1)} %get-tuple-element.632), channel_id=1, source_target_pairs={{0,4},{4,0},{8,12},{12,8},{1,5},{5,1},{9,13},{13,9},{2,6},{6,2},{1... | collective-permute-start | bytes 196616 | tf_op jit(solution)/shard_map/ppermute | solution.py:106
  578.2 16.1 %collective-permute-start.121 = (bf16[32,768]{1,0:T(8,128)(2,1)}, bf16[32,768]{1,0:T(8,128)(2,1)S(1)}, u32[]{:S(2)}, u32[]{:S(2)}) collective-permute-start(bf16[32,768]{1,0:T(8,128)(2,1)} %get-tuple-element.636), channel_id=1, source_target_pairs={{0,4},{4,0},{8,12},{12,8},{1,5},{5,1},{9,13},{13,9},{2,6},{6,2},{1... | collective-permute-start | bytes 147464 | tf_op jit(solution)/shard_map/ppermute | solution.py:106
  (211 other events, 2219.2 us)

commit v3 on v2

--- a/solution.py
+++ b/solution.py
@@ -90,11 +90,12 @@
     got = {}
     for k in list(range(1, xs)) + [0]:
         got[k] = shift(parts[k, 1].astype(BF), CORE, CORES, 1)
-    terms = [parts[0, 0]]
+    terms, sent = [parts[0, 0]], []
     for k in range(1, xs):
         both = (parts[k, 0].astype(F32) + got[k].astype(F32)).astype(BF)
+        sent.append(both)
         terms.append(shift(both, XX, xs, -k))
-    return terms + [got[0]]
+    return terms + [got[0]], sent
 
 
 def send_lo(x, xs, k, dc):
@@ -125,37 +126,24 @@
 
 def fetch(x, out, hs, ts):
     out[0, 0] = way = x
+    behind = None
     for kb in range(ts):
         came = way
         up = [shift(came, HI, hs, kh) for kh in range(1, hs)]
         if kb + 1 < ts:
             way = shift(came, BLK, ts, 1)
         after = yield came
-        up, way = tie((up, way), after)
-        for kh in range(1, hs):
-            out[kh, kb] = up[kh - 1]
+        if after:
+            behind, way = tie((behind, way), after)
+        if behind is not None:
+            for kh in range(1, hs):
+                out[kh, kb - 1] = behind[kh - 1]
+        behind = up
         if kb + 1 < ts:
             out[0, kb + 1] = way
+    for kh in range(1, hs):
+        out[kh, ts - 1] = up[kh - 1]
     return up
-
-
-def reduce(parts, out, hs, ts):
-    got = [shift(parts[kh], HI, hs, kh) for kh in range(1, hs)]
-    after = yield parts
-    got = tie(got, after)
-    total = []
-    for kb in range(ts):
-        block = parts[0][kb].astype(F32)
-        for g in got:
-            block = block + g[kb].astype(F32)
-        total.append(block if kb == 0 else block.astype(BF))
-    out.append(total[0])
-    for kb in range(1, ts):
-        way = shift(total[kb], BLK, ts, kb)
-        after = yield total
-        way = tie(way, after)
-        out.append(way)
-    return way
 
 
 def pieces_of(out, hs, ts):
@@ -243,8 +231,9 @@
     layers = wq.shape[0]
     chunk = wq.shape[2] // (3 * ts)
     half = wu.shape[2] // (2 * ts)
-    for rest, (k, dc) in zip(outs, slots_of(xs)):
+    for k, dc in slots_of(xs):
         lo = lo_plus(me, xs, k, dc)
+        rest = outs[dc].at[k]
         at = 0
         for layer in range(layers):
             if layer:
@@ -261,13 +250,12 @@
 def rest_cuts_of(me, wq, wu, xs, ts):
     layers, rows, full = wu.shape
     wide = 3 * D // ts
-    got = run(
+    return run(
         functools.partial(rest_kernel, xs, ts),
-        [shape((rows, layers * (wide + full // ts) - wide), BF)] * ts,
+        [shape((xs, rows, layers * (wide + full // ts) - wide), BF)] * CORES,
         [me],
         [wq, wu],
     )
-    return dict(zip(slots_of(xs), got))
 
 
 def fold_in(out, block, at, cols):
@@ -723,17 +711,17 @@
     sums[0:1, :] = gains
     sums[1:2, :] = shifts
     sums[2:3, :] = jnp.sum(dy[...].astype(F32), axis=0, keepdims=True)
-    width = outs[0].shape[1]
-    for j, (k, dc) in enumerate(slots_of(xs)):
+    width = outs[0].shape[2]
+    for k, dc in slots_of(xs):
         off = pl.multiple_of(lo_plus(me, xs, k, dc) * width, width)
-        outs[j][...] = nt(dy[...], w[pl.ds(off, width), :]).astype(BF)
+        outs[dc][k] = nt(dy[...], w[pl.ds(off, width), :]).astype(BF)
 
 
 def mid_back(me, terms, grad, middle, vec, layer, w, ts, xs):
     n = middle.shape[0]
     got = run(
         functools.partial(mid_back_kernel, len(terms), ts, xs, 6 * layer + 3),
-        [shape((n, D), F32), shape((n, D), BF), shape((3, D), F32)] + [shape((n, D // ts), BF)] * ts,
+        [shape((n, D), F32), shape((n, D), BF), shape((3, D), F32)] + [shape((xs, n, D // ts), BF)] * CORES,
         [me],
         terms + [grad, middle, vec, w],
         flops=2 * n * D * D,
@@ -773,10 +761,10 @@
     return total
 
 
-def cols_part(ts, xs, hs, rows, me, left, right, put):
+def cols_part(ts, xs, hs, rows, own, me, left, right, put):
     tile = CORES * ts * rows
     for kh in list(range(1, hs)) + [0]:
-        h = lax.rem(me[0] + kh, hs)
+        h = kh if own else lax.rem(me[0] + kh, hs)
         for k in range(xs):
             place_at = (h * ts + lax.rem(me[1] + k, xs) * CORES) * ts * rows
             cols = pl.ds(pl.multiple_of(place_at, tile), tile)
@@ -786,12 +774,12 @@
             for c in range(CORES):
                 dc = lax.rem(me[2] + c, CORES)
                 for b in range(ts):
-                    kb = lax.rem(b - me[3] + ts, ts)
+                    kb = b if own else lax.rem(b - me[3] + ts, ts)
                     at = (c * ts + b) * rows
                     put(kh, kb, dc, k, got[at : at + rows, :].astype(BF))
 
 
-def wgrad_cols_kernel(ts, xs, hs, rows, beside, me, *refs):
+def wgrad_cols_kernel(ts, xs, hs, rows, beside, own, me, *refs):
     left, right = refs[:ts], refs[ts : 2 * ts]
     refs = refs[2 * ts :]
     if beside:
@@ -803,23 +791,28 @@
     def put(kh, kb, dc, k, block):
         outs[kh][kb, k * CORES + dc, :, :wide] = block
 
-    cols_part(ts, xs, hs, rows, me, left, right, put)
+    cols_part(ts, xs, hs, rows, own, me, left, right, put)
     if beside:
         cols = outs[0].shape[3] - wide
         for kh in range(hs):
             for kb in range(ts):
+                to = lax.rem(me[3] + kb, ts) if own else kb
+                where = lax.rem(kh - me[0] + hs, hs) if own else kh
                 for p in range(ts):
-                    outs[kh][kb, p, :, wide:] = near[kh, kb, :, p * cols : (p + 1) * cols]
-
-
-def wgrad_cols(me, left, right, hs, xs, near=None):
+                    outs[kh][to, p, :, wide:] = near[where, kb, :, p * cols : (p + 1) * cols]
+
+
+def wgrad_cols(me, left, right, hs, xs, own, near=None):
     ts = len(left)
     rows = D // (hs * ts * ts)
     n, wide = right[0].shape
     beside = near is not None
+    outs = [shape((ts, ts, rows, wide + (D // ts if beside else 0)), BF)] * hs
+    if own:
+        outs = [shape((hs,) + outs[0].shape, BF)]
     got = run(
-        functools.partial(wgrad_cols_kernel, ts, xs, hs, rows, beside),
-        [shape((1, wide), F32)] + [shape((ts, ts, rows, wide + (D // ts if beside else 0)), BF)] * hs,
+        functools.partial(whole_kernel(wgrad_cols_kernel) if own else wgrad_cols_kernel, ts, xs, hs, rows, beside, own),
+        [shape((1, wide), F32)] + outs,
         [me],
         left + right + ([near] if beside else []),
         flops=2 * ts * n * D * wide,
@@ -827,40 +820,55 @@
     return got[0], list(got[1:])
 
 
-def wgrad_down_kernel(ts, hs, rows, tall, me, *refs):
-    hidden, dz = refs[:ts], refs[ts : 2 * ts]
-    outs = refs[2 * ts :]
-    cols = outs[0].shape[3]
+def wgrad_ffn_kernel(ts, xs, hs, rows, tall, own, me, *refs):
+    normed, du, hidden, dz = [refs[j * ts : (j + 1) * ts] for j in range(4)]
+    refs[4 * ts][...] = column_sums(du)
+    outs = refs[4 * ts + 1 :]
+    cols = du[0].shape[1]
+
+    def put(kh, kb, dc, k, block):
+        outs[kh][kb, k * CORES + dc] = block
+
+    cols_part(ts, xs, hs, rows, own, me, normed, du, put)
     group = min(ts, max(1, 256 // tall))
     for kh in list(range(1, hs)) + [0]:
-        h = lax.rem(me[0] + kh, hs)
+        h = kh if own else lax.rem(me[0] + kh, hs)
         for first in range(0, ts, group):
             take = pl.ds(pl.multiple_of((h * ts + first) * tall, group * tall), group * tall)
             got = tn(hidden[0][:, take], dz[0][...])
             for j in range(1, ts):
                 got = got + tn(hidden[j][:, take], dz[j][...])
             for b in range(group):
-                kb = lax.rem(first + b - me[3] + ts, ts)
+                kb = first + b if own else lax.rem(first + b - me[3] + ts, ts)
                 for g in range(ts):
                     p, low = (g * rows) // tall, (g * rows) % tall
-                    outs[kh][kb, g] = got[
+                    outs[kh][kb, ts + g] = got[
                         b * tall + low : b * tall + low + rows, p * cols : (p + 1) * cols
                     ].astype(BF)
 
 
-def wgrad_down(me, hidden, dz, hs):
-    ts = len(hidden)
+def wgrad_ffn(me, normed, du, hidden, dz, hs, xs, own):
+    ts = len(normed)
     rows = D // (hs * ts * ts)
-    n, wide = hidden[0].shape
-    return list(
-        run(
-            functools.partial(wgrad_down_kernel, ts, hs, rows, wide // (hs * ts)),
-            [shape((ts, ts, rows, wide), BF)] * hs,
-            [me],
-            hidden + dz,
-            flops=2 * ts * n * D * wide,
-        )
-    )
+    n, wide = du[0].shape
+    outs = [shape((ts, 2 * ts, rows, wide), BF)] * hs
+    if own:
+        outs = [shape((hs, ts, 2 * ts, rows, wide), BF)]
+    got = run(
+        functools.partial(wgrad_ffn_kernel if not own else whole_kernel(wgrad_ffn_kernel), ts, xs, hs, rows, wide // (hs * ts), own),
+        [shape((1, wide), F32)] + outs,
+        [me],
+        normed + du + hidden + dz,
+        flops=4 * ts * n * D * wide,
+    )
+    return got[0], list(got[1:])
+
+
+def whole_kernel(kernel):
+    def wrapped(ts, xs, hs, *rest):
+        return kernel(ts, xs, hs, *rest[:-1], *[rest[-1].at[h] for h in range(hs)])
+
+    return wrapped
 
 
 def wgrad_out_kernel(ts, xs, hs, rows, me, *refs):
@@ -895,52 +903,79 @@
     return got
 
 
+def finish_kernel(counts, wide, ts, xs, *refs):
+    layers = len(counts)
+    outs = refs[-ts - 2 : -2]
+    out_out, out_down = refs[-2:]
+    rows, cols = refs[0].shape[1:]
+    at = 0
+
+    def total(count, j):
+        got = refs[at][j].astype(F32)
+        for t in refs[at + 1 : at + count]:
+            got = got + t[j].astype(F32)
+        return got
+
+    for layer in range(layers):
+        for j in range(ts):
+            got = total(counts[layer], j)
+            outs[j][layer * rows : (layer + 1) * rows, wide:] = got.astype(BF)
+            got = total(counts[layer], ts + j)
+            tall = out_down.shape[1]
+            p, low = (j * rows) // tall, (j * rows) % tall
+            out_down[layer, low : low + rows, p * cols : (p + 1) * cols] = got
+        at += counts[layer]
+    for layer in range(layers):
+        for j in range(ts):
+            got = total(counts[layer], j)
+            outs[j][layer * rows : (layer + 1) * rows, :wide] = got[:, :wide].astype(BF)
+            more = got.shape[1] - wide
+            out_out[layer, :, j * more : (j + 1) * more] = got[:, wide:]
+        at += counts[layer]
+
+
+def finish(f_all, a_all, wide, ts, xs):
+    layers = len(f_all)
+    rows, cols = f_all[0][0].shape[1:]
+    tall = ts * rows * cols // D
+    got = run(
+        functools.partial(finish_kernel, [len(f) for f in f_all], wide, ts, xs),
+        [shape((layers * rows, wide + cols), BF)] * ts
+        + [shape((layers, rows, D), F32), shape((layers, tall, D), F32)],
+        [],
+        [x for terms in f_all + a_all for x in terms],
+    )
+    return dict(zip(slots_of(xs), got)), got[ts], got[ts + 1]
+
+
 def join_kernel(ts, xs, layers, me, *refs):
     out_q, out_u = refs[-2:]
     wide = out_q.shape[2] // (3 * ts)
     chunk = out_u.shape[2] // (2 * ts)
-    at = 0
-    for layer in range(layers):
-        for k, dc in slots_of(xs):
-            lo = lo_minus(me, xs, k, dc)
-            q, u = refs[at], refs[at + 1]
-            at += 2
+    rows = out_q.shape[1]
+    for block, (k, dc) in zip(refs, slots_of(xs)):
+        lo = lo_minus(me, xs, k, dc)
+        for layer in range(layers):
+            at = pl.ds(layer * rows, rows)
             for j in range(3):
-                off = pl.multiple_of(j * D + lo * wide, 128)
-                out_q[layer, :, pl.ds(off, wide)] = q[:, j * wide : (j + 1) * wide].astype(F32)
+                off = pl.multiple_of((j * ts + lo) * wide, 128)
+                out_q[layer, :, pl.ds(off, wide)] = block[at, j * wide : (j + 1) * wide].astype(F32)
             for j in range(2):
-                off = pl.multiple_of(j * (chunk * ts) + lo * chunk, 128)
-                out_u[layer, :, pl.ds(off, chunk)] = u[:, j * chunk : (j + 1) * chunk].astype(F32)
-
-
-def join(me, grads, ts, xs):
-    layers = len(grads)
-    arrays = []
-    for q, u in grads:
-        for s in slots_of(xs):
-            arrays += [q[s], u[s]]
-    rows = arrays[0].shape[0]
+                off = pl.multiple_of((j * ts + lo) * chunk, 128)
+                have = 3 * wide + j * chunk
+                out_u[layer, :, pl.ds(off, chunk)] = block[at, have : have + chunk].astype(F32)
+
+
+def join(me, blocks, layers, ts, xs):
+    arrays = [blocks[s] for s in slots_of(xs)]
+    rows = arrays[0].shape[0] // layers
+    wide = 3 * D // ts
     return run(
         functools.partial(join_kernel, ts, xs, layers),
-        [shape((layers, rows, arrays[0].shape[1] * ts), F32), shape((layers, rows, arrays[1].shape[1] * ts), F32)],
+        [shape((layers, rows, 3 * D), F32), shape((layers, rows, (arrays[0].shape[1] - wide) * ts), F32)],
         [me],
         arrays,
     )
-
-
-def sum_small(mine, shared, hs, ts, xs):
-    mine = mine + shift(mine, CORE, CORES, 1)
-    for_all = mine
-    for k in range(1, xs):
-        for_all = for_all + shift(mine, XX, xs, k)
-    both = jnp.concatenate([for_all, shared], 0)
-    total = both
-    for kh in range(1, hs):
-        total = total + shift(both, HI, hs, kh)
-    out = total
-    for kb in range(1, ts):
-        out = out + shift(total, BLK, ts, kb)
-    return out
 
 
 def on_device(
@@ -986,19 +1021,35 @@
         group = gather_lo(near, xs)
         return place_out(me, [group[s] for s in slots], hs, ts, xs)
 
+    def along_blk(x):
+        return lax.all_gather(x, BLK, axis=0, tiled=False)
+
+    def with_hi(x):
+        return [x] + [shift(x, HI, hs, kh) for kh in range(1, hs)]
+
+    tokens_own = turned(message_of(tokens[0], segment_ids))
+    attn_out, ffn_out = {}, {}
     mine = own_columns(near_cuts_of(me, qkv_weight, fields, xs, ts))
-    tokens_own = turned(tie(message_of(tokens[0], segment_ids), mine))
-    attn_out, ffn_out = {}, {}
     attn_work = Work(fetch(pack_first(mine, out_weight), attn_out, hs, ts))
     late_q, late_u = tie((qkv_weight, up_weight), mine)
-    rest = own_columns(rest_cuts_of(me, late_q, late_u, xs, ts))
+    same, other = rest_cuts_of(me, late_q, late_u, xs, ts)
+    other = shift(other, CORE, CORES, 1)
+    rest = [same[0], other[0]]
+    for k in range(1, xs):
+        pair = shift(jnp.stack([same[k], other[k]]), XX, xs, k)
+        rest += [pair[0], pair[1]]
     packed = pack_rest(rest, down_weight, out_weight, wide, cols)
-    for _ in range(ts):
-        attn_work.step()
+    attn_work.step(tokens_own)
     by = gather_lo(tokens_own, xs)
     given = [by[s] for s in slots]
+    for kb in range(1, ts):
+        attn_work.step(*([packed[0]] if kb == 1 else [by[xs - 1, 0]] if kb == 2 else []))
     attn_pieces = pieces_of(attn_out, hs, ts)
     ffn_work = Work(fetch(packed[0], ffn_out, hs, ts))
+    stacks = []
+    for l in range(1, layers):
+        attn_stack = along_blk(packed[2 * l - 1])
+        stacks.append((attn_stack, along_blk(tie(packed[2 * l], attn_stack))))
     w_qkv, out_near = place_attn(me, attn_pieces, rows, hs, ts, xs, True)
     vec, up_vec, qkv_vec = params(me, attn_pieces, rows, layers, each, cols, wide // 3, hs, ts, xs)
 
@@ -1007,54 +1058,53 @@
     segs = None
     for l in range(layers):
         more = l + 1 < layers
-        given = tie(given, ffn_work.step(w_qkv))
-        if l + 1 == layers:
-            grad_own = turned(tie(out_grad[0], given))
+        if l == 0:
+            given = tie(given, ffn_work.step(w_qkv))
         w_out = gather_out(out_near)
         qkv, out_t, lse, heads_by, all_one, segs = attn_fwd(
             me, slopes, given, w_qkv, qkv_vec, l, xs, vec if l == 0 else None, segs
         )
         own = exchange_lo({s: heads_by[j] for j, s in enumerate(slots)}, xs, -1)
-        own = tie([own[s] for s in slots], ffn_work.step(heads_by))
-        if l + 1 == layers:
-            own = tie(own, grad_own)
+        own = [own[s] for s in slots]
+        if l == 0:
+            own = tie(own, ffn_work.step(heads_by))
+        if not more:
+            own = tie(own, grad_x)
         middle, normed_two = out_project(me, own, w_out, vec, l, stream, xs)
         by = gather_lo(normed_two, xs)
         all_two = [by[s] for s in slots]
         near, far = all_two[:CORES], all_two[CORES:]
         if l == 0:
             near = tie(near, ffn_work.step(middle))
-        while ffn_work.step() is not None and (hs - 1, ts - 1) not in ffn_out:
-            pass
-        ffn_pieces = pieces_of(ffn_out, hs, ts)
-        if more:
-            next_attn, next_ffn = {}, {}
-            attn_work = Work(fetch(tie(packed[2 * l + 1], ffn_out[0, ts - 1]), next_attn, hs, ts))
+            while (hs - 1, ts - 1) not in ffn_out:
+                ffn_work.step()
+            ffn_pieces = pieces_of(ffn_out, hs, ts)
         w_up, w_down = place_ffn(me, ffn_pieces, hs, ts, xs)
         hid_a, gel_a, part_a = ffn_fwd(near, w_up, up_vec, l, w_down, [F32] + [BF] * (CORES - 1))
         far = tie(far, part_a)
         if more:
-            far = tie(far, attn_work.step(part_a))
-        else:
-            grad_by = gather_lo(tie(grad_own, all_two), xs)
+            attn_stack, ffn_stack = stacks[l]
+            attn_pieces = with_hi(tie(attn_stack, all_two))
+        if l + 2 == layers:
+            grad_own = turned(tie(out_grad[0], all_two))
         hid_b, gel_b, part_b = ffn_fwd(far, w_up, up_vec, l, w_down, [BF] * len(far))
-        terms = scatter_lo(dict(zip(slots, part_a + part_b)), xs)
+        terms, sent = scatter_lo(dict(zip(slots, part_a + part_b)), xs)
         stored.append((stream, all_one, qkv, out_t, lse, own, middle, all_two, hid_a + hid_b, gel_a + gel_b))
         weights.append((w_qkv, w_out, w_up, w_down))
         if more:
-            terms = tie(terms, attn_work.step(part_b))
-            ffn_work = Work(fetch(tie(packed[2 * l + 2], part_b), next_ffn, hs, ts))
             stream, normed = layer_end(terms, middle, vec, l, False)
             by = gather_lo(normed, xs)
             given = [by[s] for s in slots]
-            given = tie(given, attn_work.step(normed), ffn_work.step(normed))
-            while (hs - 1, ts - 1) not in next_attn:
-                attn_work.step()
-            w_qkv, out_near = place_attn(me, pieces_of(next_attn, hs, ts), rows, hs, ts, xs, True)
-            attn_out, ffn_out = next_attn, next_ffn
+            ffn_pieces = with_hi(tie(ffn_stack, normed))
+            if l + 2 == layers:
+                grad_x = [grad_own] + [shift(tie(grad_own, given), XX, xs, k) for k in range(1, xs)]
+            w_qkv, out_near = place_attn(me, attn_pieces, rows, hs, ts, xs, True)
         else:
             (final,) = layer_end(terms, middle, vec, l, True)
-    result = turned(final)
+    grad_by = {}
+    for k in range(xs):
+        grad_by[k, 0] = grad_x[k]
+        grad_by[k, 1] = shift(grad_x[k], CORE, CORES, 1)
 
     dh, dz = grad_own, grad_own
     down_sum = jnp.sum(grad_own.astype(F32), axis=0, keepdims=True)
@@ -1070,102 +1120,113 @@
         total = total.reshape(count, -1, total.shape[-1])
         return jnp.concatenate([total[p] for p in range(count)], 1)
 
-    def marker(parts):
-        return parts[-1][0, 0, :8, :128]
-
-    class Sums:
-        def __init__(self, parts, *after):
-            self.terms = []
-            if after:
-                parts = parts[:1] + list(tie(parts[1:], after))
-            self.work = Work(reduce(parts, self.terms, hs, ts))
-            self.step = self.work.step
-
-        def finish(self, *after):
-            while len(self.terms) < ts:
-                self.step(*after)
-            return self.terms
-
-    late = None
+    def added(own, got):
+        total = own.astype(F32)
+        for g in got:
+            total = total + g.astype(F32)
+        return total.astype(BF)
+
+    def scattered(x):
+        x = x.reshape((hs * ts,) + x.shape[2:])
+        return lax.psum_scatter(x, (HI, BLK), scatter_dimension=0, tiled=False)
+
+    def add_up(own, got, *after):
+        got = tie(got, after)
+        total = []
+        for kb in range(ts):
+            block = own[kb].astype(F32)
+            for g in got:
+                block = block + g[kb].astype(F32)
+            total.append(block.astype(BF) if kb else block)
+        return total
+
+    def send_blk(total):
+        return [shift(total[kb], BLK, ts, kb) for kb in range(1, ts)]
+
+    f_sums, a_sums = [None] * layers, [None] * layers
     for l in reversed(range(layers)):
         w_qkv, w_out, w_up, w_down = weights[l]
         stream, all_one, qkv, out_t, lse, own, middle, all_two, hidden, gel = stored[l]
-        first_layer = l == 0
-        by = grad_by if late is None else gather_lo(dz, xs)
+        first_layer, last = l == 0, l + 1 == layers
+        by = grad_by if last else gather_lo(dz, xs)
         all_dz = [by[s] for s in slots]
         near, far = all_dz[:CORES], all_dz[CORES:]
-        if late:
-            near = tie(near, late["d"].step(dz), late["u"].step(dz))
-            late["a"] = Sums(late["a_parts"], near)
-        else:
+        if last:
             near = tie(near, final)
         du_a, part_a = ffn_bwd(near, gel[:CORES], w_up, w_down, [F32] + [BF] * (CORES - 1))
         far = tie(far, part_a)
-        if late:
-            far = tie(far, late["d"].step(part_a))
         du_b, part_b = ffn_bwd(far, gel[CORES:], w_up, w_down, [BF] * (ts - CORES))
         all_du = du_a + du_b
-        terms = scatter_lo(dict(zip(slots, part_a + part_b)), xs)
-        d_parts = wgrad_down(me, hidden, tie(all_dz, part_b), hs)
-        d_sums = Sums(d_parts)
-        up_sum, u_parts = wgrad_cols(me, all_two, tie(all_du, marker(d_parts)), hs, xs)
+        terms, sent = scatter_lo(dict(zip(slots, part_a + part_b)), xs)
+        up_sum, f_parts = wgrad_ffn(me, all_two, tie(all_du, sent), hidden, all_dz, hs, xs, not first_layer)
         terms = tie(terms, up_sum)
-        if late:
-            terms = tie(terms, late["u"].step(part_b), late["a"].step(up_sum))
+        if first_layer:
+            f_way = [shift(g, HI, hs, kh + 1) for kh, g in enumerate(f_parts[1:])]
+        else:
+            f_sums[l] = scattered(f_parts[0])
         dh1, dy, mid_sums, d_heads = mid_back(me, terms, dh, middle, vec, l, w_out, ts, xs)
-        by = exchange_lo(dict(zip(slots, d_heads)), xs, 1)
-        d_out = [by[s] for s in slots]
-        out_part = wgrad_out(me, own, dy, hs, xs)
+        same, other = d_heads
+        other = shift(other, CORE, CORES, 1)
+        pairs = [jnp.stack([same[k], other[k]]) for k in range(1, xs)]
+        d_out = [same[0], other[0]]
+        for k in range(1, xs):
+            pair = shift(pairs[k - 1], XX, xs, k)
+            d_out += [pair[0], pair[1]]
+        out_part = wgrad_out(me, tie(own, pairs), dy, hs, xs)
         got = shift(out_part[1], CORE, CORES, 1)
         both = [(out_part[0, k].astype(F32) + got[k].astype(F32)) for k in range(xs)]
         o_sent = [both[k].astype(BF) for k in range(1, xs)]
-        o_got = [shift(o_sent[k - 1], XX, xs, k) for k in range(1, xs)]
         d_out = tie(d_out, o_sent)
-        if late:
-            d_out = tie(d_out, late["u"].step(dy), late["a"].step(dy))
+        dqkv, parts = attn_bwd(me, slopes, d_out, qkv, out_t, lse, w_qkv, *segs, xs)
+        terms, sent = scatter_lo(dict(zip(slots, parts)), xs)
+        o_got = [shift(tie(o_sent[k - 1], sent), XX, xs, k) for k in range(1, xs)]
+        o_near = both[0]
+        for g in tie(o_got, sent):
+            o_near = o_near + g.astype(F32)
+        if first_layer:
+            qkv_sum, a_parts = wgrad_cols(me, all_one, tie(dqkv, sent), hs, xs, False, o_near.astype(BF))
+            terms = tie(terms, qkv_sum)
+            f_total = add_up(f_parts[0], f_way, qkv_sum)
+            terms = tie(terms, f_total)
+            f_got = send_blk(f_total)
+            a_way = [shift(g, HI, hs, kh + 1) for kh, g in enumerate(a_parts[1:])]
         else:
-            d_out = tie(d_out, d_sums.step(dy))
-            u_sums = Sums(u_parts, d_out)
-        dqkv, parts = attn_bwd(me, slopes, d_out, qkv, out_t, lse, w_qkv, *segs, xs)
-        o_near = both[0]
-        for g in tie(o_got, dqkv):
-            o_near = o_near + g.astype(F32)
-        o_near = o_near.astype(BF)
-        terms = scatter_lo(dict(zip(slots, tie(parts, o_near))), xs)
-        qkv_sum, a_parts = wgrad_cols(me, all_one, dqkv, hs, xs, o_near)
-        terms = tie(terms, qkv_sum, d_sums.step(dqkv))
-        if late:
-            u_sums = Sums(u_parts, qkv_sum)
+            qkv_sum, a_parts = wgrad_cols(me, all_one, tie(dqkv, sent), hs, xs, True, o_near.astype(BF))
+            a_sums[l] = scattered(tie(a_parts[0], f_sums[l]))
+            terms = tie(terms, qkv_sum)
         dh, dz, start_sums = start_back(terms, dh1, stream, vec, l)
         mine_sums[l] = jnp.concatenate([down_sum, mid_sums, start_sums[:2]], 0)
         third = wide // 3
         shared_sums[l] = (up_sum, qkv_sum[:, :third], qkv_sum[:, 2 * third :])
         down_sum = start_sums[2:3]
-        if not first_layer:
-            late = dict(d=d_sums, u=u_sums, a_parts=a_parts)
-    u_sums.step(dz)
-    a_sums = Sums(a_parts, u_sums.terms)
-    late["a"].step(dz)
-    d_sums.finish(dz)
-    d_grads[0] = unfolded(d_sums.terms)
-    a_sums.step()
-    u_grads[0] = send_cols(u_sums.finish())
-    d_grads[1] = unfolded(late["d"].finish(dz))
-    u_grads[1] = send_cols(late["u"].finish(dz))
-    q_grads[1] = send_cols(late["a"].finish(dz), slice(0, wide))
-    o_grads[1] = unfolded(late["a"].terms, slice(wide, None), ts)
-    a_sums.finish()
-    q_grads[0] = send_cols(a_sums.terms, slice(0, wide))
-    o_grads[0] = unfolded(a_sums.terms, slice(wide, None), ts)
-    input_grad = turned(dz)
-
     full = max(D, shared_sums[0][0].shape[1])
     pad = lambda x: jnp.pad(x, ((0, 0), (0, full - x.shape[1])))
     both = []
     for l in range(layers):
         up_sum, q_sum, v_sum = shared_sums[l]
         both += [pad(up_sum), pad(jnp.concatenate([q_sum, v_sum], 1))]
-    sums = sum_small(jnp.concatenate(mine_sums, 0), jnp.concatenate(both, 0), hs, ts, xs)
+    mine = jnp.concatenate(mine_sums, 0)
+    mine = mine + shift(mine, CORE, CORES, 1)
+    mine_x = [shift(mine, XX, xs, k) for k in range(1, xs)]
+    a_total = add_up(a_parts[0], a_way, f_got)
+    a_got = send_blk(a_total)
+    for x in tie(mine_x, a_total):
+        mine = mine + x
+    small = jnp.concatenate([mine] + both, 0)
+    small_y = [shift(small, HI, hs, kh) for kh in range(1, hs)]
+    both_turned = turned(jnp.stack([tie(dz, a_total), final]))
+    input_grad, result = both_turned[0], both_turned[1]
+    for y in small_y:
+        small = small + y
+    small_z = send_blk([small] * ts)
+    f_all = [[f_total[0]] + f_got] + [[f_sums[l]] for l in range(1, layers)]
+    a_all = [[a_total[0]] + a_got] + [[a_sums[l]] for l in range(1, layers)]
+    blocks, out_grad_all, down_grad_all = finish(f_all, a_all, wide, ts, xs)
+    q_grad, u_grad = join(me, exchange_lo(blocks, xs, 1), layers, ts, xs)
+    sums = small
+    for z in small_z:
+        sums = sums + z
+
     device = (hi * ts + lo) * ts + blk
     vectors = lax.dynamic_slice(sums[: 6 * layers, :D], (0, device * each), (6 * layers, each))
     vectors = vectors.reshape(layers, 6, each)
@@ -1173,17 +1234,16 @@
     up_each, qv_each = up_bias.shape[1], qv_bias.shape[1]
     up_grad = lax.dynamic_slice(shared[:, 0], (0, (hi * ts + blk) * up_each), (layers, up_each))
     qv_grad = lax.dynamic_slice(shared[:, 1], (0, (hi * ts + blk) * qv_each), (layers, qv_each))
-    q_grad, u_grad = join(me, list(zip(q_grads, u_grads)), ts, xs)
     return (
         result[None],
         input_grad[None],
         q_grad,
         qv_grad,
-        jnp.stack(o_grads),
+        out_grad_all,
         vectors[:, 3],
         u_grad,
         up_grad,
-        jnp.stack(d_grads),
+        down_grad_all,
         vectors[:, 0],
         jnp.stack([vectors[:, 4], vectors[:, 1]], 1),
         jnp.stack([vectors[:, 5], vectors[:, 2]], 1),

time: 624 us -> 611 us (0.979)
  starting transfers between devices: 143 us -> 116 us
  between operations: 2.71 us -> 15.8 us
  local copies, waits for them, and re-layouts: 37.9 us -> 48.7 us
  other arithmetic: 27.7 us -> 18.4 us
    ppermute x30 -> x12, starting transfers between devices: 31.3 us -> 12.1 us  [send_lo(): return lax.ppermute(x, (XX, CORE), pairs)]
    ppermute x104 -> x82, starting transfers between devices: 103 us -> 91.9 us  [shift(): return lax.ppermute(x, axis, [(i, (i + step) % size) for i in range(size)])]
    add x13 -> x4, other arithmetic: 11.4 us -> 0.88 us  [the longest x1 0.85 us: on_device(): small = small + y]
    ppermute x30 -> x12, waiting for transfers between devices: 47.6 us -> 38 us  [send_lo(): return lax.ppermute(x, (XX, CORE), pairs)]
    unnamed x244 -> x242, local copies, waits for them, and re-layouts: 35 us -> 41.5 us
    ppermute x104 -> x82, waiting for transfers between devices: 251 us -> 257 us  [shift(): return lax.ppermute(x, axis, [(i, (i + step) % size) for i in range(size)])]
    pallas_call x40 -> x39, Pallas kernels: 104 us -> 107 us  [run(): pl.pallas_call(kernel, out_shape=tuple(outs), in_specs=[pl.BlockSpec(memo...]
  transfers between devices with their start and end apart: 138 -> 101, of which waited for: 63 -> 48; matrix products, arithmetic and copies ran while one was open for 5% -> 4% of each run, Pallas kernels for 14% -> 16%
where the time goes in v3:
time: 611 us; the launch traced here: 602 us
  waiting for transfers between devices  295 us (48%)
  starting transfers between devices  116 us (19%)
  Pallas kernels  108 us (18%)
  local copies, waits for them, and re-layouts  48.7 us (8%)
  other arithmetic  18.4 us (3%)
  between operations  15.8 us (3%)
    ppermute x82, waiting for transfers between devices, shift(): return lax.ppermute(x, axis, [(i, (i + step) % size) for i in range(size)])  257 us
    pallas_call x39, Pallas kernels, run(): pl.pallas_call(kernel, out_shape=tuple(outs), in_specs=[pl.BlockSpec(memo...  107 us
    ppermute x82, starting transfers between devices, shift(): return lax.ppermute(x, axis, [(i, (i + step) % size) for i in range(size)])  91.9 us
    unnamed x242, local copies, waits for them, and re-layouts  41.5 us
    ppermute x12, waiting for transfers between devices, send_lo(): return lax.ppermute(x, (XX, CORE), pairs)  38 us
  transfers between devices with their start and end apart: 101, of which 48 were waited for; matrix products, arithmetic and copies ran while one was open for 4% of the time, Pallas kernels for 16%

profile of v3, /device:TPU:0, one launch (start us, length us, event | category | flops | bytes accessed | tf_op | source)
XLA Modules:
  0.0 602.2 jit_solution(8399648149563169069)
XLA Ops:
  31.9 12.5 %collective-permute-done.10.refs_1_ = bf16[144,1024]{1,0:T(8,128)(2,1)S(1)} collective-permute-done((bf16[144,1024]{1,0:T(8,128)(2,1)S(1)}, bf16[144,1024]{1,0:T(8,128)(2,1)S(1)}, u32[]{:S(2)}, u32[]{:S(2)}) %collective-permute-start.10) | collective-permute-done | bytes 294944 | tf_op jit(solution)/shard_map/ppermute | solution.py:77
  44.5 3.8 collective-permute-start.12
  60.3 6.1 %collective-permute-done.14.refs_3_ = bf16[144,1024]{1,0:T(8,128)(2,1)S(1)} collective-permute-done((bf16[144,1024]{1,0:T(8,128)(2,1)S(1)}, bf16[144,1024]{1,0:T(8,128)(2,1)S(1)}, u32[]{:S(2)}, u32[]{:S(2)}) %collective-permute-start.14) | collective-permute-done | bytes 294944 | tf_op jit(solution)/shard_map/ppermute | solution.py:77
  68.0 6.3 %collective-permute-done.16.refs_7_ = bf16[144,1024]{1,0:T(8,128)(2,1)S(1)} collective-permute-done((bf16[144,1024]{1,0:T(8,128)(2,1)S(1)}, bf16[144,1024]{1,0:T(8,128)(2,1)S(1)}, u32[]{:S(2)}, u32[]{:S(2)}) %collective-permute-start.16) | collective-permute-done | bytes 294944 | tf_op jit(solution)/shard_map/ppermute | solution.py:77
  77.0 3.7 collective-permute-start.23
  81.6 12.8 %collective-permute-done.9.refs_1_ = bf16[128,2048]{1,0:T(8,128)(2,1)} collective-permute-done((bf16[128,2048]{1,0:T(8,128)(2,1)S(1)}, bf16[128,2048]{1,0:T(8,128)(2,1)}, u32[]{:S(2)}, u32[]{:S(2)}) %collective-permute-start.9) | collective-permute-done | bytes 524320 | tf_op jit(solution)/shard_map/ppermute | solution.py:77
  96.3 8.5 %shard_map.227 = (bf16[1024,768]{1,0:T(8,128)(2,1)S(1)}, f32[256,1024]{1,0:T(8,128)S(1)}, f32[2,1024]{1,0:T(2,128)S(1)}, f32[1,1024]{1,0:T(1,128)S(1)}, f32[1024...) custom-call(s32[4]{0:T(128)S(1)} %pad_add_fusion.me.rest_0_, ...), custom_call_target="tpu_custom_call" | custom-call | flops 2415919104 | bytes 9635840 | tf_op jit(solution)/shard_map/pallas_call | solution.py:44
  111.7 4.1 collective-permute-start.18
  121.6 4.5 collective-permute-done.19.refs_3_
  132.1 7.5 %collective-permute-done.31.refs_3_ = bf16[128,2048]{1,0:T(8,128)(2,1)S(1)} collective-permute-done((bf16[128,2048]{1,0:T(8,128)(2,1)}, bf16[128,2048]{1,0:T(8,128)(2,1)S(1)}, u32[]{:S(2)}, u32[]{:S(2)}) %collective-permute-start.31) | collective-permute-done | bytes 524320 | tf_op jit(solution)/shard_map/ppermute | solution.py:77
  146.4 9.9 %collective-permute-done.33.refs_7_ = bf16[128,2048]{1,0:T(8,128)(2,1)S(1)} collective-permute-done((bf16[128,2048]{1,0:T(8,128)(2,1)S(1)}, bf16[128,2048]{1,0:T(8,128)(2,1)S(1)}, u32[]{:S(2)}, u32[]{:S(2)}) %collective-permute-start.33) | collective-permute-done | bytes 524320 | tf_op jit(solution)/shard_map/ppermute | solution.py:77
  158.0 3.6 shard_map.231
  162.5 3.6 shard_map.232
  169.1 13.3 %collective-permute-done.35.refs_1_ = bf16[256,1024]{1,0:T(8,128)(2,1)S(1)} collective-permute-done((bf16[256,1024]{1,0:T(8,128)(2,1)S(1)}, bf16[256,1024]{1,0:T(8,128)(2,1)S(1)}, u32[]{:S(2)}, u32[]{:S(2)}) %collective-permute-start.35) | collective-permute-done | bytes 524320 | tf_op jit(solution)/shard_map/ppermute | solution.py:77
  188.2 4.9 collective-permute-done.40.refs_1_
  196.4 7.4 %collective-permute-done.38.refs_2_.rest_3_ = bf16[256,1024]{1,0:T(8,128)(2,1)} collective-permute-done((bf16[256,1024]{1,0:T(8,128)(2,1)}, bf16[256,1024]{1,0:T(8,128)(2,1)}, u32[]{:S(2)}, u32[]{:S(2)}) %collective-permute-start.38) | collective-permute-done | bytes 524320 | tf_op jit(solution)/shard_map/ppermute | solution.py:77
  204.8 14.0 %collective-permute-done.46.refs_2_ = bf16[2,4,32,1024]{3,2,1,0:T(8,128)(2,1)S(1)} collective-permute-done((bf16[2,4,32,1024]{3,2,1,0:T(8,128)(2,1)S(1)}, bf16[2,4,32,1024]{3,2,1,0:T(8,128)(2,1)S(1)}, u32[]{:S(2)}, u32[]{:S(2)}) %collective-permute-start.46) | collective-permute-done | bytes 524320 | tf_op jit(solution)/shard_map/ppermute | solution.py:77
  221.4 7.6 %shard_map.235 = (bf16[1024,768]{1,0:T(8,128)(2,1)S(1)}, f32[256,1024]{1,0:T(8,128)S(1)}, f32[2,1024]{1,0:T(2,128)S(1)}, bf16[256,256]{1,0:T(8,128)(2,1)S(1)}, b...) custom-call(s32[4]{0:T(128)S(1)} %pad_add_fusion.me.rest_0_, ...), custom_call_target="tpu_custom_call" | custom-call | flops 2415919104 | bytes 7358464 | tf_op jit(solution)/shard_map/pallas_call | solution.py:44
  233.7 4.0 collective-permute-done.42.refs_2_
  242.6 12.5 %collective-permute-done.50.refs_0_.rest_3_ = bf16[256,1024]{1,0:T(8,128)(2,1)S(1)} collective-permute-done((bf16[256,1024]{1,0:T(8,128)(2,1)S(1)}, bf16[256,1024]{1,0:T(8,128)(2,1)S(1)}, u32[]{:S(2)}, u32[]{:S(2)}) %collective-permute-start.50) | collective-permute-done | bytes 524320 | tf_op jit(solution)/shard_map/ppermute | solution.py:77
  256.0 3.6 shard_map.239
  259.7 3.8 shard_map.240
  267.9 12.2 %collective-permute-done.53.refs_1_ = bf16[256,1024]{1,0:T(8,128)(2,1)S(1)} collective-permute-done((bf16[256,1024]{1,0:T(8,128)(2,1)S(1)}, bf16[256,1024]{1,0:T(8,128)(2,1)S(1)}, u32[]{:S(2)}, u32[]{:S(2)}) %collective-permute-start.53) | collective-permute-done | bytes 524320 | tf_op jit(solution)/shard_map/ppermute | solution.py:77
  289.7 5.5 shard_map.244
  297.1 5.0 collective-permute-done.57.refs_1_
  313.4 7.3 %collective-permute-done.60 = bf16[2,256,256]{2,1,0:T(8,128)(2,1)S(1)} collective-permute-done((bf16[2,256,256]{2,1,0:T(8,128)(2,1)}, bf16[2,256,256]{2,1,0:T(8,128)(2,1)S(1)}, u32[]{:S(2)}, u32[]{:S(2)}) %collective-permute-start.60) | collective-permute-done | bytes 262176 | tf_op jit(solution)/shard_map/ppermute | solution.py:77
  325.9 7.8 %shard_map.247 = (bf16[256,768]{1,0:T(8,128)(2,1)S(1)}, bf16[256,768]{1,0:T(8,128)(2,1)S(1)}, bf16[256,768]{1,0:T(8,128)(2,1)S(1)}, bf16[256,768]{1,0:T(8,128)(2...) custom-call(s32[4]{0:T(128)S(1)} %pad_add_fusion.me.rest_0_, ...), custom_call_target="tpu_custom_call" | custom-call | flops 3221225472 | bytes 9449472 | tf_op jit(solution)/shard_map/pallas_call | solution.py:44
  337.9 12.7 %collective-permute-done.65 = bf16[2,4,32,1024]{3,2,1,0:T(8,128)(2,1)S(1)} collective-permute-done((bf16[2,4,32,1024]{3,2,1,0:T(8,128)(2,1)S(1)}, bf16[2,4,32,1024]{3,2,1,0:T(8,128)(2,1)S(1)}, u32[]{:S(2)}, u32[]{:S(2)}) %collective-permute-start.65) | collective-permute-done | bytes 524320 | tf_op jit(solution)/shard_map/ppermute | solution.py:77
  352.2 3.5 shard_map.248
  357.1 4.0 collective-permute-done.63.refs_1_
  363.9 11.6 %collective-permute-done.67.refs_0_.refs_14_ = bf16[256,1024]{1,0:T(8,128)(2,1)S(1)} collective-permute-done((bf16[256,1024]{1,0:T(8,128)(2,1)S(1)}, bf16[256,1024]{1,0:T(8,128)(2,1)S(1)}, u32[]{:S(2)}, u32[]{:S(2)}) %collective-permute-start.67) | collective-permute-done | bytes 524320 | tf_op jit(solution)/shard_map/ppermute | solution.py:77
  384.7 6.6 %shard_map.252 = (f32[1,1024]{1,0:T(1,128)S(1)}, bf16[4,8,32,1024]{3,2,1,0:T(8,128)(2,1)S(1)}, bf16[4,8,32,1024]{3,2,1,0:T(8,128)(2,1)}) custom-call(s32[4]{0:T(128)S(1)} %pad_add_fusion.me.rest_0_, bf16[256,1024]{1,0:T(8,128)(2,1)S(1)} %copy-done.64, bf16[256,1024]{1,0:T(8,128)(2,1)S(1)} %copy-done.68, bf16[256,1024]{1,0:T(8,128)(2,1)S(1)} %copy-done.66, ...), custom_call_target="tpu_custom_call" | custom-call | flops 4294967296 | bytes 12587008 | tf_op jit(solution)/shard_map/pallas_call | solution.py:44
  392.6 4.5 collective-permute-done.70.refs_1_
  404.9 6.4 %collective-permute-done.73 = bf16[2,256,256]{2,1,0:T(8,128)(2,1)S(1)} collective-permute-done((bf16[2,256,256]{2,1,0:T(8,128)(2,1)S(1)}, bf16[2,256,256]{2,1,0:T(8,128)(2,1)S(1)}, u32[]{:S(2)}, u32[]{:S(2)}) %collective-permute-start.73) | collective-permute-done | bytes 262176 | tf_op jit(solution)/shard_map/ppermute | solution.py:77
  412.5 8.8 %shard_map.255 = (bf16[256,768]{1,0:T(8,128)(2,1)S(1)}, bf16[256,768]{1,0:T(8,128)(2,1)S(1)}, bf16[256,768]{1,0:T(8,128)(2,1)S(1)}, bf16[256,768]{1,0:T(8,128)(2...) custom-call(s32[4]{0:T(128)S(1)} %pad_add_fusion.me.rest_0_, ...), custom_call_target="tpu_custom_call" | custom-call | flops 3221225472 | bytes 9449472 | tf_op jit(solution)/shard_map/pallas_call | solution.py:44
  431.4 12.5 %collective-permute-done.78 = bf16[2,4,32,1024]{3,2,1,0:T(8,128)(2,1)S(1)} collective-permute-done((bf16[2,4,32,1024]{3,2,1,0:T(8,128)(2,1)}, bf16[2,4,32,1024]{3,2,1,0:T(8,128)(2,1)S(1)}, u32[]{:S(2)}, u32[]{:S(2)}) %collective-permute-start.78) | collective-permute-done | bytes 524320 | tf_op jit(solution)/shard_map/ppermute | solution.py:77
  445.3 3.7 shard_map.256
  452.3 6.6 %collective-permute-done.79 = bf16[4,8,32,1024]{3,2,1,0:T(8,128)(2,1)} collective-permute-done((bf16[4,8,32,1024]{3,2,1,0:T(8,128)(2,1)}, bf16[4,8,32,1024]{3,2,1,0:T(8,128)(2,1)}, u32[]{:S(2)}, u32[]{:S(2)}) %collective-permute-start.79) | collective-permute-done | bytes 2097184 | tf_op jit(solution)/shard_map/ppermute | solution.py:77
  458.9 3.5 fusion.8
  462.4 4.5 collective-permute-start.81
  480.3 24.6 %collective-permute-done.82.refs_2_ = bf16[8,32,1024]{2,1,0:T(8,128)(2,1)} collective-permute-done((bf16[8,32,1024]{2,1,0:T(8,128)(2,1)}, bf16[8,32,1024]{2,1,0:T(8,128)(2,1)}, u32[]{:S(2)}, u32[]{:S(2)}) %collective-permute-start.82) | collective-permute-done | bytes 524320 | tf_op jit(solution)/shard_map/ppermute | solution.py:77
  509.9 14.9 %collective-permute-start.85 = (bf16[4,32,1024]{2,1,0:T(8,128)(2,1)}, bf16[4,32,1024]{2,1,0:T(8,128)(2,1)S(1)}, u32[]{:S(2)}, u32[]{:S(2)}) collective-permute-start(bf16[4,32,1024]{2,1,0:T(8,128)(2,1)} %get-tuple-element.482), channel_id=1, source_target_pairs={{0,1},{1,2},{2,3},{3,0},{4,5},{5,6},{6,7},{7,4},{8,9},{9,10},{10,1... | collective-permute-start | bytes 786440 | tf_op jit(solution)/shard_map/ppermute | solution.py:77
  524.9 3.5 collective-permute-start.86
  535.2 5.5 collective-permute-done.94
  540.6 7.1 %collective-permute-done.95 = f32[16,1024]{1,0:T(8,128)S(1)} collective-permute-done((f32[16,1024]{1,0:T(8,128)S(1)}, f32[16,1024]{1,0:T(8,128)S(1)}, u32[]{:S(2)}, u32[]{:S(2)}) %collective-permute-start.95) | collective-permute-done | bytes 65568 | tf_op jit(solution)/shard_map/ppermute | solution.py:77
  547.7 9.4 %collective-permute-start.84 = (bf16[2,256,1024]{2,1,0:T(8,128)(2,1)}, bf16[2,256,1024]{2,1,0:T(8,128)(2,1)}, u32[]{:S(2)}, u32[]{:S(2)}) collective-permute-start(bf16[2,256,1024]{2,1,0:T(8,128)(2,1)} %pad_maximum_fusion), channel_id=1, source_target_pairs={{0,0},{1,8},{2,4},{3,12},{8,1},{9,9},{10,5},{11,13},{4,2},{5,10},{... | collective-permute-start | bytes 3145736 | tf_op jit(solution)/shard_map/ppermute | solution.py:1010
  567.4 7.8 %collective-permute-done.89.refs_2_ = bf16[64,1792]{1,0:T(8,128)(2,1)S(1)} collective-permute-done((bf16[64,1792]{1,0:T(8,128)(2,1)S(1)}, bf16[64,1792]{1,0:T(8,128)(2,1)S(1)}, u32[]{:S(2)}, u32[]{:S(2)}) %collective-permute-start.89) | collective-permute-done | bytes 229408 | tf_op jit(solution)/shard_map/ppermute | solution.py:107
  575.2 18.2 %collective-permute-done.90.refs_3_ = bf16[64,1792]{1,0:T(8,128)(2,1)S(1)} collective-permute-done((bf16[64,1792]{1,0:T(8,128)(2,1)S(1)}, bf16[64,1792]{1,0:T(8,128)(2,1)S(1)}, u32[]{:S(2)}, u32[]{:S(2)}) %collective-permute-start.90) | collective-permute-done | bytes 229408 | tf_op jit(solution)/shard_map/ppermute | solution.py:107
  (493 shorter events, 210.6 us)
Async XLA Ops:
  7.2 108.7 %all-gather.5.cloned.1.call-start = ((), (), s32[]{:S(2)}) async-start(), calls=%async_computation.4 | async-start | bytes 1310720 | tf_op jit(solution)/shard_map/all_gather | solution.py:1025
  18.2 26.3 %collective-permute-start = (bf16[272,1024]{1,0:T(8,128)(2,1)S(1)}, bf16[272,1024]{1,0:T(8,128)(2,1)S(1)}, u32[]{:S(2)}, u32[]{:S(2)}) collective-permute-start(bf16[272,1024]{1,0:T(8,128)(2,1)S(1)} %shard_map.220), channel_id=1, source_target_pairs={{0,0},{1,8},{2,4},{3,12},{8,1},{9,9},{10,5},{11,13},{4,2},{5,10},{... | collective-permute-start | bytes 1671176 | tf_op jit(solution)/shard_map/ppermute | solution.py:1010
  27.2 24.9 %collective-permute-start.8 = (bf16[2,32,2816]{2,1,0:T(8,128)(2,1)S(1)}, bf16[2,32,2816]{2,1,0:T(8,128)(2,1)S(1)}, u32[]{:S(2)}, u32[]{:S(2)}) collective-permute-start(bf16[2,32,2816]{2,1,0:T(8,128)(2,1)S(1)} %pad_maximum_fusion.1), channel_id=1, source_target_pairs={{0,8},{8,0},{1,9},{9,1},{2,10},{10,2},{3,11},{11,3},{4,12},{12,4},... | collective-permute-start | bytes 1081352 | tf_op jit(solution)/shard_map/ppermute | solution.py:77
  30.4 23.3 %collective-permute-start.11 = (bf16[144,1024]{1,0:T(8,128)(2,1)S(1)}, bf16[144,1024]{1,0:T(8,128)(2,1)S(1)}, u32[]{:S(2)}, u32[]{:S(2)}) collective-permute-start(bf16[144,1024]{1,0:T(8,128)(2,1)S(1)} %shard_map.224.refs_0_), channel_id=1, source_target_pairs={{0,16},{16,0},{1,17},{17,1},{2,18},{18,2},{3,19},{19,3},{4,20},{20... | collective-permute-start | bytes 884744 | tf_op jit(solution)/shard_map/ppermute | solution.py:77
  55.9 129.5 %all-gather.7.cloned.1.call-start = ((), (), s32[]{:S(2)}) async-start(), calls=%async_computation.5 | async-start | bytes 2621440 | tf_op jit(solution)/shard_map/all_gather | solution.py:1025
  67.9 26.4 %collective-permute-start.9 = (bf16[128,2048]{1,0:T(8,128)(2,1)S(1)}, bf16[128,2048]{1,0:T(8,128)(2,1)}, u32[]{:S(2)}, u32[]{:S(2)}) collective-permute-start(bf16[128,2048]{1,0:T(8,128)(2,1)S(1)} %get-tuple-element.252.refs_0_), channel_id=1, source_target_pairs={{0,1},{1,2},{2,3},{3,0},{4,5},{5,6},{6,7},{7,4},{8,9},{9,10},{10,1... | collective-permute-start | bytes 1572872 | tf_op jit(solution)/shard_map/ppermute | solution.py:77
  67.9 26.4 %collective-permute-start.1 = (bf16[272,1024]{1,0:T(8,128)(2,1)S(1)}, bf16[272,1024]{1,0:T(8,128)(2,1)}, u32[]{:S(2)}, u32[]{:S(2)}) collective-permute-start(bf16[272,1024]{1,0:T(8,128)(2,1)S(1)} %collective-permute-done.refs_0_.refs_6_.refs_4_), channel_id=1, source_target_pairs={{0,4},{4,0},{1,5},{5,1},{2,6},{6,2},{3,7},{7,3},{8,12},{12,8},{9,1... | collective-permute-start | bytes 1671176 | tf_op jit(solution)/shard_map/ppermute | solution.py:77
  77.0 17.5 %collective-permute-start.23 = (bf16[2,4,32,1024]{3,2,1,0:T(8,128)(2,1)}, bf16[2,4,32,1024]{3,2,1,0:T(8,128)(2,1)}, u32[]{:S(2)}, u32[]{:S(2)}) collective-permute-start(bf16[2,4,32,1024]{3,2,1,0:T(8,128)(2,1)} %get-tuple-element.275.refs_0_), channel_id=1, source_target_pairs={{0,8},{8,0},{1,9},{9,1},{2,10},{10,2},{3,11},{11,3},{4,12},{12,4},... | collective-permute-start | bytes 1572872 | tf_op jit(solution)/shard_map/ppermute | solution.py:77
  80.7 15.6 %collective-permute-start.3 = (bf16[272,1024]{1,0:T(8,128)(2,1)}, bf16[272,1024]{1,0:T(8,128)(2,1)}, u32[]{:S(2)}, u32[]{:S(2)}) collective-permute-start(bf16[272,1024]{1,0:T(8,128)(2,1)} %collective-permute-done.2.refs_2_), channel_id=1, source_target_pairs={{0,4},{4,0},{1,5},{5,1},{2,6},{6,2},{3,7},{7,3},{8,12},{12,8},{9,1... | collective-permute-start | bytes 1671176 | tf_op jit(solution)/shard_map/ppermute | solution.py:77
  80.7 31.1 %collective-permute-start.20 = (bf16[128,2048]{1,0:T(8,128)(2,1)S(1)}, bf16[128,2048]{1,0:T(8,128)(2,1)}, u32[]{:S(2)}, u32[]{:S(2)}) collective-permute-start(bf16[128,2048]{1,0:T(8,128)(2,1)S(1)} %get-tuple-element.252.refs_0_), channel_id=1, source_target_pairs={{0,16},{16,0},{1,17},{17,1},{2,18},{18,2},{3,19},{19,3},{4,20},{20... | collective-permute-start | bytes 1572872 | tf_op jit(solution)/shard_map/ppermute | solution.py:77
  94.4 21.5 %collective-permute-start.21 = (bf16[128,2048]{1,0:T(8,128)(2,1)}, bf16[128,2048]{1,0:T(8,128)(2,1)}, u32[]{:S(2)}, u32[]{:S(2)}) collective-permute-start(bf16[128,2048]{1,0:T(8,128)(2,1)} %collective-permute-done.9.refs_1_), channel_id=1, source_target_pairs={{0,1},{1,2},{2,3},{3,0},{4,5},{5,6},{6,7},{7,4},{8,9},{9,10},{10,1... | collective-permute-start | bytes 1572872 | tf_op jit(solution)/shard_map/ppermute | solution.py:77
  94.4 31.7 %collective-permute-start.22 = (bf16[2,4,32,1024]{3,2,1,0:T(8,128)(2,1)}, bf16[2,4,32,1024]{3,2,1,0:T(8,128)(2,1)}, u32[]{:S(2)}, u32[]{:S(2)}) collective-permute-start(bf16[2,4,32,1024]{3,2,1,0:T(8,128)(2,1)} %get-tuple-element.275.refs_0_), channel_id=1, source_target_pairs={{0,4},{4,0},{1,5},{5,1},{2,6},{6,2},{3,7},{7,3},{8,12},{12,8},{9,1... | collective-permute-start | bytes 1572872 | tf_op jit(solution)/shard_map/ppermute | solution.py:77
  94.5 31.6 %collective-permute-start.24 = (bf16[2,4,32,1024]{3,2,1,0:T(8,128)(2,1)}, bf16[2,4,32,1024]{3,2,1,0:T(8,128)(2,1)}, u32[]{:S(2)}, u32[]{:S(2)}) collective-permute-start(bf16[2,4,32,1024]{3,2,1,0:T(8,128)(2,1)} %collective-permute-done.23.refs_2_), channel_id=1, source_target_pairs={{0,4},{4,0},{1,5},{5,1},{2,6},{6,2},{3,7},{7,3},{8,12},{12,8},{9,1... | collective-permute-start | bytes 1572872 | tf_op jit(solution)/shard_map/ppermute | solution.py:77
  115.9 310.1 %reduce-scatter.3.cloned.1.call-start = ((), (), s32[]{:S(2)}) async-start(), calls=%async_computation.2 | async-start | bytes 4718592 | tf_op jit(solution)/shard_map/reduce_scatter | solution.py:1131
  115.9 16.2 %collective-permute-start.30 = (bf16[128,2048]{1,0:T(8,128)(2,1)}, bf16[128,2048]{1,0:T(8,128)(2,1)S(1)}, u32[]{:S(2)}, u32[]{:S(2)}) collective-permute-start(bf16[128,2048]{1,0:T(8,128)(2,1)} %collective-permute-done.9.refs_1_), channel_id=1, source_target_pairs={{0,16},{16,0},{1,17},{17,1},{2,18},{18,2},{3,19},{19,3},{4,20},{20... | collective-permute-start | bytes 1572872 | tf_op jit(solution)/shard_map/ppermute | solution.py:77
  117.4 22.2 %collective-permute-start.31 = (bf16[128,2048]{1,0:T(8,128)(2,1)}, bf16[128,2048]{1,0:T(8,128)(2,1)S(1)}, u32[]{:S(2)}, u32[]{:S(2)}) collective-permute-start(bf16[128,2048]{1,0:T(8,128)(2,1)} %collective-permute-done.21.refs_2_), channel_id=1, source_target_pairs={{0,1},{1,2},{2,3},{3,0},{4,5},{5,6},{6,7},{7,4},{8,9},{9,10},{10,1... | collective-permute-start | bytes 1572872 | tf_op jit(solution)/shard_map/ppermute | solution.py:77
  131.4 15.0 %collective-permute-start.32 = (bf16[128,2048]{1,0:T(8,128)(2,1)}, bf16[128,2048]{1,0:T(8,128)(2,1)S(1)}, u32[]{:S(2)}, u32[]{:S(2)}) collective-permute-start(bf16[128,2048]{1,0:T(8,128)(2,1)} %collective-permute-done.21.refs_2_), channel_id=1, source_target_pairs={{0,16},{16,0},{1,17},{17,1},{2,18},{18,2},{3,19},{19,3},{4,20},{20... | collective-permute-start | bytes 1572872 | tf_op jit(solution)/shard_map/ppermute | solution.py:77
  139.6 16.7 %collective-permute-start.33 = (bf16[128,2048]{1,0:T(8,128)(2,1)S(1)}, bf16[128,2048]{1,0:T(8,128)(2,1)S(1)}, u32[]{:S(2)}, u32[]{:S(2)}) collective-permute-start(bf16[128,2048]{1,0:T(8,128)(2,1)S(1)} %collective-permute-done.31.refs_3_), channel_id=1, source_target_pairs={{0,16},{16,0},{1,17},{17,1},{2,18},{18,2},{3,19},{19,3},{4,20},{20... | collective-permute-start | bytes 1572872 | tf_op jit(solution)/shard_map/ppermute | solution.py:77
  143.8 18.7 %collective-permute-start.27 = (bf16[256,1024]{1,0:T(8,128)(2,1)S(1)}, bf16[256,1024]{1,0:T(8,128)(2,1)S(1)}, u32[]{:S(2)}, u32[]{:S(2)}) collective-permute-start(bf16[256,1024]{1,0:T(8,128)(2,1)S(1)} %collective-permute-done.26.refs_0_.refs_2_), channel_id=1, source_target_pairs={{0,4},{4,0},{1,5},{5,1},{2,6},{6,2},{3,7},{7,3},{8,12},{12,8},{9,1... | collective-permute-start | bytes 1572872 | tf_op jit(solution)/shard_map/ppermute | solution.py:77
  166.8 26.3 %collective-permute-start.40 = (bf16[4,128,1024]{2,1,0:T(8,128)(2,1)}, bf16[4,128,1024]{2,1,0:T(8,128)(2,1)}, u32[]{:S(2)}, u32[]{:S(2)}) collective-permute-start(bf16[4,128,1024]{2,1,0:T(8,128)(2,1)} %bitcast.14.refs_0_), channel_id=1, source_target_pairs={{0,16},{16,0},{1,17},{17,1},{2,18},{18,2},{3,19},{19,3},{4,20},{20... | collective-permute-start | bytes 3145736 | tf_op jit(solution)/shard_map/ppermute | solution.py:77
  184.7 19.1 %collective-permute-start.38 = (bf16[256,1024]{1,0:T(8,128)(2,1)}, bf16[256,1024]{1,0:T(8,128)(2,1)}, u32[]{:S(2)}, u32[]{:S(2)}) collective-permute-start(bf16[256,1024]{1,0:T(8,128)(2,1)} %get-tuple-element.293.refs_0_.rest_1_), channel_id=1, source_target_pairs={{0,8},{8,0},{1,9},{9,1},{2,10},{10,2},{3,11},{11,3},{4,12},{12,4},... | collective-permute-start | bytes 1572872 | tf_op jit(solution)/shard_map/ppermute | solution.py:77
  185.4 69.8 %collective-permute-start.49 = (bf16[4,128,2048]{2,1,0:T(8,128)(2,1)}, bf16[4,128,2048]{2,1,0:T(8,128)(2,1)S(1)}, u32[]{:S(2)}, u32[]{:S(2)}) collective-permute-start(bf16[4,128,2048]{2,1,0:T(8,128)(2,1)} %bitcast.120), channel_id=1, source_target_pairs={{0,16},{16,0},{1,17},{17,1},{2,18},{18,2},{3,19},{19,3},{4,20},{20... | collective-permute-start | bytes 6291464 | tf_op jit(solution)/shard_map/ppermute | solution.py:77
  186.1 17.7 %collective-permute-start.28 = (bf16[256,1024]{1,0:T(8,128)(2,1)}, bf16[256,1024]{1,0:T(8,128)(2,1)S(1)}, u32[]{:S(2)}, u32[]{:S(2)}) collective-permute-start(bf16[256,1024]{1,0:T(8,128)(2,1)} %bitcast.153), channel_id=1, source_target_pairs={{0,0},{1,8},{2,4},{3,12},{8,1},{9,9},{10,5},{11,13},{4,2},{5,10},{... | collective-permute-start | bytes 1572872 | tf_op jit(solution)/shard_map/ppermute | solution.py:1010
  194.9 24.0 %collective-permute-start.46 = (bf16[2,4,32,1024]{3,2,1,0:T(8,128)(2,1)S(1)}, bf16[2,4,32,1024]{3,2,1,0:T(8,128)(2,1)S(1)}, u32[]{:S(2)}, u32[]{:S(2)}) collective-permute-start(bf16[2,4,32,1024]{3,2,1,0:T(8,128)(2,1)S(1)} %get-tuple-element.308.refs_0_), channel_id=1, source_target_pairs={{0,8},{8,0},{1,9},{9,1},{2,10},{10,2},{3,11},{11,3},{4,12},{12,4},... | collective-permute-start | bytes 1572872 | tf_op jit(solution)/shard_map/ppermute | solution.py:77
  195.8 23.0 %collective-permute-start.37 = (bf16[256,1024]{1,0:T(8,128)(2,1)}, bf16[256,1024]{1,0:T(8,128)(2,1)S(1)}, u32[]{:S(2)}, u32[]{:S(2)}) collective-permute-start(bf16[256,1024]{1,0:T(8,128)(2,1)} %get-tuple-element.293.refs_0_.rest_1_), channel_id=1, source_target_pairs={{0,4},{4,0},{1,5},{5,1},{2,6},{6,2},{3,7},{7,3},{8,12},{12,8},{9,1... | collective-permute-start | bytes 1572872 | tf_op jit(solution)/shard_map/ppermute | solution.py:77
  203.8 15.0 %collective-permute-start.39 = (bf16[256,1024]{1,0:T(8,128)(2,1)}, bf16[256,1024]{1,0:T(8,128)(2,1)S(1)}, u32[]{:S(2)}, u32[]{:S(2)}) collective-permute-start(bf16[256,1024]{1,0:T(8,128)(2,1)} %collective-permute-done.38.refs_2_.rest_3_), channel_id=1, source_target_pairs={{0,4},{4,0},{1,5},{5,1},{2,6},{6,2},{3,7},{7,3},{8,12},{12,8},{9,1... | collective-permute-start | bytes 1572872 | tf_op jit(solution)/shard_map/ppermute | solution.py:77
  203.8 27.5 %collective-permute-start.45 = (bf16[2,4,32,1024]{3,2,1,0:T(8,128)(2,1)S(1)}, bf16[2,4,32,1024]{3,2,1,0:T(8,128)(2,1)S(1)}, u32[]{:S(2)}, u32[]{:S(2)}) collective-permute-start(bf16[2,4,32,1024]{3,2,1,0:T(8,128)(2,1)S(1)} %get-tuple-element.308.refs_0_), channel_id=1, source_target_pairs={{0,4},{4,0},{1,5},{5,1},{2,6},{6,2},{3,7},{7,3},{8,12},{12,8},{9,1... | collective-permute-start | bytes 1572872 | tf_op jit(solution)/shard_map/ppermute | solution.py:77
  218.9 20.3 %collective-permute-start.44 = (bf16[256,1024]{1,0:T(8,128)(2,1)S(1)}, bf16[256,1024]{1,0:T(8,128)(2,1)S(1)}, u32[]{:S(2)}, u32[]{:S(2)}) collective-permute-start(bf16[256,1024]{1,0:T(8,128)(2,1)S(1)} %collective-permute-done.28.refs_0_.rest_13_.refs_3_), channel_id=1, source_target_pairs={{0,8},{8,0},{1,9},{9,1},{2,10},{10,2},{3,11},{11,3},{4,12},{12,4},... | collective-permute-start | bytes 1572872 | tf_op jit(solution)/shard_map/ppermute | solution.py:77
  267.4 16.1 %collective-permute-start.55 = (bf16[256,1024]{1,0:T(8,128)(2,1)S(1)}, bf16[256,1024]{1,0:T(8,128)(2,1)S(1)}, u32[]{:S(2)}, u32[]{:S(2)}) collective-permute-start(bf16[256,1024]{1,0:T(8,128)(2,1)S(1)} %collective-permute-done.44.refs_0_.rest_15_), channel_id=1, source_target_pairs={{0,4},{4,0},{1,5},{5,1},{2,6},{6,2},{3,7},{7,3},{8,12},{12,8},{9,1... | collective-permute-start | bytes 1572872 | tf_op jit(solution)/shard_map/ppermute | solution.py:77
  311.7 248.0 %reduce-scatter.5.cloned.1.call-start = ((), (), s32[]{:S(2)}) async-start(), calls=%async_computation.3 | async-start | bytes 2359296 | tf_op jit(solution)/shard_map/reduce_scatter | solution.py:1131
  337.6 19.5 %collective-permute-start.64 = (bf16[256,1024]{1,0:T(8,128)(2,1)S(1)}, bf16[256,1024]{1,0:T(8,128)(2,1)S(1)}, u32[]{:S(2)}, u32[]{:S(2)}) collective-permute-start(bf16[256,1024]{1,0:T(8,128)(2,1)S(1)} %get-tuple-element.368), channel_id=1, source_target_pairs={{0,4},{4,0},{1,5},{5,1},{2,6},{6,2},{3,7},{7,3},{8,12},{12,8},{9,1... | collective-permute-start | bytes 1572872 | tf_op jit(solution)/shard_map/ppermute | solution.py:77
  337.6 23.5 %collective-permute-start.63 = (bf16[256,1024]{1,0:T(8,128)(2,1)S(1)}, bf16[256,1024]{1,0:T(8,128)(2,1)S(1)}, u32[]{:S(2)}, u32[]{:S(2)}) collective-permute-start(bf16[256,1024]{1,0:T(8,128)(2,1)S(1)} %add_convert_fusion.5), channel_id=1, source_target_pairs={{0,8},{8,0},{1,9},{9,1},{2,10},{10,2},{3,11},{11,3},{4,12},{12,4},... | collective-permute-start | bytes 1572872 | tf_op jit(solution)/shard_map/ppermute | solution.py:77
  404.4 54.4 %collective-permute-start.79 = (bf16[4,8,32,1024]{3,2,1,0:T(8,128)(2,1)}, bf16[4,8,32,1024]{3,2,1,0:T(8,128)(2,1)}, u32[]{:S(2)}, u32[]{:S(2)}) collective-permute-start(bf16[4,8,32,1024]{3,2,1,0:T(8,128)(2,1)} %get-tuple-element.449), channel_id=1, source_target_pairs={{0,16},{16,0},{1,17},{17,1},{2,18},{18,2},{3,19},{19,3},{4,20},{20... | collective-permute-start | bytes 6291464 | tf_op jit(solution)/shard_map/ppermute | solution.py:77
  431.4 37.5 %collective-permute-start.77 = (bf16[256,1024]{1,0:T(8,128)(2,1)}, bf16[256,1024]{1,0:T(8,128)(2,1)S(1)}, u32[]{:S(2)}, u32[]{:S(2)}) collective-permute-start(bf16[256,1024]{1,0:T(8,128)(2,1)} %copy-done.75), channel_id=1, source_target_pairs={{0,4},{4,0},{1,5},{5,1},{2,6},{6,2},{3,7},{7,3},{8,12},{12,8},{9,1... | collective-permute-start | bytes 1572872 | tf_op jit(solution)/shard_map/ppermute | solution.py:77
  450.0 57.2 %collective-permute-start.80 = (bf16[4,4,32,1024]{3,2,1,0:T(8,128)(2,1)}, bf16[4,4,32,1024]{3,2,1,0:T(8,128)(2,1)}, u32[]{:S(2)}, u32[]{:S(2)}) collective-permute-start(bf16[4,4,32,1024]{3,2,1,0:T(8,128)(2,1)} %get-tuple-element.457), channel_id=1, source_target_pairs={{0,16},{16,0},{1,17},{17,1},{2,18},{18,2},{3,19},{19,3},{4,20},{20... | collective-permute-start | bytes 3145736 | tf_op jit(solution)/shard_map/ppermute | solution.py:77
  450.7 21.1 %collective-permute-start.76 = (bf16[256,1024]{1,0:T(8,128)(2,1)S(1)}, bf16[256,1024]{1,0:T(8,128)(2,1)S(1)}, u32[]{:S(2)}, u32[]{:S(2)}) collective-permute-start(bf16[256,1024]{1,0:T(8,128)(2,1)S(1)} %add_convert_fusion.3), channel_id=1, source_target_pairs={{0,8},{8,0},{1,9},{9,1},{2,10},{10,2},{3,11},{11,3},{4,12},{12,4},... | collective-permute-start | bytes 1572872 | tf_op jit(solution)/shard_map/ppermute | solution.py:77
  462.4 17.2 %collective-permute-start.81 = (bf16[8,32,1024]{2,1,0:T(8,128)(2,1)}, bf16[8,32,1024]{2,1,0:T(8,128)(2,1)S(1)}, u32[]{:S(2)}, u32[]{:S(2)}) collective-permute-start(bf16[8,32,1024]{2,1,0:T(8,128)(2,1)} %get-tuple-element.478), channel_id=1, source_target_pairs={{0,1},{1,2},{2,3},{3,0},{4,5},{5,6},{6,7},{7,4},{8,9},{9,10},{10,1... | collective-permute-start | bytes 1572872 | tf_op jit(solution)/shard_map/ppermute | solution.py:77
  466.9 38.1 %collective-permute-start.82 = (bf16[8,32,1024]{2,1,0:T(8,128)(2,1)}, bf16[8,32,1024]{2,1,0:T(8,128)(2,1)}, u32[]{:S(2)}, u32[]{:S(2)}) collective-permute-start(bf16[8,32,1024]{2,1,0:T(8,128)(2,1)} %get-tuple-element.477), channel_id=1, source_target_pairs={{0,2},{1,3},{2,0},{3,1},{4,6},{5,7},{6,4},{7,5},{8,10},{9,11},{10,... | collective-permute-start | bytes 1572872 | tf_op jit(solution)/shard_map/ppermute | solution.py:77
  468.8 38.3 %collective-permute-start.83 = (bf16[8,32,1024]{2,1,0:T(8,128)(2,1)}, bf16[8,32,1024]{2,1,0:T(8,128)(2,1)}, u32[]{:S(2)}, u32[]{:S(2)}) collective-permute-start(bf16[8,32,1024]{2,1,0:T(8,128)(2,1)} %get-tuple-element.476), channel_id=1, source_target_pairs={{0,3},{1,0},{2,1},{3,2},{4,7},{5,4},{6,5},{7,6},{8,11},{9,8},{10,9... | collective-permute-start | bytes 1572872 | tf_op jit(solution)/shard_map/ppermute | solution.py:77
  476.1 33.7 %collective-permute-start.92 = (f32[12,1024]{1,0:T(8,128)S(1)}, f32[12,1024]{1,0:T(8,128)S(1)}, u32[]{:S(2)}, u32[]{:S(2)}) collective-permute-start(f32[12,1024]{1,0:T(8,128)S(1)} %add.153), channel_id=1, source_target_pairs={{0,8},{8,0},{1,9},{9,1},{2,10},{10,2},{3,11},{11,3},{4,12},{12,4},... | collective-permute-start | bytes 147464 | tf_op jit(solution)/shard_map/ppermute | solution.py:77
  509.9 18.5 %collective-permute-start.93 = (f32[16,1024]{1,0:T(8,128)S(1)}, f32[16,1024]{1,0:T(8,128)}, u32[]{:S(2)}, u32[]{:S(2)}) collective-permute-start(f32[16,1024]{1,0:T(8,128)S(1)} %concatenate.15), channel_id=1, source_target_pairs={{0,16},{16,0},{1,17},{17,1},{2,18},{18,2},{3,19},{19,3},{4,20},{20... | collective-permute-start | bytes 196616 | tf_op jit(solution)/shard_map/ppermute | solution.py:77
  509.9 49.7 %collective-permute-start.85 = (bf16[4,32,1024]{2,1,0:T(8,128)(2,1)}, bf16[4,32,1024]{2,1,0:T(8,128)(2,1)S(1)}, u32[]{:S(2)}, u32[]{:S(2)}) collective-permute-start(bf16[4,32,1024]{2,1,0:T(8,128)(2,1)} %get-tuple-element.482), channel_id=1, source_target_pairs={{0,1},{1,2},{2,3},{3,0},{4,5},{5,6},{6,7},{7,4},{8,9},{9,10},{10,1... | collective-permute-start | bytes 786440 | tf_op jit(solution)/shard_map/ppermute | solution.py:77
  524.9 34.8 %collective-permute-start.86 = (bf16[4,32,1024]{2,1,0:T(8,128)(2,1)}, bf16[4,32,1024]{2,1,0:T(8,128)(2,1)}, u32[]{:S(2)}, u32[]{:S(2)}) collective-permute-start(bf16[4,32,1024]{2,1,0:T(8,128)(2,1)} %get-tuple-element.481), channel_id=1, source_target_pairs={{0,2},{1,3},{2,0},{3,1},{4,6},{5,7},{6,4},{7,5},{8,10},{9,11},{10,... | collective-permute-start | bytes 786440 | tf_op jit(solution)/shard_map/ppermute | solution.py:77
  529.5 18.2 %collective-permute-start.95 = (f32[16,1024]{1,0:T(8,128)S(1)}, f32[16,1024]{1,0:T(8,128)S(1)}, u32[]{:S(2)}, u32[]{:S(2)}) collective-permute-start(f32[16,1024]{1,0:T(8,128)S(1)} %add.155), channel_id=1, source_target_pairs={{0,2},{1,3},{2,0},{3,1},{4,6},{5,7},{6,4},{7,5},{8,10},{9,11},{10,... | collective-permute-start | bytes 196616 | tf_op jit(solution)/shard_map/ppermute | solution.py:77
  532.9 24.2 %collective-permute-start.96 = (f32[16,1024]{1,0:T(8,128)S(1)}, f32[16,1024]{1,0:T(8,128)S(1)}, u32[]{:S(2)}, u32[]{:S(2)}) collective-permute-start(f32[16,1024]{1,0:T(8,128)S(1)} %add.155), channel_id=1, source_target_pairs={{0,3},{1,0},{2,1},{3,2},{4,7},{5,4},{6,5},{7,6},{8,11},{9,8},{10,9... | collective-permute-start | bytes 196616 | tf_op jit(solution)/shard_map/ppermute | solution.py:77
  540.6 19.0 %collective-permute-start.87 = (bf16[4,32,1024]{2,1,0:T(8,128)(2,1)}, bf16[4,32,1024]{2,1,0:T(8,128)(2,1)S(1)}, u32[]{:S(2)}, u32[]{:S(2)}) collective-permute-start(bf16[4,32,1024]{2,1,0:T(8,128)(2,1)} %get-tuple-element.480), channel_id=1, source_target_pairs={{0,3},{1,0},{2,1},{3,2},{4,7},{5,4},{6,5},{7,6},{8,11},{9,8},{10,9... | collective-permute-start | bytes 786440 | tf_op jit(solution)/shard_map/ppermute | solution.py:77
  547.7 17.5 %collective-permute-start.84 = (bf16[2,256,1024]{2,1,0:T(8,128)(2,1)}, bf16[2,256,1024]{2,1,0:T(8,128)(2,1)}, u32[]{:S(2)}, u32[]{:S(2)}) collective-permute-start(bf16[2,256,1024]{2,1,0:T(8,128)(2,1)} %pad_maximum_fusion), channel_id=1, source_target_pairs={{0,0},{1,8},{2,4},{3,12},{8,1},{9,9},{10,5},{11,13},{4,2},{5,10},{... | collective-permute-start | bytes 3145736 | tf_op jit(solution)/shard_map/ppermute | solution.py:1010
  564.8 28.6 %collective-permute-start.90 = (bf16[64,1792]{1,0:T(8,128)(2,1)S(1)}, bf16[64,1792]{1,0:T(8,128)(2,1)S(1)}, u32[]{:S(2)}, u32[]{:S(2)}) collective-permute-start(bf16[64,1792]{1,0:T(8,128)(2,1)S(1)} %get-tuple-element.466), channel_id=1, source_target_pairs={{0,12},{4,8},{8,4},{12,0},{1,13},{5,9},{9,5},{13,1},{2,14},{6,10},... | collective-permute-start | bytes 688136 | tf_op jit(solution)/shard_map/ppermute | solution.py:107
  (174 other events, 1689.3 us)
Sparse Core Ops, SparseCore 0:
  56.0 47.2 all-gather.4
  116.0 51.9 all-gather.6
  311.9 91.5 reduce-scatter.2
  426.1 87.6 reduce-scatter.4

commit v4 on v3

--- a/solution.py
+++ b/solution.py
@@ -711,17 +711,17 @@
     sums[0:1, :] = gains
     sums[1:2, :] = shifts
     sums[2:3, :] = jnp.sum(dy[...].astype(F32), axis=0, keepdims=True)
-    width = outs[0].shape[2]
-    for k, dc in slots_of(xs):
+    width = outs[0].shape[1]
+    for j, (k, dc) in enumerate(slots_of(xs)):
         off = pl.multiple_of(lo_plus(me, xs, k, dc) * width, width)
-        outs[dc][k] = nt(dy[...], w[pl.ds(off, width), :]).astype(BF)
+        outs[j][...] = nt(dy[...], w[pl.ds(off, width), :]).astype(BF)
 
 
 def mid_back(me, terms, grad, middle, vec, layer, w, ts, xs):
     n = middle.shape[0]
     got = run(
         functools.partial(mid_back_kernel, len(terms), ts, xs, 6 * layer + 3),
-        [shape((n, D), F32), shape((n, D), BF), shape((3, D), F32)] + [shape((xs, n, D // ts), BF)] * CORES,
+        [shape((n, D), F32), shape((n, D), BF), shape((3, D), F32)] + [shape((n, D // ts), BF)] * ts,
         [me],
         terms + [grad, middle, vec, w],
         flops=2 * n * D * D,
@@ -1165,14 +1165,9 @@
         else:
             f_sums[l] = scattered(f_parts[0])
         dh1, dy, mid_sums, d_heads = mid_back(me, terms, dh, middle, vec, l, w_out, ts, xs)
-        same, other = d_heads
-        other = shift(other, CORE, CORES, 1)
-        pairs = [jnp.stack([same[k], other[k]]) for k in range(1, xs)]
-        d_out = [same[0], other[0]]
-        for k in range(1, xs):
-            pair = shift(pairs[k - 1], XX, xs, k)
-            d_out += [pair[0], pair[1]]
-        out_part = wgrad_out(me, tie(own, pairs), dy, hs, xs)
+        by = exchange_lo(dict(zip(slots, d_heads)), xs, 1)
+        d_out = [by[s] for s in slots]
+        out_part = wgrad_out(me, own, dy, hs, xs)
         got = shift(out_part[1], CORE, CORES, 1)
         both = [(out_part[0, k].astype(F32) + got[k].astype(F32)) for k in range(xs)]
         o_sent = [both[k].astype(BF) for k in range(1, xs)]

time: 611 us -> 609 us (level)
    ppermute x82 -> x78, waiting for transfers between devices: 257 us -> 242 us  [shift(): return lax.ppermute(x, axis, [(i, (i + step) % size) for i in range(size)])]
    ppermute x12 -> x18, waiting for transfers between devices: 38 us -> 47.2 us  [send_lo(): return lax.ppermute(x, (XX, CORE), pairs)]
    ppermute x12 -> x18, starting transfers between devices: 12.1 us -> 16.1 us  [send_lo(): return lax.ppermute(x, (XX, CORE), pairs)]
    ppermute x82 -> x78, starting transfers between devices: 91.9 us -> 93.6 us  [shift(): return lax.ppermute(x, axis, [(i, (i + step) % size) for i in range(size)])]
    unnamed x242 -> x254, local copies, waits for them, and re-layouts: 41.5 us -> 42.4 us
  transfers between devices with their start and end apart: 101 -> 103, of which waited for: 48 -> 50; matrix products, arithmetic and copies ran while one was open for 4% -> 3% of each run, Pallas kernels for 16% -> 17%
where the time goes in v4:
time: 609 us; the launch traced here: 599 us
  waiting for transfers between devices  289 us (47%)
  starting transfers between devices  122 us (20%)
  Pallas kernels  109 us (18%)
  local copies, waits for them, and re-layouts  47 us (8%)
  other arithmetic  16.2 us (3%)
  between operations  15.8 us (3%)
    ppermute x78, waiting for transfers between devices, shift(): return lax.ppermute(x, axis, [(i, (i + step) % size) for i in range(size)])  242 us
    pallas_call x39, Pallas kernels, run(): pl.pallas_call(kernel, out_shape=tuple(outs), in_specs=[pl.BlockSpec(memo...  108 us
    ppermute x78, starting transfers between devices, shift(): return lax.ppermute(x, axis, [(i, (i + step) % size) for i in range(size)])  93.6 us
    ppermute x18, waiting for transfers between devices, send_lo(): return lax.ppermute(x, (XX, CORE), pairs)  47.2 us
    unnamed x254, local copies, waits for them, and re-layouts  42.4 us
    ppermute x18, starting transfers between devices, send_lo(): return lax.ppermute(x, (XX, CORE), pairs)  16.1 us
  transfers between devices with their start and end apart: 103, of which 50 were waited for; matrix products, arithmetic and copies ran while one was open for 3% of the time, Pallas kernels for 17%

profile of v4, /device:TPU:0, one launch (start us, length us, event | category | flops | bytes accessed | tf_op | source)
XLA Modules:
  0.0 599.4 jit_solution(1481815177972922387)
XLA Ops:
  31.9 12.5 %collective-permute-done.10.refs_1_ = bf16[144,1024]{1,0:T(8,128)(2,1)S(1)} collective-permute-done((bf16[144,1024]{1,0:T(8,128)(2,1)S(1)}, bf16[144,1024]{1,0:T(8,128)(2,1)S(1)}, u32[]{:S(2)}, u32[]{:S(2)}) %collective-permute-start.10) | collective-permute-done | bytes 294944 | tf_op jit(solution)/shard_map/ppermute | solution.py:77
  44.5 3.8 collective-permute-start.12
  60.3 6.1 %collective-permute-done.14.refs_3_ = bf16[144,1024]{1,0:T(8,128)(2,1)S(1)} collective-permute-done((bf16[144,1024]{1,0:T(8,128)(2,1)S(1)}, bf16[144,1024]{1,0:T(8,128)(2,1)S(1)}, u32[]{:S(2)}, u32[]{:S(2)}) %collective-permute-start.14) | collective-permute-done | bytes 294944 | tf_op jit(solution)/shard_map/ppermute | solution.py:77
  68.0 6.3 %collective-permute-done.16.refs_7_ = bf16[144,1024]{1,0:T(8,128)(2,1)S(1)} collective-permute-done((bf16[144,1024]{1,0:T(8,128)(2,1)S(1)}, bf16[144,1024]{1,0:T(8,128)(2,1)S(1)}, u32[]{:S(2)}, u32[]{:S(2)}) %collective-permute-start.16) | collective-permute-done | bytes 294944 | tf_op jit(solution)/shard_map/ppermute | solution.py:77
  77.0 3.7 collective-permute-start.23
  81.6 12.8 %collective-permute-done.9.refs_1_ = bf16[128,2048]{1,0:T(8,128)(2,1)} collective-permute-done((bf16[128,2048]{1,0:T(8,128)(2,1)S(1)}, bf16[128,2048]{1,0:T(8,128)(2,1)}, u32[]{:S(2)}, u32[]{:S(2)}) %collective-permute-start.9) | collective-permute-done | bytes 524320 | tf_op jit(solution)/shard_map/ppermute | solution.py:77
  96.3 8.5 %shard_map.227 = (bf16[1024,768]{1,0:T(8,128)(2,1)S(1)}, f32[256,1024]{1,0:T(8,128)S(1)}, f32[2,1024]{1,0:T(2,128)S(1)}, f32[1,1024]{1,0:T(1,128)S(1)}, f32[1024...) custom-call(s32[4]{0:T(128)S(1)} %pad_add_fusion.me.rest_0_, ...), custom_call_target="tpu_custom_call" | custom-call | flops 2415919104 | bytes 9635840 | tf_op jit(solution)/shard_map/pallas_call | solution.py:44
  111.8 4.1 collective-permute-start.18
  121.0 4.5 collective-permute-done.19.refs_3_
  131.5 8.7 %collective-permute-done.31.refs_3_ = bf16[128,2048]{1,0:T(8,128)(2,1)S(1)} collective-permute-done((bf16[128,2048]{1,0:T(8,128)(2,1)}, bf16[128,2048]{1,0:T(8,128)(2,1)S(1)}, u32[]{:S(2)}, u32[]{:S(2)}) %collective-permute-start.31) | collective-permute-done | bytes 524320 | tf_op jit(solution)/shard_map/ppermute | solution.py:77
  145.8 9.9 %collective-permute-done.33.refs_7_ = bf16[128,2048]{1,0:T(8,128)(2,1)S(1)} collective-permute-done((bf16[128,2048]{1,0:T(8,128)(2,1)S(1)}, bf16[128,2048]{1,0:T(8,128)(2,1)S(1)}, u32[]{:S(2)}, u32[]{:S(2)}) %collective-permute-start.33) | collective-permute-done | bytes 524320 | tf_op jit(solution)/shard_map/ppermute | solution.py:77
  157.4 3.6 shard_map.231
  161.9 3.6 shard_map.232
  168.6 13.3 %collective-permute-done.35.refs_1_ = bf16[256,1024]{1,0:T(8,128)(2,1)S(1)} collective-permute-done((bf16[256,1024]{1,0:T(8,128)(2,1)S(1)}, bf16[256,1024]{1,0:T(8,128)(2,1)S(1)}, u32[]{:S(2)}, u32[]{:S(2)}) %collective-permute-start.35) | collective-permute-done | bytes 524320 | tf_op jit(solution)/shard_map/ppermute | solution.py:77
  187.4 5.2 collective-permute-done.40.refs_1_
  196.8 6.5 %collective-permute-done.38.refs_2_.rest_3_ = bf16[256,1024]{1,0:T(8,128)(2,1)} collective-permute-done((bf16[256,1024]{1,0:T(8,128)(2,1)}, bf16[256,1024]{1,0:T(8,128)(2,1)}, u32[]{:S(2)}, u32[]{:S(2)}) %collective-permute-start.38) | collective-permute-done | bytes 524320 | tf_op jit(solution)/shard_map/ppermute | solution.py:77
  204.2 14.1 %collective-permute-done.46.refs_2_ = bf16[2,4,32,1024]{3,2,1,0:T(8,128)(2,1)S(1)} collective-permute-done((bf16[2,4,32,1024]{3,2,1,0:T(8,128)(2,1)S(1)}, bf16[2,4,32,1024]{3,2,1,0:T(8,128)(2,1)S(1)}, u32[]{:S(2)}, u32[]{:S(2)}) %collective-permute-start.46) | collective-permute-done | bytes 524320 | tf_op jit(solution)/shard_map/ppermute | solution.py:77
  220.9 7.6 %shard_map.235 = (bf16[1024,768]{1,0:T(8,128)(2,1)S(1)}, f32[256,1024]{1,0:T(8,128)S(1)}, f32[2,1024]{1,0:T(2,128)S(1)}, bf16[256,256]{1,0:T(8,128)(2,1)S(1)}, b...) custom-call(s32[4]{0:T(128)S(1)} %pad_add_fusion.me.rest_0_, ...), custom_call_target="tpu_custom_call" | custom-call | flops 2415919104 | bytes 7358464 | tf_op jit(solution)/shard_map/pallas_call | solution.py:44
  233.2 4.0 collective-permute-done.42.refs_2_
  243.4 12.6 %collective-permute-done.50.refs_0_.rest_3_ = bf16[256,1024]{1,0:T(8,128)(2,1)S(1)} collective-permute-done((bf16[256,1024]{1,0:T(8,128)(2,1)S(1)}, bf16[256,1024]{1,0:T(8,128)(2,1)S(1)}, u32[]{:S(2)}, u32[]{:S(2)}) %collective-permute-start.50) | collective-permute-done | bytes 524320 | tf_op jit(solution)/shard_map/ppermute | solution.py:77
  256.8 3.6 shard_map.239
  260.4 3.8 shard_map.240
  268.6 12.2 %collective-permute-done.53.refs_1_ = bf16[256,1024]{1,0:T(8,128)(2,1)S(1)} collective-permute-done((bf16[256,1024]{1,0:T(8,128)(2,1)S(1)}, bf16[256,1024]{1,0:T(8,128)(2,1)S(1)}, u32[]{:S(2)}, u32[]{:S(2)}) %collective-permute-start.53) | collective-permute-done | bytes 524320 | tf_op jit(solution)/shard_map/ppermute | solution.py:77
  293.0 5.5 shard_map.244
  300.9 4.9 collective-permute-done.57.refs_1_
  318.3 3.9 collective-permute-done.60.refs_2_
  323.4 7.9 %shard_map.247 = (bf16[256,768]{1,0:T(8,128)(2,1)S(1)}, bf16[256,768]{1,0:T(8,128)(2,1)S(1)}, bf16[256,768]{1,0:T(8,128)(2,1)S(1)}, bf16[256,768]{1,0:T(8,128)(2...) custom-call(s32[4]{0:T(128)S(1)} %pad_add_fusion.me.rest_0_, ...), custom_call_target="tpu_custom_call" | custom-call | flops 3221225472 | bytes 9449472 | tf_op jit(solution)/shard_map/pallas_call | solution.py:44
  336.4 12.6 %collective-permute-done.66 = bf16[2,4,32,1024]{3,2,1,0:T(8,128)(2,1)S(1)} collective-permute-done((bf16[2,4,32,1024]{3,2,1,0:T(8,128)(2,1)S(1)}, bf16[2,4,32,1024]{3,2,1,0:T(8,128)(2,1)S(1)}, u32[]{:S(2)}, u32[]{:S(2)}) %collective-permute-start.66) | collective-permute-done | bytes 524320 | tf_op jit(solution)/shard_map/ppermute | solution.py:77
  349.3 3.7 shard_map.248
  354.4 5.3 collective-permute-done.64.refs_1_
  362.4 11.8 %collective-permute-done.68.refs_0_.refs_14_ = bf16[256,1024]{1,0:T(8,128)(2,1)S(1)} collective-permute-done((bf16[256,1024]{1,0:T(8,128)(2,1)S(1)}, bf16[256,1024]{1,0:T(8,128)(2,1)S(1)}, u32[]{:S(2)}, u32[]{:S(2)}) %collective-permute-start.68) | collective-permute-done | bytes 524320 | tf_op jit(solution)/shard_map/ppermute | solution.py:77
  383.3 6.6 %shard_map.252 = (f32[1,1024]{1,0:T(1,128)S(1)}, bf16[4,8,32,1024]{3,2,1,0:T(8,128)(2,1)S(1)}, bf16[4,8,32,1024]{3,2,1,0:T(8,128)(2,1)}) custom-call(s32[4]{0:T(128)S(1)} %pad_add_fusion.me.rest_0_, bf16[256,1024]{1,0:T(8,128)(2,1)S(1)} %copy-done.71, bf16[256,1024]{1,0:T(8,128)(2,1)S(1)} %copy-done.75, bf16[256,1024]{1,0:T(8,128)(2,1)S(1)} %copy-done.73, ...), custom_call_target="tpu_custom_call" | custom-call | flops 4294967296 | bytes 12587008 | tf_op jit(solution)/shard_map/pallas_call | solution.py:44
  391.2 4.5 collective-permute-done.71.refs_1_
  408.6 8.7 %shard_map.255 = (bf16[256,768]{1,0:T(8,128)(2,1)S(1)}, bf16[256,768]{1,0:T(8,128)(2,1)S(1)}, bf16[256,768]{1,0:T(8,128)(2,1)S(1)}, bf16[256,768]{1,0:T(8,128)(2...) custom-call(s32[4]{0:T(128)S(1)} %pad_add_fusion.me.rest_0_, ...), custom_call_target="tpu_custom_call" | custom-call | flops 3221225472 | bytes 9449472 | tf_op jit(solution)/shard_map/pallas_call | solution.py:44
  427.6 12.8 %collective-permute-done.80 = bf16[2,4,32,1024]{3,2,1,0:T(8,128)(2,1)S(1)} collective-permute-done((bf16[2,4,32,1024]{3,2,1,0:T(8,128)(2,1)}, bf16[2,4,32,1024]{3,2,1,0:T(8,128)(2,1)S(1)}, u32[]{:S(2)}, u32[]{:S(2)}) %collective-permute-start.80) | collective-permute-done | bytes 524320 | tf_op jit(solution)/shard_map/ppermute | solution.py:77
  441.8 3.7 shard_map.256
  448.7 3.9 collective-permute-done.81
  452.7 3.7 fusion.8
  456.4 8.3 %collective-permute-start.83 = (bf16[8,32,1024]{2,1,0:T(8,128)(2,1)}, bf16[8,32,1024]{2,1,0:T(8,128)(2,1)S(1)}, u32[]{:S(2)}, u32[]{:S(2)}) collective-permute-start(bf16[8,32,1024]{2,1,0:T(8,128)(2,1)} %get-tuple-element.470), channel_id=1, source_target_pairs={{0,1},{1,2},{2,3},{3,0},{4,5},{5,6},{6,7},{7,4},{8,9},{9,10},{10,1... | collective-permute-start | bytes 1572872 | tf_op jit(solution)/shard_map/ppermute | solution.py:77
  478.2 24.5 %collective-permute-done.84.refs_2_ = bf16[8,32,1024]{2,1,0:T(8,128)(2,1)} collective-permute-done((bf16[8,32,1024]{2,1,0:T(8,128)(2,1)}, bf16[8,32,1024]{2,1,0:T(8,128)(2,1)}, u32[]{:S(2)}, u32[]{:S(2)}) %collective-permute-start.84) | collective-permute-done | bytes 524320 | tf_op jit(solution)/shard_map/ppermute | solution.py:77
  502.7 3.9 collective-permute-done.85.refs_3_
  509.8 12.3 %collective-permute-start.87 = (bf16[4,32,1024]{2,1,0:T(8,128)(2,1)}, bf16[4,32,1024]{2,1,0:T(8,128)(2,1)S(1)}, u32[]{:S(2)}, u32[]{:S(2)}) collective-permute-start(bf16[4,32,1024]{2,1,0:T(8,128)(2,1)} %get-tuple-element.474), channel_id=1, source_target_pairs={{0,1},{1,2},{2,3},{3,0},{4,5},{5,6},{6,7},{7,4},{8,9},{9,10},{10,1... | collective-permute-start | bytes 786440 | tf_op jit(solution)/shard_map/ppermute | solution.py:77
  526.9 3.5 collective-permute-start.97
  532.5 5.9 collective-permute-done.96
  538.4 7.1 %collective-permute-done.97 = f32[16,1024]{1,0:T(8,128)S(1)} collective-permute-done((f32[16,1024]{1,0:T(8,128)S(1)}, f32[16,1024]{1,0:T(8,128)S(1)}, u32[]{:S(2)}, u32[]{:S(2)}) %collective-permute-start.97) | collective-permute-done | bytes 65568 | tf_op jit(solution)/shard_map/ppermute | solution.py:77
  545.5 9.4 %collective-permute-start.86 = (bf16[2,256,1024]{2,1,0:T(8,128)(2,1)}, bf16[2,256,1024]{2,1,0:T(8,128)(2,1)}, u32[]{:S(2)}, u32[]{:S(2)}) collective-permute-start(bf16[2,256,1024]{2,1,0:T(8,128)(2,1)} %pad_maximum_fusion), channel_id=1, source_target_pairs={{0,0},{1,8},{2,4},{3,12},{8,1},{9,9},{10,5},{11,13},{4,2},{5,10},{... | collective-permute-start | bytes 3145736 | tf_op jit(solution)/shard_map/ppermute | solution.py:1010
  565.2 7.1 %collective-permute-done.91.refs_2_ = bf16[64,1792]{1,0:T(8,128)(2,1)S(1)} collective-permute-done((bf16[64,1792]{1,0:T(8,128)(2,1)S(1)}, bf16[64,1792]{1,0:T(8,128)(2,1)S(1)}, u32[]{:S(2)}, u32[]{:S(2)}) %collective-permute-start.91) | collective-permute-done | bytes 229408 | tf_op jit(solution)/shard_map/ppermute | solution.py:107
  572.3 18.2 %collective-permute-done.92.refs_3_ = bf16[64,1792]{1,0:T(8,128)(2,1)S(1)} collective-permute-done((bf16[64,1792]{1,0:T(8,128)(2,1)S(1)}, bf16[64,1792]{1,0:T(8,128)(2,1)S(1)}, u32[]{:S(2)}, u32[]{:S(2)}) %collective-permute-start.92) | collective-permute-done | bytes 229408 | tf_op jit(solution)/shard_map/ppermute | solution.py:107
  (501 shorter events, 212.9 us)
Async XLA Ops:
  7.2 108.7 %all-gather.5.cloned.1.call-start = ((), (), s32[]{:S(2)}) async-start(), calls=%async_computation.4 | async-start | bytes 1310720 | tf_op jit(solution)/shard_map/all_gather | solution.py:1025
  18.2 26.3 %collective-permute-start = (bf16[272,1024]{1,0:T(8,128)(2,1)S(1)}, bf16[272,1024]{1,0:T(8,128)(2,1)S(1)}, u32[]{:S(2)}, u32[]{:S(2)}) collective-permute-start(bf16[272,1024]{1,0:T(8,128)(2,1)S(1)} %shard_map.220), channel_id=1, source_target_pairs={{0,0},{1,8},{2,4},{3,12},{8,1},{9,9},{10,5},{11,13},{4,2},{5,10},{... | collective-permute-start | bytes 1671176 | tf_op jit(solution)/shard_map/ppermute | solution.py:1010
  27.2 24.9 %collective-permute-start.8 = (bf16[2,32,2816]{2,1,0:T(8,128)(2,1)S(1)}, bf16[2,32,2816]{2,1,0:T(8,128)(2,1)S(1)}, u32[]{:S(2)}, u32[]{:S(2)}) collective-permute-start(bf16[2,32,2816]{2,1,0:T(8,128)(2,1)S(1)} %pad_maximum_fusion.1), channel_id=1, source_target_pairs={{0,8},{8,0},{1,9},{9,1},{2,10},{10,2},{3,11},{11,3},{4,12},{12,4},... | collective-permute-start | bytes 1081352 | tf_op jit(solution)/shard_map/ppermute | solution.py:77
  30.4 23.3 %collective-permute-start.11 = (bf16[144,1024]{1,0:T(8,128)(2,1)S(1)}, bf16[144,1024]{1,0:T(8,128)(2,1)S(1)}, u32[]{:S(2)}, u32[]{:S(2)}) collective-permute-start(bf16[144,1024]{1,0:T(8,128)(2,1)S(1)} %shard_map.224.refs_0_), channel_id=1, source_target_pairs={{0,16},{16,0},{1,17},{17,1},{2,18},{18,2},{3,19},{19,3},{4,20},{20... | collective-permute-start | bytes 884744 | tf_op jit(solution)/shard_map/ppermute | solution.py:77
  55.9 128.9 %all-gather.7.cloned.1.call-start = ((), (), s32[]{:S(2)}) async-start(), calls=%async_computation.5 | async-start | bytes 2621440 | tf_op jit(solution)/shard_map/all_gather | solution.py:1025
  67.9 26.4 %collective-permute-start.9 = (bf16[128,2048]{1,0:T(8,128)(2,1)S(1)}, bf16[128,2048]{1,0:T(8,128)(2,1)}, u32[]{:S(2)}, u32[]{:S(2)}) collective-permute-start(bf16[128,2048]{1,0:T(8,128)(2,1)S(1)} %get-tuple-element.248.refs_0_), channel_id=1, source_target_pairs={{0,1},{1,2},{2,3},{3,0},{4,5},{5,6},{6,7},{7,4},{8,9},{9,10},{10,1... | collective-permute-start | bytes 1572872 | tf_op jit(solution)/shard_map/ppermute | solution.py:77
  67.9 26.4 %collective-permute-start.1 = (bf16[272,1024]{1,0:T(8,128)(2,1)S(1)}, bf16[272,1024]{1,0:T(8,128)(2,1)}, u32[]{:S(2)}, u32[]{:S(2)}) collective-permute-start(bf16[272,1024]{1,0:T(8,128)(2,1)S(1)} %collective-permute-done.refs_0_.refs_6_.refs_4_), channel_id=1, source_target_pairs={{0,4},{4,0},{1,5},{5,1},{2,6},{6,2},{3,7},{7,3},{8,12},{12,8},{9,1... | collective-permute-start | bytes 1671176 | tf_op jit(solution)/shard_map/ppermute | solution.py:77
  77.0 17.5 %collective-permute-start.23 = (bf16[2,4,32,1024]{3,2,1,0:T(8,128)(2,1)}, bf16[2,4,32,1024]{3,2,1,0:T(8,128)(2,1)}, u32[]{:S(2)}, u32[]{:S(2)}) collective-permute-start(bf16[2,4,32,1024]{3,2,1,0:T(8,128)(2,1)} %get-tuple-element.271.refs_0_), channel_id=1, source_target_pairs={{0,8},{8,0},{1,9},{9,1},{2,10},{10,2},{3,11},{11,3},{4,12},{12,4},... | collective-permute-start | bytes 1572872 | tf_op jit(solution)/shard_map/ppermute | solution.py:77
  80.7 15.6 %collective-permute-start.3 = (bf16[272,1024]{1,0:T(8,128)(2,1)}, bf16[272,1024]{1,0:T(8,128)(2,1)}, u32[]{:S(2)}, u32[]{:S(2)}) collective-permute-start(bf16[272,1024]{1,0:T(8,128)(2,1)} %collective-permute-done.2.refs_2_), channel_id=1, source_target_pairs={{0,4},{4,0},{1,5},{5,1},{2,6},{6,2},{3,7},{7,3},{8,12},{12,8},{9,1... | collective-permute-start | bytes 1671176 | tf_op jit(solution)/shard_map/ppermute | solution.py:77
  80.7 31.1 %collective-permute-start.20 = (bf16[128,2048]{1,0:T(8,128)(2,1)S(1)}, bf16[128,2048]{1,0:T(8,128)(2,1)}, u32[]{:S(2)}, u32[]{:S(2)}) collective-permute-start(bf16[128,2048]{1,0:T(8,128)(2,1)S(1)} %get-tuple-element.248.refs_0_), channel_id=1, source_target_pairs={{0,16},{16,0},{1,17},{17,1},{2,18},{18,2},{3,19},{19,3},{4,20},{20... | collective-permute-start | bytes 1572872 | tf_op jit(solution)/shard_map/ppermute | solution.py:77
  94.4 21.6 %collective-permute-start.21 = (bf16[128,2048]{1,0:T(8,128)(2,1)}, bf16[128,2048]{1,0:T(8,128)(2,1)}, u32[]{:S(2)}, u32[]{:S(2)}) collective-permute-start(bf16[128,2048]{1,0:T(8,128)(2,1)} %collective-permute-done.9.refs_1_), channel_id=1, source_target_pairs={{0,1},{1,2},{2,3},{3,0},{4,5},{5,6},{6,7},{7,4},{8,9},{9,10},{10,1... | collective-permute-start | bytes 1572872 | tf_op jit(solution)/shard_map/ppermute | solution.py:77
  94.4 31.1 %collective-permute-start.22 = (bf16[2,4,32,1024]{3,2,1,0:T(8,128)(2,1)}, bf16[2,4,32,1024]{3,2,1,0:T(8,128)(2,1)}, u32[]{:S(2)}, u32[]{:S(2)}) collective-permute-start(bf16[2,4,32,1024]{3,2,1,0:T(8,128)(2,1)} %get-tuple-element.271.refs_0_), channel_id=1, source_target_pairs={{0,4},{4,0},{1,5},{5,1},{2,6},{6,2},{3,7},{7,3},{8,12},{12,8},{9,1... | collective-permute-start | bytes 1572872 | tf_op jit(solution)/shard_map/ppermute | solution.py:77
  94.5 31.0 %collective-permute-start.24 = (bf16[2,4,32,1024]{3,2,1,0:T(8,128)(2,1)}, bf16[2,4,32,1024]{3,2,1,0:T(8,128)(2,1)}, u32[]{:S(2)}, u32[]{:S(2)}) collective-permute-start(bf16[2,4,32,1024]{3,2,1,0:T(8,128)(2,1)} %collective-permute-done.23.refs_2_), channel_id=1, source_target_pairs={{0,4},{4,0},{1,5},{5,1},{2,6},{6,2},{3,7},{7,3},{8,12},{12,8},{9,1... | collective-permute-start | bytes 1572872 | tf_op jit(solution)/shard_map/ppermute | solution.py:77
  115.9 306.7 %reduce-scatter.3.cloned.1.call-start = ((), (), s32[]{:S(2)}) async-start(), calls=%async_computation.2 | async-start | bytes 4718592 | tf_op jit(solution)/shard_map/reduce_scatter | solution.py:1131
  116.0 15.5 %collective-permute-start.30 = (bf16[128,2048]{1,0:T(8,128)(2,1)}, bf16[128,2048]{1,0:T(8,128)(2,1)S(1)}, u32[]{:S(2)}, u32[]{:S(2)}) collective-permute-start(bf16[128,2048]{1,0:T(8,128)(2,1)} %collective-permute-done.9.refs_1_), channel_id=1, source_target_pairs={{0,16},{16,0},{1,17},{17,1},{2,18},{18,2},{3,19},{19,3},{4,20},{20... | collective-permute-start | bytes 1572872 | tf_op jit(solution)/shard_map/ppermute | solution.py:77
  117.4 22.7 %collective-permute-start.31 = (bf16[128,2048]{1,0:T(8,128)(2,1)}, bf16[128,2048]{1,0:T(8,128)(2,1)S(1)}, u32[]{:S(2)}, u32[]{:S(2)}) collective-permute-start(bf16[128,2048]{1,0:T(8,128)(2,1)} %collective-permute-done.21.refs_2_), channel_id=1, source_target_pairs={{0,1},{1,2},{2,3},{3,0},{4,5},{5,6},{6,7},{7,4},{8,9},{9,10},{10,1... | collective-permute-start | bytes 1572872 | tf_op jit(solution)/shard_map/ppermute | solution.py:77
  130.8 15.0 %collective-permute-start.32 = (bf16[128,2048]{1,0:T(8,128)(2,1)}, bf16[128,2048]{1,0:T(8,128)(2,1)S(1)}, u32[]{:S(2)}, u32[]{:S(2)}) collective-permute-start(bf16[128,2048]{1,0:T(8,128)(2,1)} %collective-permute-done.21.refs_2_), channel_id=1, source_target_pairs={{0,16},{16,0},{1,17},{17,1},{2,18},{18,2},{3,19},{19,3},{4,20},{20... | collective-permute-start | bytes 1572872 | tf_op jit(solution)/shard_map/ppermute | solution.py:77
  140.2 15.5 %collective-permute-start.33 = (bf16[128,2048]{1,0:T(8,128)(2,1)S(1)}, bf16[128,2048]{1,0:T(8,128)(2,1)S(1)}, u32[]{:S(2)}, u32[]{:S(2)}) collective-permute-start(bf16[128,2048]{1,0:T(8,128)(2,1)S(1)} %collective-permute-done.31.refs_3_), channel_id=1, source_target_pairs={{0,16},{16,0},{1,17},{17,1},{2,18},{18,2},{3,19},{19,3},{4,20},{20... | collective-permute-start | bytes 1572872 | tf_op jit(solution)/shard_map/ppermute | solution.py:77
  143.2 18.7 %collective-permute-start.27 = (bf16[256,1024]{1,0:T(8,128)(2,1)S(1)}, bf16[256,1024]{1,0:T(8,128)(2,1)S(1)}, u32[]{:S(2)}, u32[]{:S(2)}) collective-permute-start(bf16[256,1024]{1,0:T(8,128)(2,1)S(1)} %collective-permute-done.26.refs_0_.refs_2_), channel_id=1, source_target_pairs={{0,4},{4,0},{1,5},{5,1},{2,6},{6,2},{3,7},{7,3},{8,12},{12,8},{9,1... | collective-permute-start | bytes 1572872 | tf_op jit(solution)/shard_map/ppermute | solution.py:77
  166.2 26.3 %collective-permute-start.40 = (bf16[4,128,1024]{2,1,0:T(8,128)(2,1)}, bf16[4,128,1024]{2,1,0:T(8,128)(2,1)}, u32[]{:S(2)}, u32[]{:S(2)}) collective-permute-start(bf16[4,128,1024]{2,1,0:T(8,128)(2,1)} %bitcast.14.refs_0_), channel_id=1, source_target_pairs={{0,16},{16,0},{1,17},{17,1},{2,18},{18,2},{3,19},{19,3},{4,20},{20... | collective-permute-start | bytes 3145736 | tf_op jit(solution)/shard_map/ppermute | solution.py:77
  184.2 19.1 %collective-permute-start.38 = (bf16[256,1024]{1,0:T(8,128)(2,1)}, bf16[256,1024]{1,0:T(8,128)(2,1)}, u32[]{:S(2)}, u32[]{:S(2)}) collective-permute-start(bf16[256,1024]{1,0:T(8,128)(2,1)} %get-tuple-element.289.refs_0_.rest_1_), channel_id=1, source_target_pairs={{0,8},{8,0},{1,9},{9,1},{2,10},{10,2},{3,11},{11,3},{4,12},{12,4},... | collective-permute-start | bytes 1572872 | tf_op jit(solution)/shard_map/ppermute | solution.py:77
  184.8 71.1 %collective-permute-start.49 = (bf16[4,128,2048]{2,1,0:T(8,128)(2,1)}, bf16[4,128,2048]{2,1,0:T(8,128)(2,1)S(1)}, u32[]{:S(2)}, u32[]{:S(2)}) collective-permute-start(bf16[4,128,2048]{2,1,0:T(8,128)(2,1)} %bitcast.104), channel_id=1, source_target_pairs={{0,16},{16,0},{1,17},{17,1},{2,18},{18,2},{3,19},{19,3},{4,20},{20... | collective-permute-start | bytes 6291464 | tf_op jit(solution)/shard_map/ppermute | solution.py:77
  185.6 17.7 %collective-permute-start.28 = (bf16[256,1024]{1,0:T(8,128)(2,1)}, bf16[256,1024]{1,0:T(8,128)(2,1)S(1)}, u32[]{:S(2)}, u32[]{:S(2)}) collective-permute-start(bf16[256,1024]{1,0:T(8,128)(2,1)} %bitcast.137), channel_id=1, source_target_pairs={{0,0},{1,8},{2,4},{3,12},{8,1},{9,9},{10,5},{11,13},{4,2},{5,10},{... | collective-permute-start | bytes 1572872 | tf_op jit(solution)/shard_map/ppermute | solution.py:1010
  194.3 24.0 %collective-permute-start.46 = (bf16[2,4,32,1024]{3,2,1,0:T(8,128)(2,1)S(1)}, bf16[2,4,32,1024]{3,2,1,0:T(8,128)(2,1)S(1)}, u32[]{:S(2)}, u32[]{:S(2)}) collective-permute-start(bf16[2,4,32,1024]{3,2,1,0:T(8,128)(2,1)S(1)} %get-tuple-element.304.refs_0_), channel_id=1, source_target_pairs={{0,8},{8,0},{1,9},{9,1},{2,10},{10,2},{3,11},{11,3},{4,12},{12,4},... | collective-permute-start | bytes 1572872 | tf_op jit(solution)/shard_map/ppermute | solution.py:77
  196.2 22.1 %collective-permute-start.37 = (bf16[256,1024]{1,0:T(8,128)(2,1)}, bf16[256,1024]{1,0:T(8,128)(2,1)S(1)}, u32[]{:S(2)}, u32[]{:S(2)}) collective-permute-start(bf16[256,1024]{1,0:T(8,128)(2,1)} %get-tuple-element.289.refs_0_.rest_1_), channel_id=1, source_target_pairs={{0,4},{4,0},{1,5},{5,1},{2,6},{6,2},{3,7},{7,3},{8,12},{12,8},{9,1... | collective-permute-start | bytes 1572872 | tf_op jit(solution)/shard_map/ppermute | solution.py:77
  203.2 15.0 %collective-permute-start.39 = (bf16[256,1024]{1,0:T(8,128)(2,1)}, bf16[256,1024]{1,0:T(8,128)(2,1)S(1)}, u32[]{:S(2)}, u32[]{:S(2)}) collective-permute-start(bf16[256,1024]{1,0:T(8,128)(2,1)} %collective-permute-done.38.refs_2_.rest_3_), channel_id=1, source_target_pairs={{0,4},{4,0},{1,5},{5,1},{2,6},{6,2},{3,7},{7,3},{8,12},{12,8},{9,1... | collective-permute-start | bytes 1572872 | tf_op jit(solution)/shard_map/ppermute | solution.py:77
  203.3 27.6 %collective-permute-start.45 = (bf16[2,4,32,1024]{3,2,1,0:T(8,128)(2,1)S(1)}, bf16[2,4,32,1024]{3,2,1,0:T(8,128)(2,1)S(1)}, u32[]{:S(2)}, u32[]{:S(2)}) collective-permute-start(bf16[2,4,32,1024]{3,2,1,0:T(8,128)(2,1)S(1)} %get-tuple-element.304.refs_0_), channel_id=1, source_target_pairs={{0,4},{4,0},{1,5},{5,1},{2,6},{6,2},{3,7},{7,3},{8,12},{12,8},{9,1... | collective-permute-start | bytes 1572872 | tf_op jit(solution)/shard_map/ppermute | solution.py:77
  218.3 20.4 %collective-permute-start.44 = (bf16[256,1024]{1,0:T(8,128)(2,1)S(1)}, bf16[256,1024]{1,0:T(8,128)(2,1)S(1)}, u32[]{:S(2)}, u32[]{:S(2)}) collective-permute-start(bf16[256,1024]{1,0:T(8,128)(2,1)S(1)} %collective-permute-done.28.refs_0_.rest_13_.refs_3_), channel_id=1, source_target_pairs={{0,8},{8,0},{1,9},{9,1},{2,10},{10,2},{3,11},{11,3},{4,12},{12,4},... | collective-permute-start | bytes 1572872 | tf_op jit(solution)/shard_map/ppermute | solution.py:77
  268.2 17.9 %collective-permute-start.55 = (bf16[256,1024]{1,0:T(8,128)(2,1)S(1)}, bf16[256,1024]{1,0:T(8,128)(2,1)S(1)}, u32[]{:S(2)}, u32[]{:S(2)}) collective-permute-start(bf16[256,1024]{1,0:T(8,128)(2,1)S(1)} %collective-permute-done.44.refs_0_.rest_15_), channel_id=1, source_target_pairs={{0,4},{4,0},{1,5},{5,1},{2,6},{6,2},{3,7},{7,3},{8,12},{12,8},{9,1... | collective-permute-start | bytes 1572872 | tf_op jit(solution)/shard_map/ppermute | solution.py:77
  300.5 257.0 %reduce-scatter.5.cloned.1.call-start = ((), (), s32[]{:S(2)}) async-start(), calls=%async_computation.3 | async-start | bytes 2359296 | tf_op jit(solution)/shard_map/reduce_scatter | solution.py:1131
  335.9 18.4 %collective-permute-start.65 = (bf16[256,1024]{1,0:T(8,128)(2,1)S(1)}, bf16[256,1024]{1,0:T(8,128)(2,1)S(1)}, u32[]{:S(2)}, u32[]{:S(2)}) collective-permute-start(bf16[256,1024]{1,0:T(8,128)(2,1)S(1)} %get-tuple-element.362), channel_id=1, source_target_pairs={{0,4},{4,0},{1,5},{5,1},{2,6},{6,2},{3,7},{7,3},{8,12},{12,8},{9,1... | collective-permute-start | bytes 1572872 | tf_op jit(solution)/shard_map/ppermute | solution.py:77
  336.0 23.7 %collective-permute-start.64 = (bf16[256,1024]{1,0:T(8,128)(2,1)S(1)}, bf16[256,1024]{1,0:T(8,128)(2,1)S(1)}, u32[]{:S(2)}, u32[]{:S(2)}) collective-permute-start(bf16[256,1024]{1,0:T(8,128)(2,1)S(1)} %add_convert_fusion.5), channel_id=1, source_target_pairs={{0,8},{8,0},{1,9},{9,1},{2,10},{10,2},{3,11},{11,3},{4,12},{12,4},... | collective-permute-start | bytes 1572872 | tf_op jit(solution)/shard_map/ppermute | solution.py:77
  399.7 52.9 %collective-permute-start.81 = (bf16[4,8,32,1024]{3,2,1,0:T(8,128)(2,1)}, bf16[4,8,32,1024]{3,2,1,0:T(8,128)(2,1)}, u32[]{:S(2)}, u32[]{:S(2)}) collective-permute-start(bf16[4,8,32,1024]{3,2,1,0:T(8,128)(2,1)} %get-tuple-element.441), channel_id=1, source_target_pairs={{0,16},{16,0},{1,17},{17,1},{2,18},{18,2},{3,19},{19,3},{4,20},{20... | collective-permute-start | bytes 6291464 | tf_op jit(solution)/shard_map/ppermute | solution.py:77
  427.5 37.8 %collective-permute-start.79 = (bf16[256,1024]{1,0:T(8,128)(2,1)}, bf16[256,1024]{1,0:T(8,128)(2,1)S(1)}, u32[]{:S(2)}, u32[]{:S(2)}) collective-permute-start(bf16[256,1024]{1,0:T(8,128)(2,1)} %copy-done.82), channel_id=1, source_target_pairs={{0,4},{4,0},{1,5},{5,1},{2,6},{6,2},{3,7},{7,3},{8,12},{12,8},{9,1... | collective-permute-start | bytes 1572872 | tf_op jit(solution)/shard_map/ppermute | solution.py:77
  445.5 61.1 %collective-permute-start.82 = (bf16[4,4,32,1024]{3,2,1,0:T(8,128)(2,1)}, bf16[4,4,32,1024]{3,2,1,0:T(8,128)(2,1)}, u32[]{:S(2)}, u32[]{:S(2)}) collective-permute-start(bf16[4,4,32,1024]{3,2,1,0:T(8,128)(2,1)} %get-tuple-element.449), channel_id=1, source_target_pairs={{0,16},{16,0},{1,17},{17,1},{2,18},{18,2},{3,19},{19,3},{4,20},{20... | collective-permute-start | bytes 3145736 | tf_op jit(solution)/shard_map/ppermute | solution.py:77
  447.0 21.3 %collective-permute-start.78 = (bf16[256,1024]{1,0:T(8,128)(2,1)S(1)}, bf16[256,1024]{1,0:T(8,128)(2,1)S(1)}, u32[]{:S(2)}, u32[]{:S(2)}) collective-permute-start(bf16[256,1024]{1,0:T(8,128)(2,1)S(1)} %add_convert_fusion.3), channel_id=1, source_target_pairs={{0,8},{8,0},{1,9},{9,1},{2,10},{10,2},{3,11},{11,3},{4,12},{12,4},... | collective-permute-start | bytes 1572872 | tf_op jit(solution)/shard_map/ppermute | solution.py:77
  456.4 21.0 %collective-permute-start.83 = (bf16[8,32,1024]{2,1,0:T(8,128)(2,1)}, bf16[8,32,1024]{2,1,0:T(8,128)(2,1)S(1)}, u32[]{:S(2)}, u32[]{:S(2)}) collective-permute-start(bf16[8,32,1024]{2,1,0:T(8,128)(2,1)} %get-tuple-element.470), channel_id=1, source_target_pairs={{0,1},{1,2},{2,3},{3,0},{4,5},{5,6},{6,7},{7,4},{8,9},{9,10},{10,1... | collective-permute-start | bytes 1572872 | tf_op jit(solution)/shard_map/ppermute | solution.py:77
  464.7 37.9 %collective-permute-start.84 = (bf16[8,32,1024]{2,1,0:T(8,128)(2,1)}, bf16[8,32,1024]{2,1,0:T(8,128)(2,1)}, u32[]{:S(2)}, u32[]{:S(2)}) collective-permute-start(bf16[8,32,1024]{2,1,0:T(8,128)(2,1)} %get-tuple-element.469), channel_id=1, source_target_pairs={{0,2},{1,3},{2,0},{3,1},{4,6},{5,7},{6,4},{7,5},{8,10},{9,11},{10,... | collective-permute-start | bytes 1572872 | tf_op jit(solution)/shard_map/ppermute | solution.py:77
  465.3 41.3 %collective-permute-start.85 = (bf16[8,32,1024]{2,1,0:T(8,128)(2,1)}, bf16[8,32,1024]{2,1,0:T(8,128)(2,1)}, u32[]{:S(2)}, u32[]{:S(2)}) collective-permute-start(bf16[8,32,1024]{2,1,0:T(8,128)(2,1)} %get-tuple-element.468), channel_id=1, source_target_pairs={{0,3},{1,0},{2,1},{3,2},{4,7},{5,4},{6,5},{7,6},{8,11},{9,8},{10,9... | collective-permute-start | bytes 1572872 | tf_op jit(solution)/shard_map/ppermute | solution.py:77
  472.5 36.7 %collective-permute-start.94 = (f32[12,1024]{1,0:T(8,128)S(1)}, f32[12,1024]{1,0:T(8,128)S(1)}, u32[]{:S(2)}, u32[]{:S(2)}) collective-permute-start(f32[12,1024]{1,0:T(8,128)S(1)} %add.153), channel_id=1, source_target_pairs={{0,8},{8,0},{1,9},{9,1},{2,10},{10,2},{3,11},{11,3},{4,12},{12,4},... | collective-permute-start | bytes 147464 | tf_op jit(solution)/shard_map/ppermute | solution.py:77
  509.3 16.3 %collective-permute-start.95 = (f32[16,1024]{1,0:T(8,128)S(1)}, f32[16,1024]{1,0:T(8,128)}, u32[]{:S(2)}, u32[]{:S(2)}) collective-permute-start(f32[16,1024]{1,0:T(8,128)S(1)} %concatenate.15), channel_id=1, source_target_pairs={{0,16},{16,0},{1,17},{17,1},{2,18},{18,2},{3,19},{19,3},{4,20},{20... | collective-permute-start | bytes 196616 | tf_op jit(solution)/shard_map/ppermute | solution.py:77
  509.8 47.7 %collective-permute-start.87 = (bf16[4,32,1024]{2,1,0:T(8,128)(2,1)}, bf16[4,32,1024]{2,1,0:T(8,128)(2,1)S(1)}, u32[]{:S(2)}, u32[]{:S(2)}) collective-permute-start(bf16[4,32,1024]{2,1,0:T(8,128)(2,1)} %get-tuple-element.474), channel_id=1, source_target_pairs={{0,1},{1,2},{2,3},{3,0},{4,5},{5,6},{6,7},{7,4},{8,9},{9,10},{10,1... | collective-permute-start | bytes 786440 | tf_op jit(solution)/shard_map/ppermute | solution.py:77
  522.1 35.4 %collective-permute-start.88 = (bf16[4,32,1024]{2,1,0:T(8,128)(2,1)}, bf16[4,32,1024]{2,1,0:T(8,128)(2,1)}, u32[]{:S(2)}, u32[]{:S(2)}) collective-permute-start(bf16[4,32,1024]{2,1,0:T(8,128)(2,1)} %get-tuple-element.473), channel_id=1, source_target_pairs={{0,2},{1,3},{2,0},{3,1},{4,6},{5,7},{6,4},{7,5},{8,10},{9,11},{10,... | collective-permute-start | bytes 786440 | tf_op jit(solution)/shard_map/ppermute | solution.py:77
  526.9 18.6 %collective-permute-start.97 = (f32[16,1024]{1,0:T(8,128)S(1)}, f32[16,1024]{1,0:T(8,128)S(1)}, u32[]{:S(2)}, u32[]{:S(2)}) collective-permute-start(f32[16,1024]{1,0:T(8,128)S(1)} %add.155), channel_id=1, source_target_pairs={{0,2},{1,3},{2,0},{3,1},{4,6},{5,7},{6,4},{7,5},{8,10},{9,11},{10,... | collective-permute-start | bytes 196616 | tf_op jit(solution)/shard_map/ppermute | solution.py:77
  530.4 24.6 %collective-permute-start.98 = (f32[16,1024]{1,0:T(8,128)S(1)}, f32[16,1024]{1,0:T(8,128)S(1)}, u32[]{:S(2)}, u32[]{:S(2)}) collective-permute-start(f32[16,1024]{1,0:T(8,128)S(1)} %add.155), channel_id=1, source_target_pairs={{0,3},{1,0},{2,1},{3,2},{4,7},{5,4},{6,5},{7,6},{8,11},{9,8},{10,9... | collective-permute-start | bytes 196616 | tf_op jit(solution)/shard_map/ppermute | solution.py:77
  538.4 19.1 %collective-permute-start.89 = (bf16[4,32,1024]{2,1,0:T(8,128)(2,1)}, bf16[4,32,1024]{2,1,0:T(8,128)(2,1)S(1)}, u32[]{:S(2)}, u32[]{:S(2)}) collective-permute-start(bf16[4,32,1024]{2,1,0:T(8,128)(2,1)} %get-tuple-element.472), channel_id=1, source_target_pairs={{0,3},{1,0},{2,1},{3,2},{4,7},{5,4},{6,5},{7,6},{8,11},{9,8},{10,9... | collective-permute-start | bytes 786440 | tf_op jit(solution)/shard_map/ppermute | solution.py:77
  545.5 17.5 %collective-permute-start.86 = (bf16[2,256,1024]{2,1,0:T(8,128)(2,1)}, bf16[2,256,1024]{2,1,0:T(8,128)(2,1)}, u32[]{:S(2)}, u32[]{:S(2)}) collective-permute-start(bf16[2,256,1024]{2,1,0:T(8,128)(2,1)} %pad_maximum_fusion), channel_id=1, source_target_pairs={{0,0},{1,8},{2,4},{3,12},{8,1},{9,9},{10,5},{11,13},{4,2},{5,10},{... | collective-permute-start | bytes 3145736 | tf_op jit(solution)/shard_map/ppermute | solution.py:1010
  561.9 28.6 %collective-permute-start.92 = (bf16[64,1792]{1,0:T(8,128)(2,1)S(1)}, bf16[64,1792]{1,0:T(8,128)(2,1)S(1)}, u32[]{:S(2)}, u32[]{:S(2)}) collective-permute-start(bf16[64,1792]{1,0:T(8,128)(2,1)S(1)} %get-tuple-element.458), channel_id=1, source_target_pairs={{0,12},{4,8},{8,4},{12,0},{1,13},{5,9},{9,5},{13,1},{2,14},{6,10},... | collective-permute-start | bytes 688136 | tf_op jit(solution)/shard_map/ppermute | solution.py:107
  (182 other events, 1746.2 us)
Sparse Core Ops, SparseCore 0:
  56.0 47.2 all-gather.4
  116.0 52.2 all-gather.6
  300.6 91.5 reduce-scatter.2
  422.8 89.7 reduce-scatter.4
